TPU v7x, 256 devices: a whole 4x4x8 slice. The times are simulated.
256 devices in a mesh: dp: 4 (over x), expert: 64 (over z, y, core).
Axes of the slice: x: 4, y: 4, z: 8, core: 2. Of those that a mesh axis runs over, the one named last changes fastest.
Arguments:
- tokens: bfloat16 [32768, 2048], P(('dp', 'expert')), may hold values from -6 to 6
- cotangent: bfloat16 [32768, 2048], P(('dp', 'expert')), may hold values from -6 to 6
- expert_ids: int32 [32768, 8], P(('dp', 'expert')), may hold values from 0 to 63, all different within a row
- combine: float32 [32768, 8], P(('dp', 'expert')), may hold values from 0.05 to 1
- capacity: int32 [64], replicated, may hold values from 4 to 8, as said below
- w_gate: bfloat16 [64, 2048, 384], P('expert', 'dp'), may hold values from -0.125 to 0.125
- w_up: bfloat16 [64, 2048, 384], P('expert', 'dp'), may hold values from -0.125 to 0.125
- w_down: bfloat16 [64, 384, 2048], P('expert', None, 'dp'), may hold values from -0.3125 to 0.3125
Outputs:
- mixed: bfloat16 [32768, 2048], P(('dp', 'expert'))
- grad_tokens: bfloat16 [32768, 2048], P(('dp', 'expert'))
- grad_combine: float32 [32768, 8], P(('dp', 'expert'))
- grad_gate: bfloat16 [64, 2048, 384], P('expert', 'dp')
- grad_up: bfloat16 [64, 2048, 384], P('expert', 'dp')
- grad_down: bfloat16 [64, 384, 2048], P('expert', None, 'dp')
Inputs may be any that keep to these rules, and one draw needn't show every extreme that they name: Some expert has capacity 8 in every draw.
All inputs are finite; a program needn't handle non-finite values.
Results may differ from a plain program's by a relative error of at most 0.013.
Values may be sent and summed in bfloat16 or wider, within the bound.
No kernel may reach another device: no remote copies, remote signals or barrier semaphores. Data moves between devices by JAX's collectives and lax.ppermute only.
A program may use at most 64 MiB of HBM per device.

v0:
```python
import jax
import jax.numpy as jnp
from jax import lax
from jax.sharding import PartitionSpec as P


def forward_part(rows, wgate, wup, wdown):
    hidden_gate = jnp.dot(rows, wgate, preferred_element_type=jnp.float32)
    hidden_up = jnp.dot(rows, wup, preferred_element_type=jnp.float32)
    sigma = jax.nn.sigmoid(hidden_gate)
    active = (hidden_gate * sigma * hidden_up).astype(jnp.bfloat16)
    output = jnp.dot(active, wdown, preferred_element_type=jnp.float32).astype(jnp.bfloat16)
    return (output, (hidden_gate, hidden_up, sigma, active))


def backward_part(rows, grads, saved, wgate, wup, wdown):
    hidden_gate, hidden_up, sigma, active = saved
    d_active = jnp.dot(grads, wdown.T, preferred_element_type=jnp.float32)
    d_gate = (d_active * hidden_up * sigma * (1.0 + hidden_gate * (1.0 - sigma))).astype(
        jnp.bfloat16
    )
    d_up = (d_active * hidden_gate * sigma).astype(jnp.bfloat16)
    d_rows = (
        jnp.dot(d_gate, wgate.T, preferred_element_type=jnp.float32)
        + jnp.dot(d_up, wup.T, preferred_element_type=jnp.float32)
    ).astype(jnp.bfloat16)
    grad_gate = jnp.dot(rows.T, d_gate, preferred_element_type=jnp.float32)
    grad_up = jnp.dot(rows.T, d_up, preferred_element_type=jnp.float32)
    grad_down = jnp.dot(active.T, grads, preferred_element_type=jnp.float32)
    return (d_rows, grad_gate, grad_up, grad_down)


def on_device(tokens, cotangent, expert_ids, combine, capacity, w_gate, w_up, w_down):
    peers = lax.axis_size("expert")
    tok_count = tokens.shape[0]
    top_count = expert_ids.shape[1]
    width = tokens.shape[1]
    experts_all = capacity.shape[0]
    slot_count = tok_count * top_count // (2 * peers)
    assign_count = tok_count * top_count
    assigned = expert_ids.reshape(-1)
    onehot = (assigned[:, None] == jnp.arange(experts_all, dtype=jnp.int32)[None, :]).astype(
        jnp.int32
    )
    ranking = jnp.sum((jnp.cumsum(onehot, axis=0) - onehot) * onehot, axis=1)
    limits = jnp.sum(onehot * capacity[None, :], axis=1)
    position = jnp.where(
        ranking < limits, assigned * slot_count + ranking, experts_all * slot_count
    )
    slot_table = jnp.full((experts_all * slot_count + 1,), assign_count, jnp.int32)
    slot_table = slot_table.at[position].set(jnp.arange(assign_count, dtype=jnp.int32))[:-1]
    padded_tokens = jnp.concatenate([tokens, jnp.zeros((1, width), jnp.bfloat16)], axis=0)
    send_tokens = padded_tokens[slot_table // top_count].reshape(peers, slot_count, width)
    scaled = (combine[:, :, None] * cotangent[:, None, :].astype(jnp.float32)).astype(jnp.bfloat16)
    padded_scaled = jnp.concatenate(
        [scaled.reshape(assign_count, width), jnp.zeros((1, width), jnp.bfloat16)], axis=0
    )
    send_scaled = padded_scaled[slot_table].reshape(peers, slot_count, width)
    gathered = (
        lax.all_gather(w_gate, "dp", axis=1, tiled=True),
        lax.all_gather(w_up, "dp", axis=1, tiled=True),
    )
    wgate = gathered[0][0]
    wup = gathered[1][0]
    wdown = lax.all_gather(w_down, "dp", axis=2, tiled=True)[0]
    recv_tokens = lax.all_to_all(send_tokens, "expert", split_axis=0, concat_axis=0, tiled=True)
    rows = recv_tokens.reshape(-1, width)
    output, saved = forward_part(rows, wgate, wup, wdown)
    back_output = lax.all_to_all(
        output.reshape(peers, slot_count, width), "expert", split_axis=0, concat_axis=0, tiled=True
    )
    recv_scaled = lax.all_to_all(send_scaled, "expert", split_axis=0, concat_axis=0, tiled=True)
    grads = recv_scaled.reshape(-1, width)
    d_rows, grad_gate, grad_up, grad_down = backward_part(rows, grads, saved, wgate, wup, wdown)
    back_rows = lax.all_to_all(
        d_rows.reshape(peers, slot_count, width), "expert", split_axis=0, concat_axis=0, tiled=True
    )
    zero_row = jnp.zeros((1, width), jnp.bfloat16)
    padded_output = jnp.concatenate([back_output.reshape(-1, width), zero_row], axis=0)
    padded_rows = jnp.concatenate([back_rows.reshape(-1, width), zero_row], axis=0)
    picked_output = padded_output[position].reshape(tok_count, top_count, width).astype(jnp.float32)
    picked_rows = padded_rows[position].reshape(tok_count, top_count, width).astype(jnp.float32)
    mixed = jnp.sum(combine[:, :, None] * picked_output, axis=1).astype(jnp.bfloat16)
    grad_tokens = jnp.sum(picked_rows, axis=1).astype(jnp.bfloat16)
    grad_combine = jnp.sum(cotangent[:, None, :].astype(jnp.float32) * picked_output, axis=2)
    summed_gate, summed_up = (
        lax.psum_scatter(
            grad_gate.astype(jnp.bfloat16), "dp", scatter_dimension=0, tiled=True
        ).astype(jnp.float32),
        lax.psum_scatter(
            grad_up.astype(jnp.bfloat16), "dp", scatter_dimension=0, tiled=True
        ).astype(jnp.float32),
    )
    summed_down = lax.psum_scatter(
        grad_down.astype(jnp.bfloat16), "dp", scatter_dimension=1, tiled=True
    )
    return (
        mixed,
        grad_tokens,
        grad_combine,
        summed_gate.astype(jnp.bfloat16)[None],
        summed_up.astype(jnp.bfloat16)[None],
        summed_down[None],
    )


def solution(mesh):
    return jax.shard_map(
        on_device,
        mesh=mesh,
        in_specs=(
            P(("dp", "expert"), None),
            P(("dp", "expert"), None),
            P(("dp", "expert"), None),
            P(("dp", "expert"), None),
            P(),
            P("expert", "dp", None),
            P("expert", "dp", None),
            P("expert", None, "dp"),
        ),
        out_specs=(
            P(("dp", "expert"), None),
            P(("dp", "expert"), None),
            P(("dp", "expert"), None),
            P("expert", "dp", None),
            P("expert", "dp", None),
            P("expert", None, "dp"),
        ),
        check_vma=False,
    )
```

profile of v0, /device:TPU:4, one launch (start us, length us, event | category | flops | bytes accessed | tf_op | source)
XLA Modules:
  0.0 324.7 jit_solution(12211417189969232457)
XLA Ops:
  7.2 0.0 copy-start.8
  7.2 0.8 copy.23
  8.0 0.1 eq.29
  8.1 0.1 eq.25
  8.2 0.7 broadcast_multiply_fusion
  8.9 18.0 %reduce-window.6 = s32[64,8,128]{2,1,0:T(8,128)S(1)} reduce-window(s32[64,8,128]{2,1,0:T(8,128)S(1)} %fusion.24, s32[]{:T(128)} %constant.16.clone.1), window={size=1x1x128 pad=0_0x0_0x127_0}, to_apply=%region_0.0 | reduce-window | flops 8323072 | bytes 524292 | tf_op jit(solution)/shard_map/reduce-window
  26.9 0.1 slice.20
  27.1 0.1 copy.25
  27.3 0.1 copy.26
  27.3 0.1 broadcast_add_fusion
  27.5 0.1 copy.27
  27.6 0.1 mul.93
  27.7 0.1 select_reduce_fusion
  27.8 4.3 %scatter_custom_fusion = s32[513]{0:T(1024)S(1)} fusion(s32[1024]{0:T(1024)S(1)} %bitcast.86, s32[1024]{0:T(1024)S(1)} %iota.11, s32[]{:T(128)} %constant.15.clone.1), kind=kCustom, calls=%fused_computation.62 | custom fusion | bytes 2056 | tf_op jit(solution)/shard_map/scatter | solution.py:51
  32.3 3.3 %gather_fusion = bf16[512,2048]{1,0:T(8,128)(2,1)} fusion(bf16[129,2048]{1,0:T(8,128)(2,1)S(1)} %concatenate.12, s32[1024]{0:T(1024)S(1)} %get-tuple-element.22), kind=kCustom, calls=%fused_computation | custom fusion | bytes 4196352 | tf_op jit(solution)/shard_map/gather | solution.py:53
  35.6 12.1 %all-to-all-start = ((bf16[64,8,2048]{2,1,0:T(8,128)(2,1)}), bf16[64,8,2048]{2,1,0:T(8,128)(2,1)S(1)}, u32[]{:S(2)}, u32[]{:S(2)}) async-start(bf16[64,8,2048]{2,1,0:T(8,128)(2,1)} %bitcast.5), calls=%async_computation | async-start | bytes 4194304 | tf_op jit(solution)/shard_map/all_to_all | solution.py:66
  47.7 0.0 copy-start.7
  47.7 0.0 all-gather.6.cloned.1.call-start
  47.8 0.7 all-gather.6.cloned.1.call-update
  48.5 0.0 all-gather.4.cloned.1.call-start
  48.5 0.7 all-gather.4.cloned.1.call-update
  49.2 1.1 convert_element_type.66
  50.4 0.1 copy.22
  50.5 0.1 mul.97
  50.6 0.9 fusion.2
  51.5 2.3 concatenate.14
  53.8 8.0 %gather_fusion.2 = bf16[512,2048]{1,0:T(8,128)(2,1)} fusion(bf16[1025,2048]{1,0:T(8,128)(2,1)} %concatenate.14, s32[1024]{0:T(1024)S(1)} %get-tuple-element.21), kind=kCustom, calls=%fused_computation.2 | custom fusion | bytes 4196352 | tf_op jit(solution)/shard_map/gather | solution.py:58
  61.8 37.3 %all-to-all-done = bf16[64,8,2048]{2,1,0:T(8,128)(2,1)S(1)} async-done(((bf16[64,8,2048]{2,1,0:T(8,128)(2,1)}), bf16[64,8,2048]{2,1,0:T(8,128)(2,1)S(1)}, u32[]{:S(2)}, u32[]{:S(2)}) %all-to-all-start) | async-done | bytes 2097184 | tf_op jit(solution)/shard_map/all_to_all | solution.py:66
  99.1 1.3 copy-done.1
  100.4 5.3 %all-to-all-start.2 = ((bf16[64,8,2048]{2,1,0:T(8,128)(2,1)}), bf16[64,8,2048]{2,1,0:T(8,128)(2,1)S(1)}, u32[]{:S(2)}, u32[]{:S(2)}) async-start(bf16[64,8,2048]{2,1,0:T(8,128)(2,1)} %bitcast.14), calls=%async_computation.2 | async-start | bytes 4194304 | tf_op jit(solution)/shard_map/all_to_all | solution.py:72
  105.8 0.0 all-gather.8.cloned.1.call-start
  105.8 0.7 all-gather.8.cloned.1.call-update
  106.5 0.2 reduce-scatter.8.cloned.1.call-start
  106.7 0.0 all-gather.6.cloned.1.call-done
  106.8 4.2 %fusion.10 = f32[512,384]{1,0:T(8,128)} fusion(bf16[64,8,2048]{2,1,0:T(8,128)(2,1)} %copy-done.1, bf16[1,2048,384]{2,1,0:T(8,128)(2,1)} %all-gather.6.cloned.1.call-done), kind=kOutput, calls=%fused_computation.24 | convolution fusion | flops 805306368 | bytes 4456448 | tf_op jit(solution)/shard_map/dot_general | solution.py:9
  110.9 4.2 %fusion.12 = f32[512,384]{1,0:T(8,128)} fusion(bf16[64,8,2048]{2,1,0:T(8,128)(2,1)} %copy-done.1, bf16[1,2048,384]{2,1,0:T(8,128)(2,1)} %all-gather.4.cloned.1.call-done), kind=kOutput, calls=%fused_computation.26 | convolution fusion | flops 805306368 | bytes 4456448 | tf_op jit(solution)/shard_map/dot_general | solution.py:8
  115.1 26.3 %all-gather.8.cloned.1.call-done = bf16[1,384,2048]{2,1,0:T(8,128)(2,1)} async-done(((bf16[1,384,512]{2,1,0:T(8,128)(2,1)}), bf16[1,384,2048]{2,1,0:T(8,128)(2,1)}) %all-gather.8.cloned.1.call-update) | async-done | bytes 1572880 | tf_op jit(solution)/shard_map/all_gather | solution.py:65
  141.4 15.7 %all-to-all-done.2 = bf16[64,8,2048]{2,1,0:T(8,128)(2,1)S(1)} async-done(((bf16[64,8,2048]{2,1,0:T(8,128)(2,1)}), bf16[64,8,2048]{2,1,0:T(8,128)(2,1)S(1)}, u32[]{:S(2)}, u32[]{:S(2)}) %all-to-all-start.2) | async-done | bytes 2097184 | tf_op jit(solution)/shard_map/all_to_all | solution.py:72
  157.1 4.2 %multiply_convert_fusion = (bf16[512,384]{1,0:T(8,128)(2,1)}, bf16[512,384]{1,0:T(8,128)(2,1)}, bf16[512,384]{1,0:T(8,128)(2,1)S(1)}) fusion(f32[512,384]{1,0:T(8,128)} %fusion.12, f32[512,384]{1,0:T(8,128)} %fusion.10, bf16[1,384,2048]{2,1,0:T(8,128)(2,1)} %all-gather.8.cloned.1.call-done, bf16[64,8,2048]{2,1,0:T(8,128)(2,1)S(1)} %all-to-all-done.2), kind=kOutput, calls=%fused_computation.35 | convolution fusion | flops 808452096 | bytes 6422528 | tf_op jit(solution)/shard_map/dot_general | solution.py:18
  161.3 0.7 copy-done.6
  162.1 2.2 convolution_convert_fusion.1
  164.2 0.0 reduce-scatter.8.cloned.1.call-update
  164.3 1.4 copy-done.2
  165.7 2.4 fusion.18
  168.1 2.6 fusion.4
  170.7 5.3 %all-to-all-start.3 = ((bf16[64,8,2048]{2,1,0:T(8,128)(2,1)}), bf16[64,8,2048]{2,1,0:T(8,128)(2,1)S(1)}, u32[]{:S(2)}, u32[]{:S(2)}) async-start(bf16[64,8,2048]{2,1,0:T(8,128)(2,1)} %fusion.4), calls=%async_computation.3 | async-start | bytes 4194304 | tf_op jit(solution)/shard_map/all_to_all | solution.py:75
  176.1 0.0 reduce-scatter.4.cloned.1.call-start
  176.1 4.2 %convolution_convert_fusion.3 = bf16[2048,384]{1,0:T(8,128)(2,1)} fusion(bf16[512,384]{1,0:T(8,128)(2,1)} %get-tuple-element.17, bf16[64,8,2048]{2,1,0:T(8,128)(2,1)} %copy-done.1), kind=kOutput, calls=%fused_computation.16 | convolution fusion | flops 806092800 | bytes 4063232 | tf_op jit(solution)/shard_map/dot_general | solution.py:27
  180.3 0.0 reduce-scatter.4.cloned.1.call-update
  180.4 4.1 %fusion.3 = bf16[64,8,2048]{2,1,0:T(8,128)(2,1)} fusion(bf16[512,384]{1,0:T(8,128)(2,1)} %copy-done.6, bf16[1,384,2048]{2,1,0:T(8,128)(2,1)} %all-gather.8.cloned.1.call-done), kind=kOutput, calls=%fused_computation.17 | convolution fusion | flops 806354944 | bytes 4063232 | tf_op jit(solution)/shard_map/dot_general | solution.py:12
  184.5 43.0 %all-to-all-done.3 = bf16[64,8,2048]{2,1,0:T(8,128)(2,1)S(1)} async-done(((bf16[64,8,2048]{2,1,0:T(8,128)(2,1)}), bf16[64,8,2048]{2,1,0:T(8,128)(2,1)S(1)}, u32[]{:S(2)}, u32[]{:S(2)}) %all-to-all-start.3) | async-done | bytes 2097184 | tf_op jit(solution)/shard_map/all_to_all | solution.py:75
  227.4 1.4 copy-done
  228.8 5.6 %all-to-all-start.1 = ((bf16[64,8,2048]{2,1,0:T(8,128)(2,1)}), bf16[64,8,2048]{2,1,0:T(8,128)(2,1)}, u32[]{:S(2)}, u32[]{:S(2)}) async-start(bf16[64,8,2048]{2,1,0:T(8,128)(2,1)} %fusion.3), calls=%async_computation.1 | async-start | bytes 4194304 | tf_op jit(solution)/shard_map/all_to_all | solution.py:69
  234.4 0.3 reduce-scatter.6.cloned.1.call-start
  234.7 4.1 %convolution_convert_fusion.2 = bf16[2048,384]{1,0:T(8,128)(2,1)} fusion(bf16[512,384]{1,0:T(8,128)(2,1)} %get-tuple-element.16, bf16[64,8,2048]{2,1,0:T(8,128)(2,1)} %copy-done.1), kind=kOutput, calls=%fused_computation.15 | convolution fusion | flops 806092800 | bytes 4063232 | tf_op jit(solution)/shard_map/dot_general | solution.py:28
  238.8 0.0 reduce-scatter.6.cloned.1.call-update
  238.8 1.7 concatenate.15
  240.5 45.1 %all-to-all-done.1 = bf16[64,8,2048]{2,1,0:T(8,128)(2,1)} async-done(((bf16[64,8,2048]{2,1,0:T(8,128)(2,1)}), bf16[64,8,2048]{2,1,0:T(8,128)(2,1)}, u32[]{:S(2)}, u32[]{:S(2)}) %all-to-all-start.1) | async-done | bytes 2097184 | tf_op jit(solution)/shard_map/all_to_all | solution.py:69
  285.6 3.2 concatenate.13
  288.8 6.0 %gather_fusion.3 = bf16[1024,2048]{1,0:T(8,128)(2,1)} fusion(bf16[513,2048]{1,0:T(8,128)(2,1)S(1)} %concatenate.15, s32[1024]{0:T(1024)S(1)} %broadcast_clamp_fusion), kind=kCustom, calls=%fused_computation.3 | custom fusion | bytes 8392704 | tf_op jit(solution)/shard_map/gather | solution.py:82
  294.8 10.7 %gather_fusion.1 = bf16[1024,2048]{1,0:T(8,128)(2,1)} fusion(bf16[513,2048]{1,0:T(8,128)(2,1)} %concatenate.13, s32[1024]{0:T(1024)S(1)} %broadcast_clamp_fusion), kind=kCustom, calls=%fused_computation.1 | custom fusion | bytes 8392704 | tf_op jit(solution)/shard_map/gather | solution.py:81
  305.6 5.7 %fusion.1 = (f32[128,8]{1,0:T(8,128)S(1)}, bf16[128,2048]{1,0:T(8,128)(2,1)}) fusion(bf16[1024,2048]{1,0:T(8,128)(2,1)} %gather_fusion.1, f32[128,2048]{1,0:T(8,128)S(1)} %convert_element_type.66, f32[128,8]{1,0:T(8,128)S(1)} %copy.22), kind=kLoop, calls=%fused_computation.8 | loop fusion | flops 10222592 | bytes 5775360 | tf_op jit(solution)/shard_map/reduce_sum | solution.py:85
  311.3 0.7 copy.29
  311.9 5.9 %bitcast_reduce_fusion = bf16[128,2048]{1,0:T(8,128)(2,1)} fusion(bf16[1024,2048]{1,0:T(8,128)(2,1)} %gather_fusion.3), kind=kLoop, calls=%fused_computation.11 | loop fusion | flops 1835008 | bytes 4718592 | tf_op jit(solution)/shard_map/reduce_sum | solution.py:84
  (25 shorter events, 0.2 us)
Async XLA Ops:
  7.2 20.5 %copy-start.8 = (s32[64]{0:T(128)S(1)}, s32[64]{0:T(128)}, u32[]{:S(2)}) copy-start(s32[64]{0:T(128)} %param.12) | copy-start | bytes 772
  7.2 25.0 %copy-start.4 = (bf16[128,2048]{1,0:T(8,128)(2,1)S(1)}, bf16[128,2048]{1,0:T(8,128)(2,1)}, u32[]{:S(2)}) copy-start(bf16[128,2048]{1,0:T(8,128)(2,1)} %param.8) | copy-start | bytes 1572868
  35.6 63.5 %all-to-all-start = ((bf16[64,8,2048]{2,1,0:T(8,128)(2,1)}), bf16[64,8,2048]{2,1,0:T(8,128)(2,1)S(1)}, u32[]{:S(2)}, u32[]{:S(2)}) async-start(bf16[64,8,2048]{2,1,0:T(8,128)(2,1)} %bitcast.5), calls=%async_computation | async-start | bytes 4194304 | tf_op jit(solution)/shard_map/all_to_all | solution.py:66
  47.7 2.6 copy-start.7
  47.7 59.0 %all-gather.6.cloned.1.call-start = ((), (), s32[]{:S(2)}) async-start(), calls=%async_computation.8 | async-start | bytes 1966080 | tf_op jit(solution)/shard_map/all_gather | solution.py:61
  48.5 62.5 %all-gather.4.cloned.1.call-start = ((), (), s32[]{:S(2)}) async-start(), calls=%async_computation.7 | async-start | bytes 1966080 | tf_op jit(solution)/shard_map/all_gather | solution.py:60
  99.1 1.3 copy-start.1
  100.4 56.7 %all-to-all-start.2 = ((bf16[64,8,2048]{2,1,0:T(8,128)(2,1)}), bf16[64,8,2048]{2,1,0:T(8,128)(2,1)S(1)}, u32[]{:S(2)}, u32[]{:S(2)}) async-start(bf16[64,8,2048]{2,1,0:T(8,128)(2,1)} %bitcast.14), calls=%async_computation.2 | async-start | bytes 4194304 | tf_op jit(solution)/shard_map/all_to_all | solution.py:72
  105.8 35.6 %all-gather.8.cloned.1.call-start = ((), (), s32[]{:S(2)}) async-start(), calls=%async_computation.9 | async-start | bytes 1966080 | tf_op jit(solution)/shard_map/all_gather | solution.py:65
  106.5 211.3 %reduce-scatter.8.cloned.1.call-start = ((), (), s32[]{:S(2)}) async-start(), calls=%async_computation.12 | async-start | bytes 1966080 | tf_op jit(solution)/shard_map/reduce_scatter | solution.py:94
  161.3 0.7 copy-start.6
  164.2 1.4 copy-start.2
  165.6 2.4 copy-start.3
  165.6 2.4 copy-start.5
  170.7 56.7 %all-to-all-start.3 = ((bf16[64,8,2048]{2,1,0:T(8,128)(2,1)}), bf16[64,8,2048]{2,1,0:T(8,128)(2,1)S(1)}, u32[]{:S(2)}, u32[]{:S(2)}) async-start(bf16[64,8,2048]{2,1,0:T(8,128)(2,1)} %fusion.4), calls=%async_computation.3 | async-start | bytes 4194304 | tf_op jit(solution)/shard_map/all_to_all | solution.py:75
  176.1 141.7 %reduce-scatter.4.cloned.1.call-start = ((), (), s32[]{:S(2)}) async-start(), calls=%async_computation.10 | async-start | bytes 1966080 | tf_op jit(solution)/shard_map/reduce_scatter | solution.py:87
  227.4 1.4 copy-start
  228.8 56.8 %all-to-all-start.1 = ((bf16[64,8,2048]{2,1,0:T(8,128)(2,1)}), bf16[64,8,2048]{2,1,0:T(8,128)(2,1)}, u32[]{:S(2)}, u32[]{:S(2)}) async-start(bf16[64,8,2048]{2,1,0:T(8,128)(2,1)} %fusion.3), calls=%async_computation.1 | async-start | bytes 4194304 | tf_op jit(solution)/shard_map/all_to_all | solution.py:69
  234.4 83.4 %reduce-scatter.6.cloned.1.call-start = ((), (), s32[]{:S(2)}) async-start(), calls=%async_computation.11 | async-start | bytes 1966080 | tf_op jit(solution)/shard_map/reduce_scatter | solution.py:90
Sparse Core Ops, SparseCore 0:
  50.4 28.9 all-gather.5
  81.2 29.1 all-gather.3
  112.2 29.1 all-gather.7
  164.4 22.8 reduce-scatter.7
  190.3 27.9 reduce-scatter.3
  238.9 27.7 reduce-scatter.5
where the time goes:
time: 326 us; the launch traced here: 325 us
  waiting for transfers between devices  169 us (52%)
  local copies, waits for them, and re-layouts  46.9 us (14%)
  other arithmetic  32.7 us (10%)
  matrix products  32.2 us (10%)
  starting transfers between devices  29 us (9%)
  between operations  14.4 us (4%)
    all_to_all x1, waiting for transfers between devices, on_device(): lax.all_to_all(output.reshape(peers, slot_count, width), 'expert', split_...  45.1 us
    all_to_all x1, waiting for transfers between devices, on_device(): lax.all_to_all(d_rows.reshape(peers, slot_count, width), 'expert', split_...  43 us
    all_to_all x1, waiting for transfers between devices, on_device(): lax.all_to_all(send_tokens, 'expert', split_axis=0, concat_axis=0, tiled=...  37.3 us
    all_gather x1, waiting for transfers between devices, on_device(): wdown = lax.all_gather(w_down, 'dp', axis=2, tiled=True)[0]  26.3 us
    another operation x3, other arithmetic  18.2 us
    all_to_all x1, waiting for transfers between devices, on_device(): lax.all_to_all(send_scaled, 'expert', split_axis=0, concat_axis=0, tiled=...  15.7 us
    all_to_all x1, starting transfers between devices, on_device(): lax.all_to_all(send_tokens, 'expert', split_axis=0, concat_axis=0, tiled=...  12.1 us
    gather x1, local copies, waits for them, and re-layouts, on_device(): padded_output[position].reshape(tok_count, top_count, width)  10.7 us
  transfers between devices with their start and end apart: 10, of which 5 were waited for; matrix products, arithmetic and copies ran while one was open for 22% of the time, Pallas kernels for 0%

commit v1 on v0

v1 whole, which is shorter than its diff:
```python
import functools

import jax
import jax.numpy as jnp
from jax import lax
from jax.experimental import pallas as pl
from jax.experimental.pallas import tpu as pltpu
from jax.sharding import PartitionSpec as P

VMEM_LIMIT = 48 * 2**20
BF = jnp.bfloat16
F32 = jnp.float32


def contract(left, right, left_dim, right_dim):
    return lax.dot_general(
        left, right, (((left_dim,), (right_dim,)), ((), ())), preferred_element_type=F32
    )


def call(body, name, out_shape, args, flops):
    outs = out_shape if isinstance(out_shape, (tuple, list)) else [out_shape]
    moved = sum(a.size * a.dtype.itemsize for a in (*args, *outs))
    return pl.pallas_call(
        body,
        out_shape=out_shape,
        name=name,
        compiler_params=pltpu.CompilerParams(vmem_limit_bytes=VMEM_LIMIT),
        cost_estimate=pl.CostEstimate(flops=flops, bytes_accessed=moved, transcendentals=0),
    )(*args)


def routing(ids, capacity, slots):
    count, top = ids.shape
    lanes = lax.broadcasted_iota(jnp.int32, (count, 128), 1)
    chosen = jnp.zeros((count, 128), F32)
    for k in range(top):
        chosen = chosen + (ids[:, k : k + 1] == lanes).astype(F32)
    earlier = (
        lax.broadcasted_iota(jnp.int32, (count, count), 1)
        < lax.broadcasted_iota(jnp.int32, (count, count), 0)
    ).astype(BF)
    rank = contract(earlier, chosen.astype(BF), 1, 0)
    kept = (chosen > 0.5) & (rank < capacity.astype(F32))
    slot = jnp.where(kept, rank, -1.0)
    return slot.T


def one_hot(slot_of, experts, slots):
    count = slot_of.shape[1]
    wanted = lax.broadcasted_iota(jnp.int32, (experts, slots, count), 1).astype(F32)
    held = jnp.broadcast_to(slot_of[:experts, None, :], (experts, slots, count))
    return (held == wanted).astype(F32).reshape(experts * slots, count)


def weight_of(ids, combine):
    count, top = ids.shape
    lanes = lax.broadcasted_iota(jnp.int32, (count, 128), 1)
    weights = jnp.zeros((count, 128), F32)
    for k in range(top):
        weights = weights + jnp.where(ids[:, k : k + 1] == lanes, combine[:, k : k + 1], 0.0)
    return weights.T


def spread(weights, experts, slots):
    count = weights.shape[1]
    return jnp.broadcast_to(weights[:experts, None, :], (experts, slots, count)).reshape(
        experts * slots, count
    )


def pick_tokens(experts, slots, ids_ref, cap_ref, tokens_ref, out_ref):
    slot_of = routing(ids_ref[...], cap_ref[...], slots)
    pick = one_hot(slot_of, experts, slots).astype(BF)
    width = tokens_ref.shape[1]
    for c in range(0, width, 512):
        out_ref[:, c : c + 512] = contract(pick, tokens_ref[:, c : c + 512], 1, 0).astype(BF)


def pick_scaled(experts, slots, ids_ref, cap_ref, comb_ref, cot_ref, out_ref):
    slot_of = routing(ids_ref[...], cap_ref[...], slots)
    held = one_hot(slot_of, experts, slots)
    weights = spread(weight_of(ids_ref[...], comb_ref[...]), experts, slots)
    scale = jnp.sum(held * weights, axis=1, keepdims=True)
    pick = held.astype(BF)
    width = cot_ref.shape[1]
    for c in range(0, width, 512):
        rows = contract(pick, cot_ref[:, c : c + 512], 1, 0)
        out_ref[:, c : c + 512] = (scale * rows).astype(BF)


def forward(x_ref, wg_ref, wu_ref, wd_ref, o_ref, h_ref, u_ref, a_ref):
    x = x_ref[...]
    h = contract(x, wg_ref[...], 1, 0)
    u = contract(x, wu_ref[...], 1, 0)
    a = (h * jax.nn.sigmoid(h) * u).astype(BF)
    h_ref[...] = h
    u_ref[...] = u
    a_ref[...] = a
    width = o_ref.shape[1]
    for c in range(0, width, 512):
        o_ref[:, c : c + 512] = contract(a, wd_ref[:, c : c + 512], 1, 0).astype(BF)


def backward(g_ref, h_ref, u_ref, wg_ref, wu_ref, wd_ref, dx_ref, dh_ref, du_ref):
    da = contract(g_ref[...], wd_ref[...], 1, 1)
    h = h_ref[...]
    s = jax.nn.sigmoid(h)
    dh = (da * u_ref[...] * s * (1.0 + h * (1.0 - s))).astype(BF)
    du = (da * h * s).astype(BF)
    dh_ref[...] = dh
    du_ref[...] = du
    width = dx_ref.shape[1]
    for c in range(0, width, 512):
        dx_ref[:, c : c + 512] = (
            contract(dh, wg_ref[c : c + 512, :], 1, 1) + contract(du, wu_ref[c : c + 512, :], 1, 1)
        ).astype(BF)


def weight_grads(x_ref, g_ref, a_ref, dh_ref, du_ref, gg_ref, gu_ref, gd_ref):
    width = x_ref.shape[1]
    dh, du, a = dh_ref[...], du_ref[...], a_ref[...]
    for c in range(0, width, 512):
        x = x_ref[:, c : c + 512]
        gg_ref[c : c + 512, :] = contract(x, dh, 0, 0).astype(BF)
        gu_ref[c : c + 512, :] = contract(x, du, 0, 0).astype(BF)
        gd_ref[:, c : c + 512] = contract(a, g_ref[:, c : c + 512], 0, 0).astype(BF)


def merge_outputs(experts, slots, ids_ref, cap_ref, comb_ref, cot_ref, o_ref, mixed_ref, gc_ref):
    ids = ids_ref[...]
    count, top = ids.shape
    slot_of = routing(ids, cap_ref[...], slots)
    held = one_hot(slot_of, experts, slots)
    weights = spread(weight_of(ids, comb_ref[...]), experts, slots)
    share = held * weights
    high = share.astype(BF)
    low = (share - high.astype(F32)).astype(BF)
    width = o_ref.shape[1]
    dots = jnp.zeros(share.shape, F32)
    for c in range(0, width, 512):
        o = o_ref[:, c : c + 512]
        mixed_ref[:, c : c + 512] = (contract(high, o, 0, 0) + contract(low, o, 0, 0)).astype(BF)
        dots = dots + contract(o, cot_ref[:, c : c + 512], 1, 1)
    per_expert = jnp.sum((held * dots).reshape(experts, slots, count), axis=1)
    pad = jnp.zeros((128 - experts, count), F32)
    by_token = jnp.concatenate([per_expert, pad], axis=0).T
    lanes = lax.broadcasted_iota(jnp.int32, (count, 128), 1)
    for k in range(top):
        gc_ref[:, k : k + 1] = jnp.sum(
            jnp.where(ids[:, k : k + 1] == lanes, by_token, 0.0), axis=1, keepdims=True
        )


def merge_rows(experts, slots, ids_ref, cap_ref, dx_ref, out_ref):
    slot_of = routing(ids_ref[...], cap_ref[...], slots)
    pick = one_hot(slot_of, experts, slots).astype(BF)
    width = dx_ref.shape[1]
    for c in range(0, width, 512):
        out_ref[:, c : c + 512] = contract(pick, dx_ref[:, c : c + 512], 0, 0).astype(BF)


def on_device(tokens, cotangent, expert_ids, combine, capacity, w_gate, w_up, w_down):
    peers = lax.axis_size("expert")
    count, width = tokens.shape
    top = expert_ids.shape[1]
    experts = capacity.shape[0]
    slots = count * top // (2 * peers)
    rows = experts * slots
    hidden = w_gate.shape[2]
    limits = jnp.pad(capacity, (0, 128 - experts)).reshape(1, 128)
    ids = expert_ids
    of = jax.ShapeDtypeStruct
    unit = 2 * rows * width * hidden
    pick_flops = 2 * rows * count * width

    def exchange(x):
        x = x.reshape(peers, slots, width)
        return lax.all_to_all(x, "expert", 0, 0, tiled=True).reshape(rows, width)

    part = functools.partial
    sent_x = call(part(pick_tokens, experts, slots), "pick_tokens", of((rows, width), BF), (ids, limits, tokens), pick_flops)
    x = exchange(sent_x)
    sent_g = call(part(pick_scaled, experts, slots), "pick_scaled", of((rows, width), BF), (ids, limits, combine, cotangent), pick_flops)
    wg = lax.all_gather(w_gate[0], "dp", axis=0, tiled=True)
    wu = lax.all_gather(w_up[0], "dp", axis=0, tiled=True)
    wd = lax.all_gather(w_down[0], "dp", axis=1, tiled=True)
    g = exchange(sent_g)
    o, h, u, a = call(
        forward, "forward",
        [of((rows, width), BF), of((rows, hidden), F32), of((rows, hidden), F32), of((rows, hidden), BF)],
        (x, wg, wu, wd), 3 * unit,
    )
    back_o = exchange(o)
    dx, dh, du = call(
        backward, "backward",
        [of((rows, width), BF), of((rows, hidden), BF), of((rows, hidden), BF)],
        (g, h, u, wg, wu, wd), 3 * unit,
    )
    back_dx = exchange(dx)
    gg, gu, gd = call(
        weight_grads, "weight_grads",
        [of((width, hidden), BF), of((width, hidden), BF), of((hidden, width), BF)],
        (x, g, a, dh, du), 3 * unit,
    )
    grad_gate = lax.psum_scatter(gg, "dp", scatter_dimension=0, tiled=True)
    grad_up = lax.psum_scatter(gu, "dp", scatter_dimension=0, tiled=True)
    grad_down = lax.psum_scatter(gd, "dp", scatter_dimension=1, tiled=True)
    mixed, grad_combine = call(
        part(merge_outputs, experts, slots), "merge_outputs",
        [of((count, width), BF), of((count, top), F32)],
        (ids, limits, combine, cotangent, back_o), 3 * pick_flops,
    )
    grad_tokens = call(
        part(merge_rows, experts, slots), "merge_rows", of((count, width), BF), (ids, limits, back_dx), pick_flops
    )
    return (mixed, grad_tokens, grad_combine, grad_gate[None], grad_up[None], grad_down[None])


def solution(mesh):
    rows = P(("dp", "expert"), None)
    return jax.shard_map(
        on_device,
        mesh=mesh,
        in_specs=(rows, rows, rows, rows, P(), P("expert", "dp", None), P("expert", "dp", None), P("expert", None, "dp")),
        out_specs=(rows, rows, rows, P("expert", "dp", None), P("expert", "dp", None), P("expert", None, "dp")),
        check_vma=False,
    )
```

time: 326 us -> 279 us (0.86)
  other arithmetic: 32.7 us -> 0 us
  matrix products: 32.2 us -> 0 us
  Pallas kernels: 0 us -> 29.6 us
  local copies, waits for them, and re-layouts: 46.9 us -> 18.2 us
  waiting for transfers between devices: 169 us -> 186 us
    dot_general x9 -> x0, matrix products: 32.2 us -> none  [the longest x1 4.2 us: backward_part(): d_active = jnp.dot(grads, wdown.T, preferred_element_type=jnp.float32)]
    pallas_call x0 -> x7, Pallas kernels: none -> 29.6 us  [call(): pl.pallas_call(body, out_shape=out_shape, name=name, compiler_params=pltp...]
    gather x4 -> x0, local copies, waits for them, and re-layouts: 28.1 us -> none  [the longest x1 10.7 us: on_device(): padded_output[position].reshape(tok_count, top_count, width)]
    another operation x3 -> x0, other arithmetic: 18.2 us -> none
    reduce_sum x3 -> x0, other arithmetic: 11.7 us -> none  [the longest x1 5.88 us: on_device(): grad_tokens = jnp.sum(picked_rows, axis=1).astype(jnp.bfloat16)]
    unnamed x21 -> x35, local copies, waits for them, and re-layouts: 6.46 us -> 17.5 us
    all_gather x3, waiting for transfers between devices: 26.3 us -> 34.5 us  [the longest x1 31 us: on_device(): wd = lax.all_gather(w_down[0], 'dp', axis=1, tiled=True)]
    concatenate x4 -> x0, local copies, waits for them, and re-layouts: 7.28 us -> none  [the longest x1 3.22 us: on_device(): jnp.concatenate([back_output.reshape(-1, width), zero_row], axis=0)]
  transfers between devices with their start and end apart: 10 -> 10, of which waited for: 5 -> 6; matrix products, arithmetic and copies ran while one was open for 22% -> 0% of each run, Pallas kernels for 0% -> 5%
where the time goes in v1:
time: 279 us; the launch traced here: 277 us
  waiting for transfers between devices  186 us (67%)
  Pallas kernels  29.6 us (11%)
  starting transfers between devices  29.6 us (11%)
  local copies, waits for them, and re-layouts  18.2 us (7%)
  between operations  14.2 us (5%)
    all_to_all x4, waiting for transfers between devices, exchange(): return lax.all_to_all(x, 'expert', 0, 0, tiled=True).reshape(rows, width)  148 us
    all_gather x1, waiting for transfers between devices, on_device(): wd = lax.all_gather(w_down[0], 'dp', axis=1, tiled=True)  31 us
    pallas_call x7, Pallas kernels, call(): pl.pallas_call(body, out_shape=out_shape, name=name, compiler_params=pltp...  29.6 us
    all_to_all x4, starting transfers between devices, exchange(): return lax.all_to_all(x, 'expert', 0, 0, tiled=True).reshape(rows, width)  29.4 us
    unnamed x35, local copies, waits for them, and re-layouts  17.5 us
  transfers between devices with their start and end apart: 10, of which 6 were waited for; matrix products, arithmetic and copies ran while one was open for 0% of the time, Pallas kernels for 5%

profile of v1, /device:TPU:4, one launch (start us, length us, event | category | flops | bytes accessed | tf_op | source)
XLA Modules:
  0.0 277.4 jit_solution(490265991591972705)
XLA Ops:
  7.2 0.8 copy.15.ids_ref
  8.0 0.7 pad_bitcast_fusion.cap_ref
  8.6 0.0 copy-start.4
  8.6 1.0 copy-done.4
  9.7 2.5 pick_tokens.1
  12.2 0.0 copy-start.15
  12.2 0.0 copy-start.5
  12.2 12.2 %all-to-all-start = ((bf16[64,8,2048]{2,1,0:T(8,128)(2,1)}), bf16[64,8,2048]{2,1,0:T(8,128)(2,1)S(1)}, u32[]{:S(2)}, u32[]{:S(2)}) async-start(bf16[64,8,2048]{2,1,0:T(8,128)(2,1)} %bitcast.1), calls=%async_computation | async-start | bytes 4194304 | tf_op jit(solution)/shard_map/all_to_all | solution.py:179
  24.4 0.0 all-gather.7.cloned.1.call-start
  24.5 0.7 all-gather.7.cloned.1.call-update
  25.1 0.0 all-gather.9.cloned.1.call-start
  25.2 0.7 all-gather.9.cloned.1.call-update
  25.9 0.0 copy-done.15
  25.9 0.1 copy.16.comb_ref
  26.0 0.0 copy-done.5
  26.0 2.6 pick_scaled.1
  28.6 47.2 %all-to-all-done = bf16[64,8,2048]{2,1,0:T(8,128)(2,1)S(1)} async-done(((bf16[64,8,2048]{2,1,0:T(8,128)(2,1)}), bf16[64,8,2048]{2,1,0:T(8,128)(2,1)S(1)}, u32[]{:S(2)}, u32[]{:S(2)}) %all-to-all-start) | async-done | bytes 2097184 | tf_op jit(solution)/shard_map/all_to_all | solution.py:179
  75.8 0.0 copy-start.14
  75.8 1.4 copy-done.14
  77.2 5.6 %all-to-all-start.2 = ((bf16[64,8,2048]{2,1,0:T(8,128)(2,1)}), bf16[64,8,2048]{2,1,0:T(8,128)(2,1)}, u32[]{:S(2)}, u32[]{:S(2)}) async-start(bf16[64,8,2048]{2,1,0:T(8,128)(2,1)} %bitcast.8), calls=%async_computation.2 | async-start | bytes 4194304 | tf_op jit(solution)/shard_map/all_to_all | solution.py:179
  82.8 0.0 all-gather.11.cloned.1.call-start
  82.8 0.7 all-gather.11.cloned.1.call-update
  83.5 0.0 reduce-scatter.4.cloned.1.call-start
  83.5 0.0 all-gather.7.cloned.1.call-done
  83.6 3.5 %all-gather.9.cloned.1.call-done = bf16[1,2048,384]{2,1,0:T(8,128)(2,1)} async-done(((bf16[1,512,384]{2,1,0:T(8,128)(2,1)}), bf16[1,2048,384]{2,1,0:T(8,128)(2,1)}) %all-gather.9.cloned.1.call-update) | async-done | bytes 1572880 | tf_op jit(solution)/shard_map/all_gather | solution.py:186
  87.1 31.0 %all-gather.11.cloned.1.call-done = bf16[1,384,2048]{2,1,0:T(8,128)(2,1)} async-done(((bf16[1,384,512]{2,1,0:T(8,128)(2,1)}), bf16[1,384,2048]{2,1,0:T(8,128)(2,1)}) %all-gather.11.cloned.1.call-update) | async-done | bytes 1572880 | tf_op jit(solution)/shard_map/all_gather | solution.py:187
  118.1 0.0 copy-start.6
  118.1 1.4 copy-done.6
  119.5 1.4 copy-done.8
  120.9 0.0 copy-start.7
  120.9 7.0 %forward.1 = (bf16[512,2048]{1,0:T(8,128)(2,1)}, f32[512,384]{1,0:T(8,128)S(1)}, f32[512,384]{1,0:T(8,128)S(1)}, bf16[512,384]{1,0:T(8,128)(2,1)S(1)}) custom-call(bf16[512,2048]{1,0:T(8,128)(2,1)} %bitcast.22, bf16[2048,384]{1,0:T(8,128)(2,1)S(1)} %bitcast.18, bf16[2048,384]{1,0:T(8,128)(2,1)S(1)} %bitcast.20, bf16[384,2048]{1,0:T(8,128)(2,1)} %bitcast.26), custom_call_target="tpu_custom_call" | custom-call | flops 2415919104 | bytes 10878976 | tf_op jit(solution)/shard_map/forward/pallas_call | solution.py:24
  127.9 0.0 copy-start.10
  127.9 0.9 copy-done.10
  128.8 0.0 copy-start.12
  128.8 0.9 copy-done.12
  129.7 4.3 %all-to-all-done.2 = bf16[64,8,2048]{2,1,0:T(8,128)(2,1)} async-done(((bf16[64,8,2048]{2,1,0:T(8,128)(2,1)}), bf16[64,8,2048]{2,1,0:T(8,128)(2,1)}, u32[]{:S(2)}, u32[]{:S(2)}) %all-to-all-start.2) | async-done | bytes 2097184 | tf_op jit(solution)/shard_map/all_to_all | solution.py:179
  134.0 0.0 copy-done.7
  134.0 1.4 copy-done.9
  135.4 0.0 copy-start.11
  135.4 1.1 copy-done.11
  136.5 0.0 copy-start.13
  136.5 1.1 copy-done.13
  137.6 7.1 %backward.1 = (bf16[512,2048]{1,0:T(8,128)(2,1)}, bf16[512,384]{1,0:T(8,128)(2,1)S(1)}, bf16[512,384]{1,0:T(8,128)(2,1)S(1)}) custom-call(bf16[512,2048]{1,0:T(8,128)(2,1)} %bitcast.9.g_ref, f32[512,384]{1,0:T(8,128)S(1)} %copy-done.11, f32[512,384]{1,0:T(8,128)S(1)} %copy-done.13, bf16[2048,384]{1,0:T(8,128)(2,1)S(1)} %bitcast.19, ...), custom_call_target="tpu_custom_call" | custom-call | flops 2415919104 | bytes 11272192 | tf_op jit(solution)/shard_map/backward/pallas_call | solution.py:24
  144.7 6.2 %weight_grads.1 = (bf16[2048,384]{1,0:T(8,128)(2,1)}, bf16[2048,384]{1,0:T(8,128)(2,1)S(1)}, bf16[384,2048]{1,0:T(8,128)(2,1)S(1)}) custom-call(bf16[512,2048]{1,0:T(8,128)(2,1)} %bitcast.23, bf16[512,2048]{1,0:T(8,128)(2,1)} %bitcast.9.g_ref, bf16[512,384]{1,0:T(8,128)(2,1)S(1)} %get-tuple-element.24.a_ref, bf16[512,384]{1,0:T(8,128)(2,1)S(1)} %get-tuple-element.25.dh_ref, ...), custom_call_target="tpu_custom_call" | custom-call | flops 2415919104 | bytes 10092544 | tf_op jit(solution)/shard_map/weight_grads/pallas_call | solution.py:24
  150.9 0.0 copy-start.2
  150.9 1.1 copy-done.2
  152.0 0.0 copy-start.3
  152.0 1.2 copy-done.3
  153.2 0.0 reduce-scatter.4.cloned.1.call-update
  153.2 6.2 %all-to-all-start.1 = ((bf16[64,8,2048]{2,1,0:T(8,128)(2,1)}), bf16[64,8,2048]{2,1,0:T(8,128)(2,1)S(1)}, u32[]{:S(2)}, u32[]{:S(2)}) async-start(bf16[64,8,2048]{2,1,0:T(8,128)(2,1)} %bitcast.25), calls=%async_computation.1 | async-start | bytes 4194304 | tf_op jit(solution)/shard_map/all_to_all | solution.py:179
  159.4 0.0 reduce-scatter.6.cloned.1.call-start
  159.4 0.5 reduce-scatter.6.cloned.1.call-update
  160.0 50.8 %all-to-all-done.1 = bf16[64,8,2048]{2,1,0:T(8,128)(2,1)S(1)} async-done(((bf16[64,8,2048]{2,1,0:T(8,128)(2,1)}), bf16[64,8,2048]{2,1,0:T(8,128)(2,1)S(1)}, u32[]{:S(2)}, u32[]{:S(2)}) %all-to-all-start.1) | async-done | bytes 2097184 | tf_op jit(solution)/shard_map/all_to_all | solution.py:179
  210.8 0.0 copy-start
  210.8 1.4 copy-done
  212.1 5.3 %all-to-all-start.3 = ((bf16[64,8,2048]{2,1,0:T(8,128)(2,1)}), bf16[64,8,2048]{2,1,0:T(8,128)(2,1)S(1)}, u32[]{:S(2)}, u32[]{:S(2)}) async-start(bf16[64,8,2048]{2,1,0:T(8,128)(2,1)} %bitcast.24), calls=%async_computation.3 | async-start | bytes 4194304 | tf_op jit(solution)/shard_map/all_to_all | solution.py:179
  217.5 0.0 reduce-scatter.8.cloned.1.call-start
  217.5 0.5 reduce-scatter.8.cloned.1.call-update
  218.0 0.0 copy-start.1
  218.0 1.6 copy-done.1
  219.6 2.5 merge_outputs.1
  222.1 0.7 copy.20
  222.8 46.0 %all-to-all-done.3 = bf16[64,8,2048]{2,1,0:T(8,128)(2,1)S(1)} async-done(((bf16[64,8,2048]{2,1,0:T(8,128)(2,1)}), bf16[64,8,2048]{2,1,0:T(8,128)(2,1)S(1)}, u32[]{:S(2)}, u32[]{:S(2)}) %all-to-all-start.3) | async-done | bytes 2097184 | tf_op jit(solution)/shard_map/all_to_all | solution.py:179
  268.8 1.8 merge_rows.1
  (5 shorter events, 0.0 us)
Async XLA Ops:
  8.6 1.0 copy-start.4
  12.2 13.7 %copy-start.15 = (f32[128,8]{0,1:T(8,128)S(1)}, f32[128,8]{0,1:T(8,128)}, u32[]{:S(2)}) copy-start(f32[128,8]{0,1:T(8,128)} %param.11) | copy-start | bytes 12292
  12.2 13.9 %copy-start.5 = (bf16[128,2048]{1,0:T(8,128)(2,1)S(1)}, bf16[128,2048]{1,0:T(8,128)(2,1)}, u32[]{:S(2)}) copy-start(bf16[128,2048]{1,0:T(8,128)(2,1)} %cot_ref.3) | copy-start | bytes 1572868
  12.2 63.6 %all-to-all-start = ((bf16[64,8,2048]{2,1,0:T(8,128)(2,1)}), bf16[64,8,2048]{2,1,0:T(8,128)(2,1)S(1)}, u32[]{:S(2)}, u32[]{:S(2)}) async-start(bf16[64,8,2048]{2,1,0:T(8,128)(2,1)} %bitcast.1), calls=%async_computation | async-start | bytes 4194304 | tf_op jit(solution)/shard_map/all_to_all | solution.py:179
  24.4 59.1 %all-gather.7.cloned.1.call-start = ((), (), s32[]{:S(2)}) async-start(), calls=%async_computation.10 | async-start | bytes 1966080 | tf_op jit(solution)/shard_map/all_gather | solution.py:185
  25.1 61.9 %all-gather.9.cloned.1.call-start = ((), (), s32[]{:S(2)}) async-start(), calls=%async_computation.11 | async-start | bytes 1966080 | tf_op jit(solution)/shard_map/all_gather | solution.py:186
  75.8 1.4 copy-start.14
  77.2 56.8 %all-to-all-start.2 = ((bf16[64,8,2048]{2,1,0:T(8,128)(2,1)}), bf16[64,8,2048]{2,1,0:T(8,128)(2,1)}, u32[]{:S(2)}, u32[]{:S(2)}) async-start(bf16[64,8,2048]{2,1,0:T(8,128)(2,1)} %bitcast.8), calls=%async_computation.2 | async-start | bytes 4194304 | tf_op jit(solution)/shard_map/all_to_all | solution.py:179
  82.8 35.3 %all-gather.11.cloned.1.call-start = ((), (), s32[]{:S(2)}) async-start(), calls=%async_computation.12 | async-start | bytes 1966080 | tf_op jit(solution)/shard_map/all_gather | solution.py:187
  83.5 187.1 %reduce-scatter.4.cloned.1.call-start = ((), (), s32[]{:S(2)}) async-start(), calls=%async_computation.7 | async-start | bytes 1966080 | tf_op jit(solution)/shard_map/reduce_scatter | solution.py:206
  118.1 1.4 copy-start.6
  119.5 1.4 copy-start.8
  120.9 13.1 %copy-start.7 = (bf16[1,2048,384]{2,1,0:T(8,128)(2,1)S(1)}, bf16[1,2048,384]{2,1,0:T(8,128)(2,1)}, u32[]{:S(2)}) copy-start(bf16[1,2048,384]{2,1,0:T(8,128)(2,1)} %all-gather.7.cloned.1.call-done) | copy-start | bytes 4718596
  127.9 0.9 copy-start.10
  128.8 0.9 copy-start.12
  134.0 1.4 copy-start.9
  135.4 1.1 copy-start.11
  136.5 1.1 copy-start.13
  150.9 1.1 copy-start.2
  152.0 1.2 copy-start.3
  153.2 57.6 %all-to-all-start.1 = ((bf16[64,8,2048]{2,1,0:T(8,128)(2,1)}), bf16[64,8,2048]{2,1,0:T(8,128)(2,1)S(1)}, u32[]{:S(2)}, u32[]{:S(2)}) async-start(bf16[64,8,2048]{2,1,0:T(8,128)(2,1)} %bitcast.25), calls=%async_computation.1 | async-start | bytes 4194304 | tf_op jit(solution)/shard_map/all_to_all | solution.py:179
  159.4 111.2 %reduce-scatter.6.cloned.1.call-start = ((), (), s32[]{:S(2)}) async-start(), calls=%async_computation.8 | async-start | bytes 1966080 | tf_op jit(solution)/shard_map/reduce_scatter | solution.py:207
  210.8 1.4 copy-start
  212.1 56.7 %all-to-all-start.3 = ((bf16[64,8,2048]{2,1,0:T(8,128)(2,1)}), bf16[64,8,2048]{2,1,0:T(8,128)(2,1)S(1)}, u32[]{:S(2)}, u32[]{:S(2)}) async-start(bf16[64,8,2048]{2,1,0:T(8,128)(2,1)} %bitcast.24), calls=%async_computation.3 | async-start | bytes 4194304 | tf_op jit(solution)/shard_map/all_to_all | solution.py:179
  217.5 53.1 %reduce-scatter.8.cloned.1.call-start = ((), (), s32[]{:S(2)}) async-start(), calls=%async_computation.9 | async-start | bytes 1966080 | tf_op jit(solution)/shard_map/reduce_scatter | solution.py:208
  218.0 1.6 copy-start.1
Sparse Core Ops, SparseCore 0:
  27.1 28.9 all-gather.6
  57.9 29.1 all-gather.8
  88.9 29.1 all-gather.10
  153.3 23.6 reduce-scatter.3
  180.0 27.9 reduce-scatter.5
  221.1 27.8 reduce-scatter.7

commit v2 on v1

v2 whole, which is shorter than its diff:
```python
import functools

import jax
import jax.numpy as jnp
from jax import lax
from jax.experimental import pallas as pl
from jax.experimental.pallas import tpu as pltpu
from jax.sharding import PartitionSpec as P

VMEM_LIMIT = 48 * 2**20
BF = jnp.bfloat16
F32 = jnp.float32


def contract(left, right, left_dim, right_dim):
    return lax.dot_general(
        left, right, (((left_dim,), (right_dim,)), ((), ())), preferred_element_type=F32
    )


def call(body, name, out_shape, args, flops):
    outs = out_shape if isinstance(out_shape, (tuple, list)) else [out_shape]
    moved = sum(a.size * a.dtype.itemsize for a in (*args, *outs))
    return pl.pallas_call(
        body,
        out_shape=out_shape,
        name=name,
        compiler_params=pltpu.CompilerParams(vmem_limit_bytes=VMEM_LIMIT),
        cost_estimate=pl.CostEstimate(flops=flops, bytes_accessed=moved, transcendentals=0),
    )(*args)


def routing(ids, capacity, slots):
    count, top = ids.shape
    lanes = lax.broadcasted_iota(jnp.int32, (count, 128), 1)
    chosen = jnp.zeros((count, 128), F32)
    for k in range(top):
        chosen = chosen + (ids[:, k : k + 1] == lanes).astype(F32)
    earlier = (
        lax.broadcasted_iota(jnp.int32, (count, count), 1)
        < lax.broadcasted_iota(jnp.int32, (count, count), 0)
    ).astype(BF)
    rank = contract(earlier, chosen.astype(BF), 1, 0)
    kept = (chosen > 0.5) & (rank < capacity.astype(F32))
    slot = jnp.where(kept, rank, -1.0)
    return slot.T


def one_hot(slot_of, experts, slots):
    count = slot_of.shape[1]
    wanted = lax.broadcasted_iota(jnp.int32, (experts, slots, count), 1).astype(F32)
    held = jnp.broadcast_to(slot_of[:experts, None, :], (experts, slots, count))
    return (held == wanted).astype(F32).reshape(experts * slots, count)


def weight_of(ids, combine):
    count, top = ids.shape
    lanes = lax.broadcasted_iota(jnp.int32, (count, 128), 1)
    weights = jnp.zeros((count, 128), F32)
    for k in range(top):
        weights = weights + jnp.where(ids[:, k : k + 1] == lanes, combine[:, k : k + 1], 0.0)
    return weights.T


def spread(weights, experts, slots):
    count = weights.shape[1]
    return jnp.broadcast_to(weights[:experts, None, :], (experts, slots, count)).reshape(
        experts * slots, count
    )


def pick_rows(experts, slots, ids_ref, cap_ref, comb_ref, tokens_ref, cot_ref, out_ref):
    slot_of = routing(ids_ref[...], cap_ref[...], slots)
    held = one_hot(slot_of, experts, slots)
    weights = spread(weight_of(ids_ref[...], comb_ref[...]), experts, slots)
    scale = jnp.sum(held * weights, axis=1, keepdims=True)
    pick = held.astype(BF)
    width = tokens_ref.shape[1]
    for c in range(0, width, 512):
        out_ref[:, c : c + 512] = contract(pick, tokens_ref[:, c : c + 512], 1, 0).astype(BF)
    for c in range(0, width, 512):
        rows = contract(pick, cot_ref[:, c : c + 512], 1, 0)
        out_ref[:, width + c : width + c + 512] = (scale * rows).astype(BF)


def expert_math(xg_ref, wg_ref, wu_ref, wd_ref, od_ref, a_ref, dh_ref, du_ref):
    width = wg_ref.shape[0]
    x = xg_ref[:, :width]
    h = contract(x, wg_ref[...], 1, 0)
    u = contract(x, wu_ref[...], 1, 0)
    s = jax.nn.sigmoid(h)
    a = (h * s * u).astype(BF)
    a_ref[...] = a
    for c in range(0, width, 512):
        od_ref[:, c : c + 512] = contract(a, wd_ref[:, c : c + 512], 1, 0).astype(BF)
    da = contract(xg_ref[:, width:], wd_ref[...], 1, 1)
    dh = (da * u * s * (1.0 + h * (1.0 - s))).astype(BF)
    du = (da * h * s).astype(BF)
    dh_ref[...] = dh
    du_ref[...] = du
    for c in range(0, width, 512):
        od_ref[:, width + c : width + c + 512] = (
            contract(dh, wg_ref[c : c + 512, :], 1, 1) + contract(du, wu_ref[c : c + 512, :], 1, 1)
        ).astype(BF)


def weight_grads(xg_ref, a_ref, dh_ref, du_ref, gg_ref, gu_ref, gd_ref):
    width = gg_ref.shape[0]
    dh, du, a = dh_ref[...], du_ref[...], a_ref[...]
    for c in range(0, width, 512):
        x = xg_ref[:, c : c + 512]
        gg_ref[c : c + 512, :] = contract(x, dh, 0, 0).astype(BF)
        gu_ref[c : c + 512, :] = contract(x, du, 0, 0).astype(BF)
        gd_ref[:, c : c + 512] = contract(a, xg_ref[:, width + c : width + c + 512], 0, 0).astype(BF)


def merge(experts, slots, ids_ref, cap_ref, comb_ref, cot_ref, od_ref, mixed_ref, rows_ref, gc_ref):
    ids = ids_ref[...]
    count, top = ids.shape
    slot_of = routing(ids, cap_ref[...], slots)
    held = one_hot(slot_of, experts, slots)
    weights = spread(weight_of(ids, comb_ref[...]), experts, slots)
    share = held * weights
    high = share.astype(BF)
    low = (share - high.astype(F32)).astype(BF)
    width = cot_ref.shape[1]
    dots = jnp.zeros(share.shape, F32)
    for c in range(0, width, 512):
        o = od_ref[:, c : c + 512]
        mixed_ref[:, c : c + 512] = (contract(high, o, 0, 0) + contract(low, o, 0, 0)).astype(BF)
        dots = dots + contract(o, cot_ref[:, c : c + 512], 1, 1)
    pick = held.astype(BF)
    for c in range(0, width, 512):
        rows_ref[:, c : c + 512] = contract(pick, od_ref[:, width + c : width + c + 512], 0, 0).astype(BF)
    per_expert = jnp.sum((held * dots).reshape(experts, slots, count), axis=1)
    pad = jnp.zeros((128 - experts, count), F32)
    by_token = jnp.concatenate([per_expert, pad], axis=0).T
    lanes = lax.broadcasted_iota(jnp.int32, (count, 128), 1)
    for k in range(top):
        gc_ref[:, k : k + 1] = jnp.sum(
            jnp.where(ids[:, k : k + 1] == lanes, by_token, 0.0), axis=1, keepdims=True
        )


def on_device(tokens, cotangent, expert_ids, combine, capacity, w_gate, w_up, w_down):
    peers = lax.axis_size("expert")
    count, width = tokens.shape
    top = expert_ids.shape[1]
    experts = capacity.shape[0]
    slots = count * top // (2 * peers)
    rows = experts * slots
    hidden = w_gate.shape[2]
    limits = jnp.pad(capacity, (0, 128 - experts)).reshape(1, 128)
    ids = expert_ids
    of = jax.ShapeDtypeStruct
    unit = 2 * rows * width * hidden
    pick_flops = 2 * rows * count * width

    def exchange(x):
        x = x.reshape(peers, slots, 2 * width)
        return lax.all_to_all(x, "expert", 0, 0, tiled=True).reshape(rows, 2 * width)

    part = functools.partial
    sent = call(
        part(pick_rows, experts, slots), "pick_rows", of((rows, 2 * width), BF),
        (ids, limits, combine, tokens, cotangent), 2 * pick_flops,
    )
    xg = exchange(sent)
    wg = lax.all_gather(w_gate[0], "dp", axis=0, tiled=True)
    wu = lax.all_gather(w_up[0], "dp", axis=0, tiled=True)
    wd = lax.all_gather(w_down[0], "dp", axis=1, tiled=True)
    od, a, dh, du = call(
        expert_math, "expert_math",
        [of((rows, 2 * width), BF), of((rows, hidden), BF), of((rows, hidden), BF), of((rows, hidden), BF)],
        (xg, wg, wu, wd), 6 * unit,
    )
    back = exchange(od)
    gg, gu, gd = call(
        weight_grads, "weight_grads",
        [of((width, hidden), BF), of((width, hidden), BF), of((hidden, width), BF)],
        (xg, a, dh, du), 3 * unit,
    )
    grad_gate = lax.psum_scatter(gg, "dp", scatter_dimension=0, tiled=True)
    grad_up = lax.psum_scatter(gu, "dp", scatter_dimension=0, tiled=True)
    grad_down = lax.psum_scatter(gd, "dp", scatter_dimension=1, tiled=True)
    mixed, grad_tokens, grad_combine = call(
        part(merge, experts, slots), "merge",
        [of((count, width), BF), of((count, width), BF), of((count, top), F32)],
        (ids, limits, combine, cotangent, back), 4 * pick_flops,
    )
    return (mixed, grad_tokens, grad_combine, grad_gate[None], grad_up[None], grad_down[None])


def solution(mesh):
    rows = P(("dp", "expert"), None)
    return jax.shard_map(
        on_device,
        mesh=mesh,
        in_specs=(rows, rows, rows, rows, P(), P("expert", "dp", None), P("expert", "dp", None), P("expert", None, "dp")),
        out_specs=(rows, rows, rows, P("expert", "dp", None), P("expert", "dp", None), P("expert", None, "dp")),
        check_vma=False,
    )
```

time: 279 us -> 265 us (0.950)
  starting transfers between devices: 29.6 us -> 20.7 us
  local copies, waits for them, and re-layouts: 18.2 us -> 11.2 us
  waiting for transfers between devices: 186 us -> 192 us
  Pallas kernels: 29.6 us -> 25.1 us
    all_to_all x4 -> x2, waiting for transfers between devices: 148 us -> 97.7 us  [exchange(): lax.all_to_all(x, 'expert', 0, 0, tiled=True).reshape(rows, 2 * width)]
    all_gather x1, waiting for transfers between devices: 0.02 us -> 29.3 us  [on_device(): wg = lax.all_gather(w_gate[0], 'dp', axis=0, tiled=True)]
    all_gather x1, waiting for transfers between devices: 3.51 us -> 31 us  [on_device(): wu = lax.all_gather(w_up[0], 'dp', axis=0, tiled=True)]
    all_to_all x4 -> x2, starting transfers between devices: 29.4 us -> 20.5 us  [exchange(): lax.all_to_all(x, 'expert', 0, 0, tiled=True).reshape(rows, 2 * width)]
    unnamed x35 -> x17, local copies, waits for them, and re-layouts: 17.5 us -> 10.5 us
    pallas_call x7 -> x4, Pallas kernels: 29.6 us -> 25.1 us  [call(): pl.pallas_call(body, out_shape=out_shape, name=name, compiler_params=pltp...]
  transfers between devices with their start and end apart: 10 -> 8, of which waited for: 6 -> 5; matrix products, arithmetic and copies ran while one was open for 0% -> 0% of each run, Pallas kernels for 5% -> 2%
where the time goes in v2:
time: 265 us; the launch traced here: 263 us
  waiting for transfers between devices  192 us (72%)
  Pallas kernels  25.1 us (9%)
  starting transfers between devices  20.7 us (8%)
  between operations  14.2 us (5%)
  local copies, waits for them, and re-layouts  11.2 us (4%)
    all_to_all x2, waiting for transfers between devices, exchange(): lax.all_to_all(x, 'expert', 0, 0, tiled=True).reshape(rows, 2 * width)  97.7 us
    all_gather x1, waiting for transfers between devices, on_device(): wd = lax.all_gather(w_down[0], 'dp', axis=1, tiled=True)  31 us
    all_gather x1, waiting for transfers between devices, on_device(): wu = lax.all_gather(w_up[0], 'dp', axis=0, tiled=True)  31 us
    all_gather x1, waiting for transfers between devices, on_device(): wg = lax.all_gather(w_gate[0], 'dp', axis=0, tiled=True)  29.3 us
    pallas_call x4, Pallas kernels, call(): pl.pallas_call(body, out_shape=out_shape, name=name, compiler_params=pltp...  25.1 us
    all_to_all x2, starting transfers between devices, exchange(): lax.all_to_all(x, 'expert', 0, 0, tiled=True).reshape(rows, 2 * width)  20.5 us
    unnamed x17, local copies, waits for them, and re-layouts  10.5 us
  transfers between devices with their start and end apart: 8, of which 5 were waited for; matrix products, arithmetic and copies ran while one was open for 0% of the time, Pallas kernels for 2%

profile of v2, /device:TPU:4, one launch (start us, length us, event | category | flops | bytes accessed | tf_op | source)
XLA Modules:
  0.0 263.3 jit_solution(8390106319208317311)
XLA Ops:
  7.2 0.7 pad_bitcast_fusion.cap_ref
  7.8 0.8 copy.16.ids_ref
  8.6 0.8 copy.17.comb_ref
  9.4 0.0 copy-start.1
  9.4 1.0 copy-done.1
  10.4 0.0 copy-start.3
  10.4 1.0 copy-done.3
  11.5 1.7 pick_rows.1
  13.2 0.0 copy-start
  13.2 2.0 copy-done
  15.2 12.4 %all-to-all-start = ((bf16[64,8,4096]{2,1,0:T(8,128)(2,1)}), bf16[64,8,4096]{2,1,0:T(8,128)(2,1)}, u32[]{:S(2)}, u32[]{:S(2)}) async-start(bf16[64,8,4096]{2,1,0:T(8,128)(2,1)} %bitcast.12), calls=%async_computation | async-start | bytes 8388608 | tf_op jit(solution)/shard_map/all_to_all | solution.py:161
  27.6 0.0 all-gather.7.cloned.1.call-start
  27.6 0.7 all-gather.7.cloned.1.call-update
  28.3 0.0 all-gather.9.cloned.1.call-start
  28.4 0.7 all-gather.9.cloned.1.call-update
  29.1 0.0 all-gather.11.cloned.1.call-start
  29.1 0.7 all-gather.11.cloned.1.call-update
  29.8 0.0 reduce-scatter.4.cloned.1.call-start
  29.9 29.3 %all-gather.7.cloned.1.call-done = bf16[1,2048,384]{2,1,0:T(8,128)(2,1)} async-done(((bf16[1,512,384]{2,1,0:T(8,128)(2,1)}), bf16[1,2048,384]{2,1,0:T(8,128)(2,1)}) %all-gather.7.cloned.1.call-update) | async-done | bytes 1572880 | tf_op jit(solution)/shard_map/all_gather | solution.py:169
  59.2 31.0 %all-gather.9.cloned.1.call-done = bf16[1,2048,384]{2,1,0:T(8,128)(2,1)} async-done(((bf16[1,512,384]{2,1,0:T(8,128)(2,1)}), bf16[1,2048,384]{2,1,0:T(8,128)(2,1)}) %all-gather.9.cloned.1.call-update) | async-done | bytes 1572880 | tf_op jit(solution)/shard_map/all_gather | solution.py:170
  90.2 31.0 %all-gather.11.cloned.1.call-done = bf16[1,384,2048]{2,1,0:T(8,128)(2,1)} async-done(((bf16[1,384,512]{2,1,0:T(8,128)(2,1)}), bf16[1,384,2048]{2,1,0:T(8,128)(2,1)}) %all-gather.11.cloned.1.call-update) | async-done | bytes 1572880 | tf_op jit(solution)/shard_map/all_gather | solution.py:171
  121.2 2.6 all-to-all-done
  123.8 0.0 copy-start.4
  123.8 1.4 copy-done.4
  125.2 0.0 copy-start.5
  125.2 1.4 copy-done.5
  126.6 0.0 copy-start.6
  126.6 1.4 copy-done.6
  128.1 11.1 %expert_math.1 = (bf16[512,4096]{1,0:T(8,128)(2,1)}, bf16[512,384]{1,0:T(8,128)(2,1)S(1)}, bf16[512,384]{1,0:T(8,128)(2,1)S(1)}, bf16[512,384]{1,0:T(8,128)(2,1)S(1)}) custom-call(bf16[512,4096]{1,0:T(8,128)(2,1)} %bitcast.2.xg_ref, bf16[2048,384]{1,0:T(8,128)(2,1)S(1)} %bitcast.13, bf16[2048,384]{1,0:T(8,128)(2,1)S(1)} %bitcast.14, ...), custom_call_target="tpu_custom_call" | custom-call | flops 4831838208 | bytes 14286848 | tf_op jit(solution)/shard_map/expert_math/pallas_call | solution.py:24
  139.1 7.2 %weight_grads.1 = (bf16[2048,384]{1,0:T(8,128)(2,1)}, bf16[2048,384]{1,0:T(8,128)(2,1)}, bf16[384,2048]{1,0:T(8,128)(2,1)}) custom-call(bf16[512,4096]{1,0:T(8,128)(2,1)} %bitcast.2.xg_ref, bf16[512,384]{1,0:T(8,128)(2,1)S(1)} %get-tuple-element.20.a_ref, bf16[512,384]{1,0:T(8,128)(2,1)S(1)} %get-tuple-element.21.dh_ref, ...), custom_call_target="tpu_custom_call" | custom-call | flops 2415919104 | bytes 10092544 | tf_op jit(solution)/shard_map/weight_grads/pallas_call | solution.py:24
  146.3 0.0 reduce-scatter.4.cloned.1.call-update
  146.3 8.1 %all-to-all-start.1 = ((bf16[64,8,4096]{2,1,0:T(8,128)(2,1)}), bf16[64,8,4096]{2,1,0:T(8,128)(2,1)}, u32[]{:S(2)}, u32[]{:S(2)}) async-start(bf16[64,8,4096]{2,1,0:T(8,128)(2,1)} %bitcast.16), calls=%async_computation.1 | async-start | bytes 8388608 | tf_op jit(solution)/shard_map/all_to_all | solution.py:161
  154.5 0.0 reduce-scatter.6.cloned.1.call-start
  154.5 0.0 copy-start.2
  154.5 0.5 reduce-scatter.6.cloned.1.call-update
  155.0 0.0 reduce-scatter.8.cloned.1.call-start
  155.1 0.5 reduce-scatter.8.cloned.1.call-update
  155.6 95.1 %all-to-all-done.1 = bf16[64,8,4096]{2,1,0:T(8,128)(2,1)} async-done(((bf16[64,8,4096]{2,1,0:T(8,128)(2,1)}), bf16[64,8,4096]{2,1,0:T(8,128)(2,1)}, u32[]{:S(2)}, u32[]{:S(2)}) %all-to-all-start.1) | async-done | bytes 4194336 | tf_op jit(solution)/shard_map/all_to_all | solution.py:161
  250.7 0.0 copy-done.2
  250.7 5.1 %merge.1 = (bf16[128,2048]{1,0:T(8,128)(2,1)}, bf16[128,2048]{1,0:T(8,128)(2,1)}, f32[128,8]{1,0:T(8,128)S(1)}) custom-call(s32[128,8]{1,0:T(8,128)S(1)} %copy.16.ids_ref, s32[1,128]{1,0:T(1,128)S(1)} %pad_bitcast_fusion.cap_ref, f32[128,8]{1,0:T(8,128)S(1)} %copy.17.comb_ref, bf16[128,2048]{1,0:T(8,128)(2,1)S(1)} %copy-done.2, bf16[512,4096]{1,0:T(8,128)(2,1)} %bitcast.7.od_ref), custom_call_target="tpu_custom_call" | custom-call | flops 1073741824 | bytes 5779968 | tf_op jit(solution)/shard_map/merge/pallas_call | solution.py:24
  255.8 0.7 copy.18
  256.5 0.0 reduce-scatter.4.cloned.1.call-done
  256.5 0.0 reduce-scatter.6.cloned.1.call-done
  256.5 0.0 reduce-scatter.8.cloned.1.call-done
Async XLA Ops:
  9.4 1.0 copy-start.1
  10.4 1.0 copy-start.3
  13.2 2.0 copy-start
  15.2 108.6 %all-to-all-start = ((bf16[64,8,4096]{2,1,0:T(8,128)(2,1)}), bf16[64,8,4096]{2,1,0:T(8,128)(2,1)}, u32[]{:S(2)}, u32[]{:S(2)}) async-start(bf16[64,8,4096]{2,1,0:T(8,128)(2,1)} %bitcast.12), calls=%async_computation | async-start | bytes 8388608 | tf_op jit(solution)/shard_map/all_to_all | solution.py:161
  27.6 31.6 %all-gather.7.cloned.1.call-start = ((), (), s32[]{:S(2)}) async-start(), calls=%async_computation.8 | async-start | bytes 1966080 | tf_op jit(solution)/shard_map/all_gather | solution.py:169
  28.3 61.9 %all-gather.9.cloned.1.call-start = ((), (), s32[]{:S(2)}) async-start(), calls=%async_computation.9 | async-start | bytes 1966080 | tf_op jit(solution)/shard_map/all_gather | solution.py:170
  29.1 92.1 %all-gather.11.cloned.1.call-start = ((), (), s32[]{:S(2)}) async-start(), calls=%async_computation.10 | async-start | bytes 1966080 | tf_op jit(solution)/shard_map/all_gather | solution.py:171
  29.8 226.7 %reduce-scatter.4.cloned.1.call-start = ((), (), s32[]{:S(2)}) async-start(), calls=%async_computation.5 | async-start | bytes 1966080 | tf_op jit(solution)/shard_map/reduce_scatter | solution.py:183
  123.8 1.4 copy-start.4
  125.2 1.4 copy-start.5
  126.6 1.4 copy-start.6
  146.3 104.4 %all-to-all-start.1 = ((bf16[64,8,4096]{2,1,0:T(8,128)(2,1)}), bf16[64,8,4096]{2,1,0:T(8,128)(2,1)}, u32[]{:S(2)}, u32[]{:S(2)}) async-start(bf16[64,8,4096]{2,1,0:T(8,128)(2,1)} %bitcast.16), calls=%async_computation.1 | async-start | bytes 8388608 | tf_op jit(solution)/shard_map/all_to_all | solution.py:161
  154.5 102.0 %reduce-scatter.6.cloned.1.call-start = ((), (), s32[]{:S(2)}) async-start(), calls=%async_computation.6 | async-start | bytes 1966080 | tf_op jit(solution)/shard_map/reduce_scatter | solution.py:184
  154.5 96.2 %copy-start.2 = (bf16[128,2048]{1,0:T(8,128)(2,1)S(1)}, bf16[128,2048]{1,0:T(8,128)(2,1)}, u32[]{:S(2)}) copy-start(bf16[128,2048]{1,0:T(8,128)(2,1)} %cot_ref.3) | copy-start | bytes 1572868
  155.0 101.4 %reduce-scatter.8.cloned.1.call-start = ((), (), s32[]{:S(2)}) async-start(), calls=%async_computation.7 | async-start | bytes 1966080 | tf_op jit(solution)/shard_map/reduce_scatter | solution.py:185
Sparse Core Ops, SparseCore 0:
  30.2 28.8 all-gather.6
  61.0 29.1 all-gather.8
  92.0 29.1 all-gather.10
  146.4 25.3 reduce-scatter.3
  174.8 27.9 reduce-scatter.5
  205.8 27.9 reduce-scatter.7

commit v3 on v0

v3 whole, which is shorter than its diff:
```python
import functools

import jax
import jax.numpy as jnp
from jax import lax
from jax.experimental import pallas as pl
from jax.experimental.pallas import tpu as pltpu
from jax.sharding import PartitionSpec as P

MIB = 2**20
BF = jnp.bfloat16
F32 = jnp.float32
STEP = 512


def contract(left, right, left_dim, right_dim):
    return lax.dot_general(
        left, right, (((left_dim,), (right_dim,)), ((), ())), preferred_element_type=F32
    )


def together(*arrays):
    return lax.optimization_barrier(arrays)


def hits(ids_ref, cap_ref, slots):
    top, count = ids_ref.shape
    experts = cap_ref.shape[1]
    numbers = lax.broadcasted_iota(jnp.int32, (experts, count), 0)
    chosen = [ids_ref[k : k + 1, :] == numbers for k in range(top)]
    taken = sum(c.astype(F32) for c in chosen)
    earlier = (
        lax.broadcasted_iota(jnp.int32, (count, count), 0)
        < lax.broadcasted_iota(jnp.int32, (count, count), 1)
    ).astype(BF)
    rank = contract(taken.astype(BF), earlier, 1, 0)
    same = lax.broadcasted_iota(jnp.int32, (experts, experts), 0) == lax.broadcasted_iota(
        jnp.int32, (experts, experts), 1
    )
    limit = jnp.sum(jnp.where(same, cap_ref[...].astype(F32), 0.0), axis=1, keepdims=True)
    slot_of = jnp.where((taken > 0.5) & (rank < limit), rank, -1.0)
    wanted = lax.broadcasted_iota(jnp.int32, (experts, slots, count), 1).astype(F32)
    held = (jnp.broadcast_to(slot_of[:, None, :], (experts, slots, count)) == wanted).astype(F32)
    return held.reshape(experts * slots, count), chosen


def shares(held, chosen, comb_ref, slots):
    weights = sum(jnp.where(c, comb_ref[k : k + 1, :], 0.0) for k, c in enumerate(chosen))
    experts, count = weights.shape
    spread = jnp.broadcast_to(weights[:, None, :], (experts, slots, count)).reshape(experts * slots, count)
    return held * spread


def pick_rows(slots, ids_ref, cap_ref, comb_ref, tokens_ref, cot_ref, out_ref, pick_ref, scale_ref):
    i = pl.program_id(0)
    steps = pl.num_programs(0)

    @pl.when(i == 0)
    def _():
        held, chosen = hits(ids_ref, cap_ref, slots)
        pick_ref[...] = held.astype(BF)
        scale = jnp.sum(shares(held, chosen, comb_ref, slots), axis=1, keepdims=True)
        scale_ref[...] = jnp.broadcast_to(scale, scale_ref.shape)

    wide = out_ref.shape[1]

    @pl.when(i < steps // 2)
    def _():
        for c in range(0, wide, STEP):
            out_ref[:, c : c + STEP] = contract(pick_ref[...], tokens_ref[:, c : c + STEP], 1, 0).astype(BF)

    @pl.when(i >= steps // 2)
    def _():
        scale = scale_ref[:, :1]
        for c in range(0, wide, STEP):
            rows = contract(pick_ref[...], cot_ref[:, c : c + STEP], 1, 0)
            out_ref[:, c : c + STEP] = (scale * rows).astype(BF)


def stack_weights(gate_ref, up_ref, down_ref, out_ref):
    out_ref[0] = gate_ref[...]
    out_ref[1] = up_ref[...]
    out_ref[2] = down_ref[...].T


def expert_math(xg_hbm, w_hbm, od_hbm, saved_ref, xg_ref, w_ref, od_ref, in_sems, w_sems, out_sems):
    parts, _, deep, hidden = w_ref.shape

    def piece(ref, d):
        return ref.at[:, pl.ds(d * deep, deep)]

    def arrive(d):
        return pltpu.make_async_copy(piece(xg_hbm, d), piece(xg_ref, d), in_sems.at[d])

    def weights(d):
        if d < parts:
            return pltpu.make_async_copy(w_hbm.at[d, pl.ds(0, 2)], w_ref.at[d, pl.ds(0, 2)], w_sems.at[d])
        d -= parts
        return pltpu.make_async_copy(w_hbm.at[d, 2], w_ref.at[d, 2], w_sems.at[parts + d])

    def leave(d):
        return pltpu.make_async_copy(piece(od_ref, d), piece(od_hbm, d), out_sems.at[d])

    for d in range(parts):
        weights(d).start()
        arrive(d).start()
    for d in range(parts):
        weights(parts + d).start()
    for d in range(parts):
        arrive(parts + d).start()
    h = u = da = 0.0
    for d in range(parts):
        weights(d).wait()
        arrive(d).wait()
        x = xg_ref[:, d * deep : (d + 1) * deep]
        h = h + contract(x, w_ref[d, 0], 1, 0)
        u = u + contract(x, w_ref[d, 1], 1, 0)
    s = jax.nn.sigmoid(h)
    a = (h * s * u).astype(BF)
    saved_ref[:, :hidden] = a
    for d in range(parts):
        weights(parts + d).wait()
        od_ref[:, d * deep : (d + 1) * deep] = contract(a, w_ref[d, 2], 1, 1).astype(BF)
        leave(d).start()
    for d in range(parts):
        arrive(parts + d).wait()
        da = da + contract(xg_ref[:, (parts + d) * deep : (parts + d + 1) * deep], w_ref[d, 2], 1, 0)
    dh = (da * u * s * (1.0 + h * (1.0 - s))).astype(BF)
    du = (da * h * s).astype(BF)
    saved_ref[:, hidden : 2 * hidden] = dh
    saved_ref[:, 2 * hidden :] = du
    for d in range(parts):
        n = parts + d
        od_ref[:, n * deep : (n + 1) * deep] = (
            contract(dh, w_ref[d, 0], 1, 1) + contract(du, w_ref[d, 1], 1, 1)
        ).astype(BF)
        leave(n).start()
    for d in range(2 * parts):
        leave(d).wait()


def unstack_weights(in_ref, gate_ref, up_ref, down_ref):
    gate_ref[...] = in_ref[0]
    up_ref[...] = in_ref[1]
    down_ref[...] = in_ref[2].T


def weight_grads(x_ref, g_ref, saved_ref, out_ref):
    hidden = out_ref.shape[3]
    a, dh, du = (saved_ref[:, i * hidden : (i + 1) * hidden] for i in range(3))
    x = x_ref[...]
    out_ref[0, 0] = contract(x, dh, 0, 0).astype(BF)
    out_ref[0, 1] = contract(x, du, 0, 0).astype(BF)
    out_ref[0, 2] = contract(g_ref[...], a, 0, 0).astype(BF)


def merge(
    slots, ids_ref, cap_ref, comb_ref, cot_ref, o_ref, d_ref, mixed_ref, rows_ref, gc_ref, high_ref, low_ref, pick_ref, dots_ref
):
    i = pl.program_id(0)

    @pl.when(i == 0)
    def _():
        held, chosen = hits(ids_ref, cap_ref, slots)
        share = shares(held, chosen, comb_ref, slots)
        high = share.astype(BF)
        pick_ref[...] = held.astype(BF)
        high_ref[...] = high
        low_ref[...] = (share - high.astype(F32)).astype(BF)
        dots_ref[...] = jnp.zeros(dots_ref.shape, F32)

    o = o_ref[...]
    mixed_ref[...] = (contract(high_ref[...], o, 0, 0) + contract(low_ref[...], o, 0, 0)).astype(BF)
    rows_ref[...] = contract(pick_ref[...], d_ref[...], 0, 0).astype(BF)
    dots_ref[...] += contract(o, cot_ref[...], 1, 1)

    @pl.when(i == pl.num_programs(0) - 1)
    def _():
        top, count = ids_ref.shape
        experts = cap_ref.shape[1]
        found = dots_ref[...] * pick_ref[...].astype(F32)
        per_expert = jnp.sum(found.reshape(experts, slots, count), axis=1)
        numbers = lax.broadcasted_iota(jnp.int32, (experts, count), 0)
        for k in range(top):
            hit = ids_ref[k : k + 1, :] == numbers
            gc_ref[k : k + 1, :] = jnp.sum(jnp.where(hit, per_expert, 0.0), axis=0, keepdims=True)


def on_device(tokens, cotangent, expert_ids, combine, capacity, w_gate, w_up, w_down):
    part = functools.partial
    of = jax.ShapeDtypeStruct
    peers = lax.axis_size("expert")
    count, width = tokens.shape
    top = expert_ids.shape[1]
    experts = capacity.shape[0]
    slots = count * top // (2 * peers)
    rows = experts * slots
    hidden = w_gate.shape[2]
    limits = capacity.reshape(1, experts)
    ids, comb = expert_ids.T, combine.T
    unit = 2 * rows * width * hidden
    pick_flops = 2 * rows * count * width

    def cost(flops, moved):
        return pl.CostEstimate(flops=flops, bytes_accessed=moved, transcendentals=0)

    def room(mib):
        return pltpu.CompilerParams(vmem_limit_bytes=mib * MIB)

    def fixed(shape):
        return pl.BlockSpec(shape, lambda i: (0,) * len(shape))

    def exchange(x):
        x = x.reshape(peers, slots, 2 * width)
        return lax.all_to_all(x, "expert", 0, 0, tiled=True).reshape(rows, 2 * width)

    block = width // 2
    sent = pl.pallas_call(
        part(pick_rows, slots),
        grid=(4,),
        in_specs=[
            fixed((top, count)), fixed((1, experts)), fixed((top, count)),
            pl.BlockSpec((count, block), lambda i: (0, jnp.minimum(i, 1))),
            pl.BlockSpec((count, block), lambda i: (0, jnp.maximum(i - 2, 0))),
        ],
        out_specs=pl.BlockSpec((rows, block), lambda i: (0, i)),
        out_shape=of((rows, 2 * width), BF),
        scratch_shapes=[pltpu.VMEM((rows, count), BF), pltpu.VMEM((rows, 128), F32)],
        name="pick_rows", compiler_params=room(60), cost_estimate=cost(2 * pick_flops, 5 * rows * width),
    )(ids, limits, comb, tokens, cotangent)
    xg = exchange(sent)

    parts = lax.axis_size("dp")
    deep = width // parts
    stacked = pl.pallas_call(
        stack_weights, out_shape=of((3, deep, hidden), BF), name="stack_weights", compiler_params=room(16),
        cost_estimate=cost(0, 12 * deep * hidden),
    )(w_gate[0], w_up[0], w_down[0])
    weights = lax.all_gather(stacked, "dp", axis=0, tiled=False)

    whole = pl.BlockSpec(memory_space=pl.ANY)
    od, saved = pl.pallas_call(
        expert_math,
        in_specs=[whole, whole],
        out_specs=[whole, pl.BlockSpec(memory_space=pltpu.VMEM)],
        out_shape=[of((rows, 2 * width), BF), of((rows, 3 * hidden), BF)],
        scratch_shapes=[
            pltpu.VMEM((rows, 2 * width), BF), pltpu.VMEM(weights.shape, BF), pltpu.VMEM((rows, 2 * width), BF),
            pltpu.SemaphoreType.DMA((2 * parts,)), pltpu.SemaphoreType.DMA((2 * parts,)), pltpu.SemaphoreType.DMA((2 * parts,)),
        ],
        name="expert_math", compiler_params=room(60), cost_estimate=cost(6 * unit, 10 * rows * width),
    )(xg, weights)
    back = exchange(od)

    partial_grads = pl.pallas_call(
        weight_grads,
        grid=(parts,),
        in_specs=[
            pl.BlockSpec((rows, deep), lambda d: (0, d)),
            pl.BlockSpec((rows, deep), lambda d: (0, d + width // deep)),
            fixed((rows, 3 * hidden)),
        ],
        out_specs=pl.BlockSpec((1, 3, deep, hidden), lambda d: (d, 0, 0, 0)),
        out_shape=of((parts, 3, deep, hidden), BF),
        name="weight_grads", compiler_params=room(60), cost_estimate=cost(3 * unit, 6 * rows * width),
    )(xg, xg, saved)
    summed = lax.psum_scatter(partial_grads, "dp", scatter_dimension=0, tiled=False)
    grad_gate, grad_up, grad_down = pl.pallas_call(
        unstack_weights, out_shape=[of((deep, hidden), BF), of((deep, hidden), BF), of((hidden, deep), BF)],
        name="unstack_weights", compiler_params=room(16), cost_estimate=cost(0, 12 * deep * hidden),
    )(summed)
    back, grad_gate, grad_up, grad_down = together(back, grad_gate, grad_up, grad_down)

    mixed, grad_tokens, grad_combine = pl.pallas_call(
        part(merge, slots),
        grid=(width // STEP,),
        in_specs=[
            fixed((top, count)), fixed((1, experts)), fixed((top, count)),
            pl.BlockSpec((count, STEP), lambda i: (0, i)),
            pl.BlockSpec((rows, STEP), lambda i: (0, i)),
            pl.BlockSpec((rows, STEP), lambda i: (0, i + width // STEP)),
        ],
        out_specs=[
            pl.BlockSpec((count, STEP), lambda i: (0, i)), pl.BlockSpec((count, STEP), lambda i: (0, i)), fixed((top, count)),
        ],
        out_shape=[of((count, width), BF), of((count, width), BF), of((top, count), F32)],
        scratch_shapes=[pltpu.VMEM((rows, count), BF)] * 3 + [pltpu.VMEM((rows, count), F32)],
        name="merge", compiler_params=room(60), cost_estimate=cost(4 * pick_flops, 5 * rows * width),
    )(ids, limits, comb, cotangent, back, back)
    return (mixed, grad_tokens, grad_combine.T, grad_gate[None], grad_up[None], grad_down[None])


def solution(mesh):
    rows = P(("dp", "expert"), None)
    deep, wide = P("expert", "dp", None), P("expert", None, "dp")
    return jax.shard_map(
        on_device,
        mesh=mesh,
        in_specs=(rows, rows, rows, rows, P(), deep, deep, wide),
        out_specs=(rows, rows, rows, deep, deep, wide),
        check_vma=False,
    )
```

time: 326 us -> 255 us (0.78)
  local copies, waits for them, and re-layouts: 46.9 us -> 1.28 us
  other arithmetic: 32.7 us -> 0 us
  matrix products: 32.2 us -> 0 us
  Pallas kernels: 0 us -> 32.2 us
  waiting for transfers between devices: 169 us -> 189 us
  starting transfers between devices: 29 us -> 18.3 us
    all_to_all x4 -> x2, waiting for transfers between devices: 141 us -> 89.4 us  [exchange(): lax.all_to_all(x, 'expert', 0, 0, tiled=True).reshape(rows, 2 * width)]
    reduce_scatter x3 -> x1, waiting for transfers between devices: 0.01 us -> 42.6 us  [on_device(): lax.psum_scatter(partial_grads, 'dp', scatter_dimension=0, tiled=False)]
    dot_general x9 -> x0, matrix products: 32.2 us -> none  [the longest x1 4.2 us: backward_part(): d_active = jnp.dot(grads, wdown.T, preferred_element_type=jnp.float32)]
    pallas_call x0 -> x6, Pallas kernels: none -> 32.2 us  [the longest x1 11.8 us: on_device(): pl.pallas_call(expert_math, in_specs=[whole, whole], out_specs=[whole, pl...]
    all_gather x3 -> x1, waiting for transfers between devices: 26.3 us -> 56.7 us  [on_device(): weights = lax.all_gather(stacked, 'dp', axis=0, tiled=False)]
    gather x4 -> x0, local copies, waits for them, and re-layouts: 28.1 us -> none  [the longest x1 10.7 us: on_device(): padded_output[position].reshape(tok_count, top_count, width)]
    another operation x3 -> x0, other arithmetic: 18.2 us -> none
    reduce_sum x3 -> x0, other arithmetic: 11.7 us -> none  [the longest x1 5.88 us: on_device(): grad_tokens = jnp.sum(picked_rows, axis=1).astype(jnp.bfloat16)]
  transfers between devices with their start and end apart: 10 -> 4, of which waited for: 5 -> 4; matrix products, arithmetic and copies ran while one was open for 22% -> 0% of each run, Pallas kernels for 0% -> 1%
where the time goes in v3:
time: 255 us
  waiting for transfers between devices  189 us (74%)
  Pallas kernels  32.2 us (13%)
  starting transfers between devices  18.3 us (7%)
  between operations  14.1 us (6%)
    all_to_all x2, waiting for transfers between devices, exchange(): lax.all_to_all(x, 'expert', 0, 0, tiled=True).reshape(rows, 2 * width)  89.4 us
    all_gather x1, waiting for transfers between devices, on_device(): weights = lax.all_gather(stacked, 'dp', axis=0, tiled=False)  56.7 us
    reduce_scatter x1, waiting for transfers between devices, on_device(): lax.psum_scatter(partial_grads, 'dp', scatter_dimension=0, tiled=False)  42.6 us
    all_to_all x2, starting transfers between devices, exchange(): lax.all_to_all(x, 'expert', 0, 0, tiled=True).reshape(rows, 2 * width)  18.2 us
    pallas_call x1, Pallas kernels, on_device(): pl.pallas_call(expert_math, in_specs=[whole, whole], out_specs=[whole, pl...  11.8 us
    pallas_call x1, Pallas kernels, on_device(): pl.pallas_call(weight_grads, grid=(parts,), in_specs=[pl.BlockSpec((rows,...  7.46 us
    pallas_call x1, Pallas kernels, on_device(): pl.pallas_call(part(merge, slots), grid=(width // STEP,), in_specs=[fixed...  5.46 us
    pallas_call x1, Pallas kernels, on_device(): pl.pallas_call(part(pick_rows, slots), grid=(4,), in_specs=[fixed((top, c...  5.16 us
  transfers between devices with their start and end apart: 4, of which 4 were waited for; matrix products, arithmetic and copies ran while one was open for 0% of the time, Pallas kernels for 1%

profile of v3, /device:TPU:4, one launch (start us, length us, event | category | flops | bytes accessed | tf_op | source)
XLA Modules:
  0.0 254.6 jit_solution(3916189054511344164)
XLA Ops:
  7.2 5.2 %pick_rows.1 = bf16[512,4096]{1,0:T(8,128)(2,1)} custom-call(s32[8,128]{1,0:T(8,128)} %bitcast.22, s32[1,64]{1,0:T(1,128)} %bitcast.26, f32[8,128]{1,0:T(8,128)} %bitcast.24, bf16[128,2048]{1,0:T(8,128)(2,1)} %tokens_ref.1, bf16[128,2048]{1,0:T(8,128)(2,1)} %cot_ref.3), custom_call_target="tpu_custom_call" | custom-call | flops 536870912 | bytes 5242880 | tf_op jit(solution)/shard_map/pick_rows/pallas_call | solution.py:218
  12.3 0.0 copy-start.1
  12.3 0.0 copy-start.2
  12.3 0.0 copy-start.3
  12.3 12.5 %all-to-all-start = ((bf16[64,8,4096]{2,1,0:T(8,128)(2,1)}), bf16[64,8,4096]{2,1,0:T(8,128)(2,1)}, u32[]{:S(2)}, u32[]{:S(2)}) async-start(bf16[64,8,4096]{2,1,0:T(8,128)(2,1)} %bitcast.20), calls=%async_computation | async-start | bytes 8388608 | tf_op jit(solution)/shard_map/all_to_all | solution.py:215
  24.9 0.0 all-gather.3.cloned.1.call-start
  24.9 0.0 copy-done.1
  24.9 0.0 copy-done.2
  24.9 0.0 copy-done.3
  24.9 1.2 stack_weights.1
  26.1 0.0 all-gather.3.cloned.1.call-update
  26.2 0.0 reduce-scatter.2.cloned.1.call-start
  26.2 56.7 %all-gather.3.cloned.1.call-done = bf16[12,512,384]{2,1,0:T(8,128)(2,1)} async-done(((bf16[3,512,384]{2,1,0:T(8,128)(2,1)}), bf16[12,512,384]{2,1,0:T(8,128)(2,1)}) %all-gather.3.cloned.1.call-update) | async-done | bytes 4718608 | tf_op jit(solution)/shard_map/all_gather | solution.py:239
  82.9 38.2 %all-to-all-done = bf16[64,8,4096]{2,1,0:T(8,128)(2,1)} async-done(((bf16[64,8,4096]{2,1,0:T(8,128)(2,1)}), bf16[64,8,4096]{2,1,0:T(8,128)(2,1)}, u32[]{:S(2)}, u32[]{:S(2)}) %all-to-all-start) | async-done | bytes 4194336 | tf_op jit(solution)/shard_map/all_to_all | solution.py:215
  121.1 11.8 %expert_math.1 = (bf16[512,4096]{1,0:T(8,128)(2,1)}, bf16[512,1152]{1,0:T(8,128)(2,1)}) custom-call(bf16[512,4096]{1,0:T(8,128)(2,1)} %bitcast.4.xg_hbm.x_ref.g_ref, bf16[4,3,512,384]{3,2,1,0:T(8,128)(2,1)} %bitcast.28), custom_call_target="tpu_custom_call" | custom-call | flops 4831838208 | bytes 10485760 | tf_op jit(solution)/shard_map/expert_math/pallas_call | solution.py:242
  132.9 7.5 %weight_grads.1 = bf16[4,3,512,384]{3,2,1,0:T(8,128)(2,1)} custom-call(bf16[512,4096]{1,0:T(8,128)(2,1)} %bitcast.4.xg_hbm.x_ref.g_ref, bf16[512,4096]{1,0:T(8,128)(2,1)} %bitcast.4.xg_hbm.x_ref.g_ref, bf16[512,1152]{1,0:T(8,128)(2,1)} %get-tuple-element.19.saved_ref), custom_call_target="tpu_custom_call" | custom-call | flops 2415919104 | bytes 6291456 | tf_op jit(solution)/shard_map/weight_grads/pallas_call | solution.py:255
  140.4 0.0 reduce-scatter.2.cloned.1.call-update
  140.4 5.7 %all-to-all-start.1 = ((bf16[64,8,4096]{2,1,0:T(8,128)(2,1)}), bf16[64,8,4096]{2,1,0:T(8,128)(2,1)}, u32[]{:S(2)}, u32[]{:S(2)}) async-start(bf16[64,8,4096]{2,1,0:T(8,128)(2,1)} %bitcast.21), calls=%async_computation.1 | async-start | bytes 8388608 | tf_op jit(solution)/shard_map/all_to_all | solution.py:215
  146.1 42.6 %reduce-scatter.2.cloned.1.call-done = bf16[1,3,512,384]{3,2,1,0:T(8,128)(2,1)} async-done(((bf16[4,3,512,384]{3,2,1,0:T(8,128)(2,1)}), bf16[1,3,512,384]{3,2,1,0:T(8,128)(2,1)}) %reduce-scatter.2.cloned.1.call-update) | async-done | bytes 1179664 | tf_op jit(solution)/shard_map/reduce_scatter | solution.py:267
  188.7 0.0 copy-start
  188.7 1.3 copy-done
  190.0 1.1 unstack_weights.1
  191.1 51.2 %all-to-all-done.1 = bf16[64,8,4096]{2,1,0:T(8,128)(2,1)} async-done(((bf16[64,8,4096]{2,1,0:T(8,128)(2,1)}), bf16[64,8,4096]{2,1,0:T(8,128)(2,1)}, u32[]{:S(2)}, u32[]{:S(2)}) %all-to-all-start.1) | async-done | bytes 4194336 | tf_op jit(solution)/shard_map/all_to_all | solution.py:215
  242.3 5.5 %merge.1 = (bf16[128,2048]{1,0:T(8,128)(2,1)}, bf16[128,2048]{1,0:T(8,128)(2,1)}, f32[8,128]{1,0:T(8,128)}) custom-call(s32[8,128]{1,0:T(8,128)} %bitcast.23, s32[1,64]{1,0:T(1,128)} %bitcast.27, f32[8,128]{1,0:T(8,128)} %bitcast.25, bf16[128,2048]{1,0:T(8,128)(2,1)} %cot_ref.3, bf16[512,4096]{1,0:T(8,128)(2,1)} %bitcast.10.o_ref.d_ref, ...), custom_call_target="tpu_custom_call" | custom-call | flops 1073741824 | bytes 5242880 | tf_op jit(solution)/shard_map/merge/pallas_call | solution.py:274
Async XLA Ops:
  12.3 12.6 %copy-start.1 = (bf16[1,512,384]{2,1,0:T(8,128)(2,1)S(1)}, bf16[1,512,384]{2,1,0:T(8,128)(2,1)}, u32[]{:S(2)}) copy-start(bf16[1,512,384]{2,1,0:T(8,128)(2,1)} %param.13) | copy-start | bytes 1179652
  12.3 12.6 %copy-start.2 = (bf16[1,512,384]{2,1,0:T(8,128)(2,1)S(1)}, bf16[1,512,384]{2,1,0:T(8,128)(2,1)}, u32[]{:S(2)}) copy-start(bf16[1,512,384]{2,1,0:T(8,128)(2,1)} %param.14) | copy-start | bytes 1179652
  12.3 12.6 %copy-start.3 = (bf16[1,384,512]{2,1,0:T(8,128)(2,1)S(1)}, bf16[1,384,512]{2,1,0:T(8,128)(2,1)}, u32[]{:S(2)}) copy-start(bf16[1,384,512]{2,1,0:T(8,128)(2,1)} %param.15) | copy-start | bytes 1179652
  12.3 108.7 %all-to-all-start = ((bf16[64,8,4096]{2,1,0:T(8,128)(2,1)}), bf16[64,8,4096]{2,1,0:T(8,128)(2,1)}, u32[]{:S(2)}, u32[]{:S(2)}) async-start(bf16[64,8,4096]{2,1,0:T(8,128)(2,1)} %bitcast.20), calls=%async_computation | async-start | bytes 8388608 | tf_op jit(solution)/shard_map/all_to_all | solution.py:215
  24.9 58.0 %all-gather.3.cloned.1.call-start = ((), (), s32[]{:S(2)}) async-start(), calls=%async_computation.4 | async-start | bytes 5898240 | tf_op jit(solution)/shard_map/all_gather | solution.py:239
  26.2 162.6 %reduce-scatter.2.cloned.1.call-start = ((), (), s32[]{:S(2)}) async-start(), calls=%async_computation.3 | async-start | bytes 5898240 | tf_op jit(solution)/shard_map/reduce_scatter | solution.py:267
  140.4 101.9 %all-to-all-start.1 = ((bf16[64,8,4096]{2,1,0:T(8,128)(2,1)}), bf16[64,8,4096]{2,1,0:T(8,128)(2,1)}, u32[]{:S(2)}, u32[]{:S(2)}) async-start(bf16[64,8,4096]{2,1,0:T(8,128)(2,1)} %bitcast.21), calls=%async_computation.1 | async-start | bytes 8388608 | tf_op jit(solution)/shard_map/all_to_all | solution.py:215
  188.7 1.3 copy-start
Sparse Core Ops, SparseCore 0:
  27.5 55.3 all-gather.2
  140.5 48.1 reduce-scatter.1

commit v4 on v3

v4 whole, which is shorter than its diff:
```python
import functools

import jax
import jax.numpy as jnp
from jax import lax
from jax.experimental import pallas as pl
from jax.experimental.pallas import tpu as pltpu
from jax.sharding import PartitionSpec as P

MIB = 2**20
BF = jnp.bfloat16
F32 = jnp.float32
STEP = 512


def contract(left, right, left_dim, right_dim):
    return lax.dot_general(
        left, right, (((left_dim,), (right_dim,)), ((), ())), preferred_element_type=F32
    )


def together(*arrays):
    return lax.optimization_barrier(arrays)


def hits(ids_ref, cap_ref, slots):
    top, count = ids_ref.shape
    experts = cap_ref.shape[1]
    numbers = lax.broadcasted_iota(jnp.int32, (experts, count), 0)
    chosen = [ids_ref[k : k + 1, :] == numbers for k in range(top)]
    taken = sum(c.astype(F32) for c in chosen)
    earlier = (
        lax.broadcasted_iota(jnp.int32, (count, count), 0)
        < lax.broadcasted_iota(jnp.int32, (count, count), 1)
    ).astype(BF)
    rank = contract(taken.astype(BF), earlier, 1, 0)
    same = lax.broadcasted_iota(jnp.int32, (experts, experts), 0) == lax.broadcasted_iota(
        jnp.int32, (experts, experts), 1
    )
    limit = jnp.sum(jnp.where(same, cap_ref[...].astype(F32), 0.0), axis=1, keepdims=True)
    slot_of = jnp.where((taken > 0.5) & (rank < limit), rank, -1.0)
    wanted = lax.broadcasted_iota(jnp.int32, (experts, slots, count), 1).astype(F32)
    held = (jnp.broadcast_to(slot_of[:, None, :], (experts, slots, count)) == wanted).astype(F32)
    return held.reshape(experts * slots, count), chosen


def shares(held, chosen, comb_ref, slots):
    weights = sum(jnp.where(c, comb_ref[k : k + 1, :], 0.0) for k, c in enumerate(chosen))
    experts, count = weights.shape
    spread = jnp.broadcast_to(weights[:, None, :], (experts, slots, count)).reshape(experts * slots, count)
    return held * spread


def pick_rows(slots, ids_ref, cap_ref, comb_ref, tokens_ref, cot_ref, out_ref, pick_ref, high_ref, low_ref, scale_ref):
    i = pl.program_id(0)
    steps = pl.num_programs(0)

    @pl.when(i == 0)
    def _():
        held, chosen = hits(ids_ref, cap_ref, slots)
        pick_ref[...] = held.astype(BF)
        share = shares(held, chosen, comb_ref, slots)
        high_ref[...] = share.astype(BF)
        low_ref[...] = (share - share.astype(BF).astype(F32)).astype(BF)
        scale = jnp.sum(share, axis=1, keepdims=True)
        scale_ref[...] = jnp.broadcast_to(scale, scale_ref.shape)

    wide = out_ref.shape[1]

    @pl.when(i < steps // 2)
    def _():
        for c in range(0, wide, STEP):
            out_ref[:, c : c + STEP] = contract(pick_ref[...], tokens_ref[:, c : c + STEP], 1, 0).astype(BF)

    @pl.when(i >= steps // 2)
    def _():
        scale = scale_ref[:, :1]
        for c in range(0, wide, STEP):
            rows = contract(pick_ref[...], cot_ref[:, c : c + STEP], 1, 0)
            out_ref[:, c : c + STEP] = (scale * rows).astype(BF)


def lay_weights(gate_ref, up_ref, down_ref, out_ref):
    hidden = gate_ref.shape[1]
    out_ref[:, :hidden] = gate_ref[...]
    out_ref[:, hidden : 2 * hidden] = up_ref[...]
    out_ref[:, 2 * hidden :] = down_ref[...].T


def expert_math(
    me_ref, xg_hbm, own_hbm, next_hbm, far_low_hbm, far_high_hbm, prev_hbm, od_hbm, saved_ref, xg_ref, w_ref, od_ref, in_sems, w_sems, out_sems
):
    parts, deep, hidden = w_ref.shape
    hidden //= 3
    half = deep // 2
    order = (0, 1, 3, 2)

    def lanes(n):
        block = lax.rem(me_ref[0] + n % parts, parts) + n // parts * parts
        return pl.ds(pl.multiple_of(block * deep, deep), deep)

    def arrive(n):
        return pltpu.make_async_copy(xg_hbm.at[:, lanes(n)], xg_ref.at[:, pl.ds(n * deep, deep)], in_sems.at[n])

    def leave(n):
        return pltpu.make_async_copy(od_ref.at[:, pl.ds(n * deep, deep)], od_hbm.at[:, lanes(n)], out_sems.at[n])

    def weights(n):
        if n != 2:
            source = {0: own_hbm, 1: next_hbm, 3: prev_hbm}[n]
            return [pltpu.make_async_copy(source, w_ref.at[n], w_sems.at[n])]
        return [
            pltpu.make_async_copy(far_low_hbm, w_ref.at[n, pl.ds(0, half)], w_sems.at[n]),
            pltpu.make_async_copy(far_high_hbm, w_ref.at[n, pl.ds(half, half)], w_sems.at[parts]),
        ]

    for n in order:
        for copy in weights(n):
            copy.start()
        arrive(n).start()
    for n in order:
        arrive(parts + n).start()
    hu = da = 0.0
    for n in order:
        for copy in weights(n):
            copy.wait()
        arrive(n).wait()
        hu = hu + contract(xg_ref[:, n * deep : (n + 1) * deep], w_ref[n, :, : 2 * hidden], 1, 0)
    h, u = hu[:, :hidden], hu[:, hidden:]
    s = jax.nn.sigmoid(h)
    a = (h * s * u).astype(BF)
    saved_ref[:, 2 * hidden :] = a
    for n in order:
        od_ref[:, n * deep : (n + 1) * deep] = contract(a, w_ref[n, :, 2 * hidden :], 1, 1).astype(BF)
        leave(n).start()
    for n in order:
        arrive(parts + n).wait()
        g = xg_ref[:, (parts + n) * deep : (parts + n + 1) * deep]
        da = da + contract(g, w_ref[n, :, 2 * hidden :], 1, 0)
    dh = (da * u * s * (1.0 + h * (1.0 - s))).astype(BF)
    du = (da * h * s).astype(BF)
    saved_ref[:, :hidden] = dh
    saved_ref[:, hidden : 2 * hidden] = du
    both = jnp.concatenate([dh, du], axis=1)
    for n in order:
        m = parts + n
        od_ref[:, m * deep : (m + 1) * deep] = contract(both, w_ref[n, :, : 2 * hidden], 1, 1).astype(BF)
        leave(m).start()
    for n in range(2 * parts):
        leave(n).wait()


def weight_grads(me_ref, x_ref, g_ref, saved_ref, out_ref):
    hidden = out_ref.shape[2] // 3
    out_ref[0, :, : 2 * hidden] = contract(x_ref[...], saved_ref[:, : 2 * hidden], 0, 0).astype(BF)
    out_ref[0, :, 2 * hidden :] = contract(g_ref[...], saved_ref[:, 2 * hidden :], 0, 0).astype(BF)


def add_far(next_ref, prev_ref, low_ref, high_ref, right_ref, left_ref):
    half = low_ref.shape[0]
    right_ref[:half, :] = (next_ref[0, :half, :].astype(F32) + low_ref[...].astype(F32)).astype(BF)
    right_ref[half:, :] = next_ref[0, half:, :]
    left_ref[:half, :] = prev_ref[0, :half, :]
    left_ref[half:, :] = (prev_ref[0, half:, :].astype(F32) + high_ref[...].astype(F32)).astype(BF)


def add_last(own_ref, below_ref, above_ref, gate_ref, up_ref, down_ref):
    hidden = gate_ref.shape[1]
    total = own_ref[0].astype(F32) + below_ref[...].astype(F32) + above_ref[...].astype(F32)
    gate_ref[...] = total[:, :hidden].astype(BF)
    up_ref[...] = total[:, hidden : 2 * hidden].astype(BF)
    down_ref[...] = total[:, 2 * hidden :].astype(BF).T


def merge(
    slots, experts, ids_ref, pick_ref, high_ref, low_ref, cot_ref, o_ref, d_ref, mixed_ref, rows_ref, gc_ref, dots_ref
):
    i = pl.program_id(0)

    @pl.when(i == 0)
    def _():
        dots_ref[...] = jnp.zeros(dots_ref.shape, F32)

    o = o_ref[...]
    mixed_ref[...] = (contract(high_ref[...], o, 0, 0) + contract(low_ref[...], o, 0, 0)).astype(BF)
    rows_ref[...] = contract(pick_ref[...], d_ref[...], 0, 0).astype(BF)
    dots_ref[...] += contract(o, cot_ref[...], 1, 1)

    @pl.when(i == pl.num_programs(0) - 1)
    def _():
        top, count = ids_ref.shape
        found = dots_ref[...] * pick_ref[...].astype(F32)
        per_expert = jnp.sum(found.reshape(experts, slots, count), axis=1)
        numbers = lax.broadcasted_iota(jnp.int32, (experts, count), 0)
        for k in range(top):
            hit = ids_ref[k : k + 1, :] == numbers
            gc_ref[k : k + 1, :] = jnp.sum(jnp.where(hit, per_expert, 0.0), axis=0, keepdims=True)


def on_device(tokens, cotangent, expert_ids, combine, capacity, w_gate, w_up, w_down):
    part = functools.partial
    of = jax.ShapeDtypeStruct
    peers = lax.axis_size("expert")
    count, width = tokens.shape
    top = expert_ids.shape[1]
    experts = capacity.shape[0]
    slots = count * top // (2 * peers)
    rows = experts * slots
    hidden = w_gate.shape[2]
    limits = capacity.reshape(1, experts)
    ids, comb = expert_ids.T, combine.T
    unit = 2 * rows * width * hidden
    pick_flops = 2 * rows * count * width

    def cost(flops, moved):
        return pl.CostEstimate(flops=flops, bytes_accessed=moved, transcendentals=0)

    def room(mib):
        return pltpu.CompilerParams(vmem_limit_bytes=mib * MIB)

    def fixed(shape):
        return pl.BlockSpec(shape, lambda i: (0,) * len(shape))

    def exchange(x):
        x = x.reshape(peers, slots, 2 * width)
        return lax.all_to_all(x, "expert", 0, 0, tiled=True).reshape(rows, 2 * width)

    block = width // 2
    sent, *tables = pl.pallas_call(
        part(pick_rows, slots),
        grid=(4,),
        in_specs=[
            fixed((top, count)), fixed((1, experts)), fixed((top, count)),
            pl.BlockSpec((count, block), lambda i: (0, jnp.minimum(i, 1))),
            pl.BlockSpec((count, block), lambda i: (0, jnp.maximum(i - 2, 0))),
        ],
        out_specs=[pl.BlockSpec((rows, block), lambda i: (0, i))] + [fixed((rows, count))] * 3,
        out_shape=[of((rows, 2 * width), BF)] + [of((rows, count), BF)] * 3,
        scratch_shapes=[pltpu.VMEM((rows, 128), F32)],
        name="pick_rows", compiler_params=room(60), cost_estimate=cost(2 * pick_flops, 5 * rows * width),
    )(ids, limits, comb, tokens, cotangent)
    xg = exchange(sent)

    parts = lax.axis_size("dp")
    deep = width // parts
    half = deep // 2
    me = lax.axis_index("dp").astype(jnp.int32).reshape(1)

    def up(x):
        return lax.ppermute(x, "dp", [(i, (i + 1) % parts) for i in range(parts)])

    def down(x):
        return lax.ppermute(x, "dp", [(i, (i - 1) % parts) for i in range(parts)])

    own = pl.pallas_call(
        lay_weights, out_shape=of((deep, 3 * hidden), BF), name="lay_weights", compiler_params=room(60),
        cost_estimate=cost(0, 12 * deep * hidden),
    )(w_gate[0], w_up[0], w_down[0])
    before, after = up(own), down(own)
    far_low, far_high = up(before[:half]), down(after[half:])

    whole = pl.BlockSpec(memory_space=pl.ANY)
    vmem = pl.BlockSpec(memory_space=pltpu.VMEM)
    od, saved = pl.pallas_call(
        expert_math,
        in_specs=[pl.BlockSpec(memory_space=pltpu.SMEM)] + [whole] * 6,
        out_specs=[whole, vmem],
        out_shape=[of((rows, 2 * width), BF), of((rows, 3 * hidden), BF)],
        scratch_shapes=[
            pltpu.VMEM((rows, 2 * width), BF), pltpu.VMEM((parts, deep, 3 * hidden), BF), pltpu.VMEM((rows, 2 * width), BF),
            pltpu.SemaphoreType.DMA((2 * parts,)), pltpu.SemaphoreType.DMA((parts + 1,)), pltpu.SemaphoreType.DMA((2 * parts,)),
        ],
        name="expert_math", compiler_params=room(60), cost_estimate=cost(6 * unit, 10 * rows * width),
    )(me, xg, own, after, far_low, far_high, before)
    back = exchange(od)

    grads = pl.pallas_call(
        weight_grads,
        grid_spec=pltpu.PrefetchScalarGridSpec(
            num_scalar_prefetch=1,
            grid=(parts,),
            in_specs=[
                pl.BlockSpec((rows, deep), lambda i, me: (0, lax.rem(me[0] + i, parts))),
                pl.BlockSpec((rows, deep), lambda i, me: (0, lax.rem(me[0] + i, parts) + parts)),
                pl.BlockSpec((rows, 3 * hidden), lambda i, me: (0, 0)),
            ],
            out_specs=pl.BlockSpec((1, deep, 3 * hidden), lambda i, me: (i, 0, 0)),
        ),
        out_shape=of((parts, deep, 3 * hidden), BF),
        name="weight_grads", compiler_params=room(60), cost_estimate=cost(3 * unit, 6 * rows * width),
    )(me, xg, xg, saved)
    low, high = up(grads[2, :half]), down(grads[2, half:])

    def block(n):
        return pl.BlockSpec((1, deep, 3 * hidden), lambda i: (n, 0, 0))

    flat = fixed((deep, 3 * hidden))
    right, left = pl.pallas_call(
        add_far,
        grid=(1,),
        in_specs=[block(1), block(3), fixed((half, 3 * hidden)), fixed((half, 3 * hidden))],
        out_specs=[flat, flat],
        out_shape=[of((deep, 3 * hidden), BF)] * 2,
        name="add_far", compiler_params=room(60), cost_estimate=cost(0, 30 * deep * hidden),
    )(grads, grads, low, high)
    grad_gate, grad_up, grad_down = pl.pallas_call(
        add_last,
        grid=(1,),
        in_specs=[block(0), flat, flat],
        out_specs=[fixed((deep, hidden)), fixed((deep, hidden)), fixed((hidden, deep))],
        out_shape=[of((deep, hidden), BF), of((deep, hidden), BF), of((hidden, deep), BF)],
        name="add_last", compiler_params=room(60), cost_estimate=cost(0, 24 * deep * hidden),
    )(grads, up(right), down(left))
    back, grad_gate, grad_up, grad_down = together(back, grad_gate, grad_up, grad_down)

    mixed, grad_tokens, grad_combine = pl.pallas_call(
        part(merge, slots, experts),
        grid=(width // STEP,),
        in_specs=[
            fixed((top, count)), *[fixed((rows, count))] * 3,
            pl.BlockSpec((count, STEP), lambda i: (0, i)),
            pl.BlockSpec((rows, STEP), lambda i: (0, i)),
            pl.BlockSpec((rows, STEP), lambda i: (0, i + width // STEP)),
        ],
        out_specs=[
            pl.BlockSpec((count, STEP), lambda i: (0, i)), pl.BlockSpec((count, STEP), lambda i: (0, i)), fixed((top, count)),
        ],
        out_shape=[of((count, width), BF), of((count, width), BF), of((top, count), F32)],
        scratch_shapes=[pltpu.VMEM((rows, count), F32)],
        name="merge", compiler_params=room(60), cost_estimate=cost(4 * pick_flops, 5 * rows * width),
    )(ids, *tables, cotangent, back, back)
    return (mixed, grad_tokens, grad_combine.T, grad_gate[None], grad_up[None], grad_down[None])


def solution(mesh):
    rows = P(("dp", "expert"), None)
    deep, wide = P("expert", "dp", None), P("expert", None, "dp")
    return jax.shard_map(
        on_device,
        mesh=mesh,
        in_specs=(rows, rows, rows, rows, P(), deep, deep, wide),
        out_specs=(rows, rows, rows, deep, deep, wide),
        check_vma=False,
    )
```

time: 255 us -> 234 us (0.918)
  waiting for transfers between devices: 189 us -> 163 us
  between operations: 14.1 us -> 0.83 us
  starting transfers between devices: 18.3 us -> 26.9 us
  Pallas kernels: 32.2 us -> 39 us
    ppermute x0 -> x8, waiting for transfers between devices: none -> 79.4 us  [the longest x4 63.3 us: up(): return lax.ppermute(x, 'dp', [(i, (i + 1) % parts) for i in range(parts)])]
    all_gather x1 -> x0, waiting for transfers between devices: 56.7 us -> none  [on_device(): weights = lax.all_gather(stacked, 'dp', axis=0, tiled=False)]
    reduce_scatter x1 -> x0, waiting for transfers between devices: 42.6 us -> none  [on_device(): lax.psum_scatter(partial_grads, 'dp', scatter_dimension=0, tiled=False)]
    ppermute x0 -> x8, starting transfers between devices: none -> 8.7 us  [the longest x4 6.35 us: up(): return lax.ppermute(x, 'dp', [(i, (i + 1) % parts) for i in range(parts)])]
    pallas_call x5 -> x6, Pallas kernels: 27 us -> 33.7 us  [the longest x1 11.6 us: on_device(): pl.pallas_call(expert_math, in_specs=[pl.BlockSpec(memory_space=pltpu.SME...]
    all_to_all x2, waiting for transfers between devices: 89.4 us -> 83.7 us  [exchange(): lax.all_to_all(x, 'expert', 0, 0, tiled=True).reshape(rows, 2 * width)]
  transfers between devices with their start and end apart: 4 -> 10, of which waited for: 4 -> 9; matrix products, arithmetic and copies ran while one was open for 0% -> 1% of each run, Pallas kernels for 1% -> 7%
where the time goes in v4:
time: 234 us
  waiting for transfers between devices  163 us (70%)
  Pallas kernels  39 us (17%)
  starting transfers between devices  26.9 us (11%)
  local copies, waits for them, and re-layouts  3.83 us (2%)
    all_to_all x2, waiting for transfers between devices, exchange(): lax.all_to_all(x, 'expert', 0, 0, tiled=True).reshape(rows, 2 * width)  83.7 us
    ppermute x4, waiting for transfers between devices, up(): return lax.ppermute(x, 'dp', [(i, (i + 1) % parts) for i in range(parts)])  63.3 us
    all_to_all x2, starting transfers between devices, exchange(): lax.all_to_all(x, 'expert', 0, 0, tiled=True).reshape(rows, 2 * width)  18.2 us
    ppermute x4, waiting for transfers between devices, down(): return lax.ppermute(x, 'dp', [(i, (i - 1) % parts) for i in range(parts)])  16.1 us
    pallas_call x1, Pallas kernels, on_device(): pl.pallas_call(expert_math, in_specs=[pl.BlockSpec(memory_space=pltpu.SME...  11.6 us
    pallas_call x1, Pallas kernels, on_device(): pl.pallas_call(weight_grads, grid_spec=pltpu.PrefetchScalarGridSpec(num_s...  7.07 us
    ppermute x4, starting transfers between devices, up(): return lax.ppermute(x, 'dp', [(i, (i + 1) % parts) for i in range(parts)])  6.35 us
    pallas_call x1, Pallas kernels, on_device(): pl.pallas_call(part(merge, slots, experts), grid=(width // STEP,), in_spe...  5.52 us
  transfers between devices with their start and end apart: 10, of which 9 were waited for; matrix products, arithmetic and copies ran while one was open for 1% of the time, Pallas kernels for 7%

profile of v4, /device:TPU:4, one launch (start us, length us, event | category | flops | bytes accessed | tf_op | source)
XLA Modules:
  0.0 233.8 jit_solution(5231030509230178059)
XLA Ops:
  0.6 5.3 %pick_rows.1 = (bf16[512,4096]{1,0:T(8,128)(2,1)}, bf16[512,128]{1,0:T(8,128)(2,1)}, bf16[512,128]{1,0:T(8,128)(2,1)}, bf16[512,128]{1,0:T(8,128)(2,1)}) custom-call(s32[8,128]{1,0:T(8,128)} %bitcast.24, s32[1,64]{1,0:T(1,128)} %bitcast.31, f32[8,128]{1,0:T(8,128)} %bitcast.29, bf16[128,2048]{1,0:T(8,128)(2,1)} %tokens_ref.1, bf16[128,2048]{1,0:T(8,128)(2,1)} %cot_ref.3), custom_call_target="tpu_custom_call" | custom-call | flops 536870912 | bytes 5242880 | tf_op jit(solution)/shard_map/pick_rows/pallas_call | solution.py:229
  6.0 12.4 %all-to-all-start = ((bf16[64,8,4096]{2,1,0:T(8,128)(2,1)}), bf16[64,8,4096]{2,1,0:T(8,128)(2,1)}, u32[]{:S(2)}, u32[]{:S(2)}) async-start(bf16[64,8,4096]{2,1,0:T(8,128)(2,1)} %bitcast.20), calls=%async_computation | async-start | bytes 8388608 | tf_op jit(solution)/shard_map/all_to_all | solution.py:226
  18.3 2.4 %lay_weights.1.own_hbm = bf16[512,1152]{1,0:T(8,128)(2,1)} custom-call(bf16[512,384]{1,0:T(8,128)(2,1)} %bitcast.21, bf16[512,384]{1,0:T(8,128)(2,1)} %bitcast.22, bf16[384,512]{1,0:T(8,128)(2,1)} %bitcast.23), custom_call_target="tpu_custom_call" | custom-call | bytes 2359296 | tf_op jit(solution)/shard_map/lay_weights/pallas_call | solution.py:255
  20.8 1.2 collective-permute-start.1
  22.0 0.8 collective-permute-start
  22.8 26.0 %collective-permute-done.1.prev_hbm = bf16[512,1152]{1,0:T(8,128)(2,1)S(1)} collective-permute-done((bf16[512,1152]{1,0:T(8,128)(2,1)}, bf16[512,1152]{1,0:T(8,128)(2,1)S(1)}, u32[]{:S(2)}, u32[]{:S(2)}) %collective-permute-start.1) | collective-permute-done | bytes 1179680 | tf_op jit(solution)/shard_map/ppermute | solution.py:250
  48.8 0.0 copy-start.4
  48.9 1.3 collective-permute-start.2
  50.2 0.0 collective-permute-done.next_hbm
  50.2 0.0 copy-start.5
  50.2 0.0 copy-done.4
  50.2 0.9 collective-permute-start.3
  51.1 12.4 %collective-permute-done.2.far_low_hbm = bf16[256,1152]{1,0:T(8,128)(2,1)} collective-permute-done((bf16[256,1152]{1,0:T(8,128)(2,1)S(1)}, bf16[256,1152]{1,0:T(8,128)(2,1)}, u32[]{:S(2)}, u32[]{:S(2)}) %collective-permute-start.2) | collective-permute-done | bytes 589856 | tf_op jit(solution)/shard_map/ppermute | solution.py:250
  63.5 1.1 collective-permute-done.3.far_high_hbm
  64.6 50.0 %all-to-all-done = bf16[64,8,4096]{2,1,0:T(8,128)(2,1)} async-done(((bf16[64,8,4096]{2,1,0:T(8,128)(2,1)}), bf16[64,8,4096]{2,1,0:T(8,128)(2,1)}, u32[]{:S(2)}, u32[]{:S(2)}) %all-to-all-start) | async-done | bytes 4194336 | tf_op jit(solution)/shard_map/all_to_all | solution.py:226
  114.6 0.0 copy-done.5
  114.6 11.6 %expert_math.1 = (bf16[512,4096]{1,0:T(8,128)(2,1)}, bf16[512,1152]{1,0:T(8,128)(2,1)}) custom-call(s32[1]{0:T(128)} %bitcast.3.me_ref, bf16[512,4096]{1,0:T(8,128)(2,1)} %bitcast.5.xg_hbm.x_ref.g_ref, bf16[512,1152]{1,0:T(8,128)(2,1)} %lay_weights.1.own_hbm, bf16[512,1152]{1,0:T(8,128)(2,1)} %copy-done.5, ...), custom_call_target="tpu_custom_call" | custom-call | flops 4831838208 | bytes 10485760 | tf_op jit(solution)/shard_map/expert_math/pallas_call | solution.py:264
  126.2 5.8 %all-to-all-start.1 = ((bf16[64,8,4096]{2,1,0:T(8,128)(2,1)}), bf16[64,8,4096]{2,1,0:T(8,128)(2,1)}, u32[]{:S(2)}, u32[]{:S(2)}) async-start(bf16[64,8,4096]{2,1,0:T(8,128)(2,1)} %bitcast.19), calls=%async_computation.1 | async-start | bytes 8388608 | tf_op jit(solution)/shard_map/all_to_all | solution.py:226
  132.1 7.1 %weight_grads.1.next_ref.prev_ref.own_ref = bf16[4,512,1152]{2,1,0:T(8,128)(2,1)} custom-call(s32[1]{0:T(128)} %bitcast.3.me_ref, bf16[512,4096]{1,0:T(8,128)(2,1)} %bitcast.5.xg_hbm.x_ref.g_ref, bf16[512,4096]{1,0:T(8,128)(2,1)} %bitcast.5.xg_hbm.x_ref.g_ref, bf16[512,1152]{1,0:T(8,128)(2,1)} %get-tuple-element.29.saved_ref), custom_call_target="tpu_custom_call" | custom-call | flops 2415919104 | bytes 6291456 | tf_op jit(solution)/shard_map/weight_grads/pallas_call | solution.py:277
  139.1 1.3 slice_bitcast_fusion
  140.5 0.6 collective-permute-start.5
  141.1 1.5 collective-permute-start.4
  142.6 12.9 %collective-permute-done.5.high_ref = bf16[256,1152]{1,0:T(8,128)(2,1)S(1)} collective-permute-done((bf16[256,1152]{1,0:T(8,128)(2,1)S(1)}, bf16[256,1152]{1,0:T(8,128)(2,1)S(1)}, u32[]{:S(2)}, u32[]{:S(2)}) %collective-permute-start.5) | collective-permute-done | bytes 589856 | tf_op jit(solution)/shard_map/ppermute | solution.py:253
  155.5 0.0 copy-start.2
  155.5 0.2 collective-permute-done.4.low_ref
  155.7 0.6 copy-done.2
  156.3 0.0 copy-start.3
  156.3 0.8 copy-done.3
  157.1 3.6 %add_far.1 = (bf16[512,1152]{1,0:T(8,128)(2,1)}, bf16[512,1152]{1,0:T(8,128)(2,1)}) custom-call(bf16[4,512,1152]{2,1,0:T(8,128)(2,1)} %weight_grads.1.next_ref.prev_ref.own_ref, bf16[4,512,1152]{2,1,0:T(8,128)(2,1)} %weight_grads.1.next_ref.prev_ref.own_ref, bf16[256,1152]{1,0:T(8,128)(2,1)} %copy-done.3, bf16[256,1152]{1,0:T(8,128)(2,1)} %copy-done.2), custom_call_target="tpu_custom_call" | custom-call | bytes 5898240 | tf_op jit(solution)/shard_map/add_far/pallas_call | solution.py:298
  160.7 2.4 %collective-permute-start.6 = (bf16[512,1152]{1,0:T(8,128)(2,1)}, bf16[512,1152]{1,0:T(8,128)(2,1)S(1)}, u32[]{:S(2)}, u32[]{:S(2)}) collective-permute-start(bf16[512,1152]{1,0:T(8,128)(2,1)} %get-tuple-element.30), channel_id=1, source_target_pairs={{0,64},{64,128},{128,192},{192,0},{1,65},{65,129},{129,193},{193,1... | collective-permute-start | bytes 3538952 | tf_op jit(solution)/shard_map/ppermute | solution.py:250
  163.1 0.0 collective-permute-start.7
  163.1 24.6 %collective-permute-done.6.below_ref = bf16[512,1152]{1,0:T(8,128)(2,1)S(1)} collective-permute-done((bf16[512,1152]{1,0:T(8,128)(2,1)}, bf16[512,1152]{1,0:T(8,128)(2,1)S(1)}, u32[]{:S(2)}, u32[]{:S(2)}) %collective-permute-start.6) | collective-permute-done | bytes 1179680 | tf_op jit(solution)/shard_map/ppermute | solution.py:250
  187.7 0.0 copy-start
  187.7 2.2 collective-permute-done.7.above_ref
  189.9 0.0 copy-done
  189.9 0.0 copy-start.1
  189.9 1.0 copy-done.1
  190.9 3.4 %add_last.1 = (bf16[512,384]{1,0:T(8,128)(2,1)}, bf16[512,384]{1,0:T(8,128)(2,1)}, bf16[384,512]{1,0:T(8,128)(2,1)}) custom-call(bf16[4,512,1152]{2,1,0:T(8,128)(2,1)} %weight_grads.1.next_ref.prev_ref.own_ref, bf16[512,1152]{1,0:T(8,128)(2,1)} %copy-done, bf16[512,1152]{1,0:T(8,128)(2,1)} %copy-done.1), custom_call_target="tpu_custom_call" | custom-call | bytes 4718592 | tf_op jit(solution)/shard_map/add_last/pallas_call | solution.py:306
  194.3 33.8 %all-to-all-done.1 = bf16[64,8,4096]{2,1,0:T(8,128)(2,1)} async-done(((bf16[64,8,4096]{2,1,0:T(8,128)(2,1)}), bf16[64,8,4096]{2,1,0:T(8,128)(2,1)}, u32[]{:S(2)}, u32[]{:S(2)}) %all-to-all-start.1) | async-done | bytes 4194336 | tf_op jit(solution)/shard_map/all_to_all | solution.py:226
  228.1 5.5 %merge.1 = (bf16[128,2048]{1,0:T(8,128)(2,1)}, bf16[128,2048]{1,0:T(8,128)(2,1)}, f32[8,128]{1,0:T(8,128)}) custom-call(s32[8,128]{1,0:T(8,128)} %bitcast.25, bf16[512,128]{1,0:T(8,128)(2,1)} %get-tuple-element.24.pick_ref, bf16[512,128]{1,0:T(8,128)(2,1)} %get-tuple-element.25.high_ref, bf16[512,128]{1,0:T(8,128)(2,1)} %get-tuple-element.26.low_ref, ...), custom_call_target="tpu_custom_call" | custom-call | flops 1073741824 | bytes 5242880 | tf_op jit(solution)/shard_map/merge/pallas_call | solution.py:316
  (2 shorter events, 0.1 us)
Async XLA Ops:
  6.0 108.6 %all-to-all-start = ((bf16[64,8,4096]{2,1,0:T(8,128)(2,1)}), bf16[64,8,4096]{2,1,0:T(8,128)(2,1)}, u32[]{:S(2)}, u32[]{:S(2)}) async-start(bf16[64,8,4096]{2,1,0:T(8,128)(2,1)} %bitcast.20), calls=%async_computation | async-start | bytes 8388608 | tf_op jit(solution)/shard_map/all_to_all | solution.py:226
  20.8 28.1 %collective-permute-start.1 = (bf16[512,1152]{1,0:T(8,128)(2,1)}, bf16[512,1152]{1,0:T(8,128)(2,1)S(1)}, u32[]{:S(2)}, u32[]{:S(2)}) collective-permute-start(bf16[512,1152]{1,0:T(8,128)(2,1)} %lay_weights.1.own_hbm), channel_id=1, source_target_pairs={{0,64},{64,128},{128,192},{192,0},{1,65},{65,129},{129,193},{193,1... | collective-permute-start | bytes 3538952 | tf_op jit(solution)/shard_map/ppermute | solution.py:250
  22.0 28.2 %collective-permute-start = (bf16[512,1152]{1,0:T(8,128)(2,1)}, bf16[512,1152]{1,0:T(8,128)(2,1)S(1)}, u32[]{:S(2)}, u32[]{:S(2)}) collective-permute-start(bf16[512,1152]{1,0:T(8,128)(2,1)} %lay_weights.1.own_hbm), channel_id=1, source_target_pairs={{0,192},{64,0},{128,64},{192,128},{1,193},{65,1},{129,65},{193,129... | collective-permute-start | bytes 3538952 | tf_op jit(solution)/shard_map/ppermute | solution.py:253
  48.8 1.4 copy-start.4
  48.9 14.6 %collective-permute-start.2 = (bf16[256,1152]{1,0:T(8,128)(2,1)S(1)}, bf16[256,1152]{1,0:T(8,128)(2,1)}, u32[]{:S(2)}, u32[]{:S(2)}) collective-permute-start(bf16[256,1152]{1,0:T(8,128)(2,1)S(1)} %slice.16), channel_id=1, source_target_pairs={{0,64},{64,128},{128,192},{192,0},{1,65},{65,129},{129,193},{193,1... | collective-permute-start | bytes 1769480 | tf_op jit(solution)/shard_map/ppermute | solution.py:250
  50.2 64.4 %copy-start.5 = (bf16[512,1152]{1,0:T(8,128)(2,1)}, bf16[512,1152]{1,0:T(8,128)(2,1)S(1)}, u32[]{:S(2)}) copy-start(bf16[512,1152]{1,0:T(8,128)(2,1)S(1)} %collective-permute-done.next_hbm) | copy-start | bytes 3538948
  50.2 14.4 %collective-permute-start.3 = (bf16[256,1152]{1,0:T(8,128)(2,1)S(1)}, bf16[256,1152]{1,0:T(8,128)(2,1)}, u32[]{:S(2)}, u32[]{:S(2)}) collective-permute-start(bf16[256,1152]{1,0:T(8,128)(2,1)S(1)} %slice.17), channel_id=1, source_target_pairs={{0,192},{64,0},{128,64},{192,128},{1,193},{65,1},{129,65},{193,129... | collective-permute-start | bytes 1769480 | tf_op jit(solution)/shard_map/ppermute | solution.py:253
  126.2 101.9 %all-to-all-start.1 = ((bf16[64,8,4096]{2,1,0:T(8,128)(2,1)}), bf16[64,8,4096]{2,1,0:T(8,128)(2,1)}, u32[]{:S(2)}, u32[]{:S(2)}) async-start(bf16[64,8,4096]{2,1,0:T(8,128)(2,1)} %bitcast.19), calls=%async_computation.1 | async-start | bytes 8388608 | tf_op jit(solution)/shard_map/all_to_all | solution.py:226
  140.5 15.0 %collective-permute-start.5 = (bf16[256,1152]{1,0:T(8,128)(2,1)S(1)}, bf16[256,1152]{1,0:T(8,128)(2,1)S(1)}, u32[]{:S(2)}, u32[]{:S(2)}) collective-permute-start(bf16[256,1152]{1,0:T(8,128)(2,1)S(1)} %get-tuple-element.42), channel_id=1, source_target_pairs={{0,192},{64,0},{128,64},{192,128},{1,193},{65,1},{129,65},{193,129... | collective-permute-start | bytes 1769480 | tf_op jit(solution)/shard_map/ppermute | solution.py:253
  141.1 14.7 %collective-permute-start.4 = (bf16[256,1152]{1,0:T(8,128)(2,1)S(1)}, bf16[256,1152]{1,0:T(8,128)(2,1)S(1)}, u32[]{:S(2)}, u32[]{:S(2)}) collective-permute-start(bf16[256,1152]{1,0:T(8,128)(2,1)S(1)} %get-tuple-element.43), channel_id=1, source_target_pairs={{0,64},{64,128},{128,192},{192,0},{1,65},{65,129},{129,193},{193,1... | collective-permute-start | bytes 1769480 | tf_op jit(solution)/shard_map/ppermute | solution.py:250
  155.5 0.8 copy-start.2
  156.3 0.8 copy-start.3
  160.7 27.0 %collective-permute-start.6 = (bf16[512,1152]{1,0:T(8,128)(2,1)}, bf16[512,1152]{1,0:T(8,128)(2,1)S(1)}, u32[]{:S(2)}, u32[]{:S(2)}) collective-permute-start(bf16[512,1152]{1,0:T(8,128)(2,1)} %get-tuple-element.30), channel_id=1, source_target_pairs={{0,64},{64,128},{128,192},{192,0},{1,65},{65,129},{129,193},{193,1... | collective-permute-start | bytes 3538952 | tf_op jit(solution)/shard_map/ppermute | solution.py:250
  163.1 26.8 %collective-permute-start.7 = (bf16[512,1152]{1,0:T(8,128)(2,1)}, bf16[512,1152]{1,0:T(8,128)(2,1)S(1)}, u32[]{:S(2)}, u32[]{:S(2)}) collective-permute-start(bf16[512,1152]{1,0:T(8,128)(2,1)} %get-tuple-element.31), channel_id=1, source_target_pairs={{0,192},{64,0},{128,64},{192,128},{1,193},{65,1},{129,65},{193,129... | collective-permute-start | bytes 3538952 | tf_op jit(solution)/shard_map/ppermute | solution.py:253
  187.7 2.2 copy-start
  189.9 1.0 copy-start.1

commit v5 on v4

--- a/solution.py
+++ b/solution.py
@@ -11,6 +11,7 @@
 BF = jnp.bfloat16
 F32 = jnp.float32
 STEP = 512
+MERGE = 1024
 
 
 def contract(left, right, left_dim, right_dim):
@@ -51,7 +52,7 @@
     return held * spread
 
 
-def pick_rows(slots, ids_ref, cap_ref, comb_ref, tokens_ref, cot_ref, out_ref, pick_ref, high_ref, low_ref, scale_ref):
+def pick_rows(slots, ids_ref, cap_ref, comb_ref, tokens_ref, cot_ref, out_ref, pick_ref, shares_ref, scale_ref):
     i = pl.program_id(0)
     steps = pl.num_programs(0)
 
@@ -60,8 +61,9 @@
         held, chosen = hits(ids_ref, cap_ref, slots)
         pick_ref[...] = held.astype(BF)
         share = shares(held, chosen, comb_ref, slots)
-        high_ref[...] = share.astype(BF)
-        low_ref[...] = (share - share.astype(BF).astype(F32)).astype(BF)
+        count = share.shape[1]
+        shares_ref[:, :count] = share.astype(BF)
+        shares_ref[:, count:] = (share - share.astype(BF).astype(F32)).astype(BF)
         scale = jnp.sum(share, axis=1, keepdims=True)
         scale_ref[...] = jnp.broadcast_to(scale, scale_ref.shape)
 
@@ -80,7 +82,10 @@
             out_ref[:, c : c + STEP] = (scale * rows).astype(BF)
 
 
-def lay_weights(gate_ref, up_ref, down_ref, out_ref):
+def lay_weights(gate_ref, up_ref, down_ref, pick_ref, both_ref, out_ref, turned_ref):
+    count = pick_ref.shape[1]
+    turned_ref[:count, :] = pick_ref[...].T
+    turned_ref[count:, :] = both_ref[...].T
     hidden = gate_ref.shape[1]
     out_ref[:, :hidden] = gate_ref[...]
     out_ref[:, hidden : 2 * hidden] = up_ref[...]
@@ -173,7 +178,7 @@
 
 
 def merge(
-    slots, experts, ids_ref, pick_ref, high_ref, low_ref, cot_ref, o_ref, d_ref, mixed_ref, rows_ref, gc_ref, dots_ref
+    slots, experts, ids_ref, tables_ref, pick_ref, cot_ref, o_ref, d_ref, mixed_ref, rows_ref, gc_ref, dots_ref
 ):
     i = pl.program_id(0)
 
@@ -182,8 +187,10 @@
         dots_ref[...] = jnp.zeros(dots_ref.shape, F32)
 
     o = o_ref[...]
-    mixed_ref[...] = (contract(high_ref[...], o, 0, 0) + contract(low_ref[...], o, 0, 0)).astype(BF)
-    rows_ref[...] = contract(pick_ref[...], d_ref[...], 0, 0).astype(BF)
+    count = ids_ref.shape[1]
+    both = contract(tables_ref[count:, :], o, 1, 0)
+    mixed_ref[...] = (both[:count] + both[count:]).astype(BF)
+    rows_ref[...] = contract(tables_ref[:count, :], d_ref[...], 1, 0).astype(BF)
     dots_ref[...] += contract(o, cot_ref[...], 1, 1)
 
     @pl.when(i == pl.num_programs(0) - 1)
@@ -225,17 +232,17 @@
         x = x.reshape(peers, slots, 2 * width)
         return lax.all_to_all(x, "expert", 0, 0, tiled=True).reshape(rows, 2 * width)
 
-    block = width // 2
-    sent, *tables = pl.pallas_call(
+    block = width
+    sent, pick, both = pl.pallas_call(
         part(pick_rows, slots),
-        grid=(4,),
+        grid=(2,),
         in_specs=[
             fixed((top, count)), fixed((1, experts)), fixed((top, count)),
-            pl.BlockSpec((count, block), lambda i: (0, jnp.minimum(i, 1))),
-            pl.BlockSpec((count, block), lambda i: (0, jnp.maximum(i - 2, 0))),
+            pl.BlockSpec((count, block), lambda i: (0, 0)),
+            pl.BlockSpec((count, block), lambda i: (0, 0)),
         ],
-        out_specs=[pl.BlockSpec((rows, block), lambda i: (0, i))] + [fixed((rows, count))] * 3,
-        out_shape=[of((rows, 2 * width), BF)] + [of((rows, count), BF)] * 3,
+        out_specs=[pl.BlockSpec((rows, block), lambda i: (0, i)), fixed((rows, count)), fixed((rows, 2 * count))],
+        out_shape=[of((rows, 2 * width), BF), of((rows, count), BF), of((rows, 2 * count), BF)],
         scratch_shapes=[pltpu.VMEM((rows, 128), F32)],
         name="pick_rows", compiler_params=room(60), cost_estimate=cost(2 * pick_flops, 5 * rows * width),
     )(ids, limits, comb, tokens, cotangent)
@@ -252,10 +259,10 @@
     def down(x):
         return lax.ppermute(x, "dp", [(i, (i - 1) % parts) for i in range(parts)])
 
-    own = pl.pallas_call(
-        lay_weights, out_shape=of((deep, 3 * hidden), BF), name="lay_weights", compiler_params=room(60),
+    own, turned = pl.pallas_call(
+        lay_weights, out_shape=[of((deep, 3 * hidden), BF), of((3 * count, rows), BF)], name="lay_weights", compiler_params=room(60),
         cost_estimate=cost(0, 12 * deep * hidden),
-    )(w_gate[0], w_up[0], w_down[0])
+    )(w_gate[0], w_up[0], w_down[0], pick, both)
     before, after = up(own), down(own)
     far_low, far_high = up(before[:half]), down(after[half:])
 
@@ -315,20 +322,20 @@
 
     mixed, grad_tokens, grad_combine = pl.pallas_call(
         part(merge, slots, experts),
-        grid=(width // STEP,),
+        grid=(width // MERGE,),
         in_specs=[
-            fixed((top, count)), *[fixed((rows, count))] * 3,
-            pl.BlockSpec((count, STEP), lambda i: (0, i)),
-            pl.BlockSpec((rows, STEP), lambda i: (0, i)),
-            pl.BlockSpec((rows, STEP), lambda i: (0, i + width // STEP)),
+            fixed((top, count)), fixed((3 * count, rows)), fixed((rows, count)),
+            pl.BlockSpec((count, MERGE), lambda i: (0, i)),
+            pl.BlockSpec((rows, MERGE), lambda i: (0, i)),
+            pl.BlockSpec((rows, MERGE), lambda i: (0, i + width // MERGE)),
         ],
         out_specs=[
-            pl.BlockSpec((count, STEP), lambda i: (0, i)), pl.BlockSpec((count, STEP), lambda i: (0, i)), fixed((top, count)),
+            pl.BlockSpec((count, MERGE), lambda i: (0, i)), pl.BlockSpec((count, MERGE), lambda i: (0, i)), fixed((top, count)),
         ],
         out_shape=[of((count, width), BF), of((count, width), BF), of((top, count), F32)],
         scratch_shapes=[pltpu.VMEM((rows, count), F32)],
         name="merge", compiler_params=room(60), cost_estimate=cost(4 * pick_flops, 5 * rows * width),
-    )(ids, *tables, cotangent, back, back)
+    )(ids, turned, pick, cotangent, back, back)
     return (mixed, grad_tokens, grad_combine.T, grad_gate[None], grad_up[None], grad_down[None])
 
 

time: 234 us -> 233 us (level)
  no operation moved by 1% of the time
where the time goes in v5:
time: 233 us; the launch traced here: 232 us
  waiting for transfers between devices  163 us (70%)
  Pallas kernels  37.7 us (16%)
  starting transfers between devices  26.9 us (12%)
  local copies, waits for them, and re-layouts  3.83 us (2%)
    all_to_all x2, waiting for transfers between devices, exchange(): lax.all_to_all(x, 'expert', 0, 0, tiled=True).reshape(rows, 2 * width)  83.5 us
    ppermute x4, waiting for transfers between devices, up(): return lax.ppermute(x, 'dp', [(i, (i + 1) % parts) for i in range(parts)])  63.3 us
    all_to_all x2, starting transfers between devices, exchange(): lax.all_to_all(x, 'expert', 0, 0, tiled=True).reshape(rows, 2 * width)  18.2 us
    ppermute x4, waiting for transfers between devices, down(): return lax.ppermute(x, 'dp', [(i, (i - 1) % parts) for i in range(parts)])  16.1 us
    pallas_call x1, Pallas kernels, on_device(): pl.pallas_call(expert_math, in_specs=[pl.BlockSpec(memory_space=pltpu.SME...  11.6 us
    pallas_call x1, Pallas kernels, on_device(): pl.pallas_call(weight_grads, grid_spec=pltpu.PrefetchScalarGridSpec(num_s...  7.08 us
    ppermute x4, starting transfers between devices, up(): return lax.ppermute(x, 'dp', [(i, (i + 1) % parts) for i in range(parts)])  6.34 us
    pallas_call x1, Pallas kernels, on_device(): pl.pallas_call(part(merge, slots, experts), grid=(width // MERGE,), in_sp...  4.81 us
  transfers between devices with their start and end apart: 10, of which 9 were waited for; matrix products, arithmetic and copies ran while one was open for 1% of the time, Pallas kernels for 7%

profile of v5, /device:TPU:4, one launch (start us, length us, event | category | flops | bytes accessed | tf_op | source)
XLA Modules:
  0.0 232.3 jit_solution(14206690150337007063)
XLA Ops:
  0.6 4.5 %pick_rows.1 = (bf16[512,4096]{1,0:T(8,128)(2,1)}, bf16[512,128]{1,0:T(8,128)(2,1)}, bf16[512,256]{1,0:T(8,128)(2,1)}) custom-call(s32[8,128]{1,0:T(8,128)} %bitcast.24, s32[1,64]{1,0:T(1,128)} %bitcast.31, f32[8,128]{1,0:T(8,128)} %bitcast.29, bf16[128,2048]{1,0:T(8,128)(2,1)} %tokens_ref.1, bf16[128,2048]{1,0:T(8,128)(2,1)} %cot_ref.3), custom_call_target="tpu_custom_call" | custom-call | flops 536870912 | bytes 5242880 | tf_op jit(solution)/shard_map/pick_rows/pallas_call | solution.py:236
  5.1 12.4 %all-to-all-start = ((bf16[64,8,4096]{2,1,0:T(8,128)(2,1)}), bf16[64,8,4096]{2,1,0:T(8,128)(2,1)}, u32[]{:S(2)}, u32[]{:S(2)}) async-start(bf16[64,8,4096]{2,1,0:T(8,128)(2,1)} %bitcast.20), calls=%async_computation | async-start | bytes 8388608 | tf_op jit(solution)/shard_map/all_to_all | solution.py:233
  17.5 2.7 %lay_weights.1 = (bf16[512,1152]{1,0:T(8,128)(2,1)}, bf16[384,512]{1,0:T(8,128)(2,1)}) custom-call(bf16[512,384]{1,0:T(8,128)(2,1)} %bitcast.21, bf16[512,384]{1,0:T(8,128)(2,1)} %bitcast.22, bf16[384,512]{1,0:T(8,128)(2,1)} %bitcast.23, bf16[512,128]{1,0:T(8,128)(2,1)} %get-tuple-element.25.pick_ref, bf16[512,256]{1,0:T(8,128)(2,1)} %get-tuple-element.26.both_ref), custom_call_target="tpu_custom_call" | custom-call | bytes 2359296 | tf_op jit(solution)/shard_map/lay_weights/pallas_call | solution.py:262
  20.2 1.2 collective-permute-start.1
  21.4 0.8 collective-permute-start
  22.2 26.0 %collective-permute-done.1.prev_hbm = bf16[512,1152]{1,0:T(8,128)(2,1)S(1)} collective-permute-done((bf16[512,1152]{1,0:T(8,128)(2,1)}, bf16[512,1152]{1,0:T(8,128)(2,1)S(1)}, u32[]{:S(2)}, u32[]{:S(2)}) %collective-permute-start.1) | collective-permute-done | bytes 1179680 | tf_op jit(solution)/shard_map/ppermute | solution.py:257
  48.3 0.0 copy-start.4
  48.3 1.3 collective-permute-start.2
  49.6 0.0 collective-permute-done.next_hbm
  49.6 0.0 copy-start.5
  49.6 0.9 collective-permute-start.3
  50.6 0.0 copy-done.4
  50.6 12.4 %collective-permute-done.2.far_low_hbm = bf16[256,1152]{1,0:T(8,128)(2,1)} collective-permute-done((bf16[256,1152]{1,0:T(8,128)(2,1)S(1)}, bf16[256,1152]{1,0:T(8,128)(2,1)}, u32[]{:S(2)}, u32[]{:S(2)}) %collective-permute-start.2) | collective-permute-done | bytes 589856 | tf_op jit(solution)/shard_map/ppermute | solution.py:257
  63.0 1.0 collective-permute-done.3.far_high_hbm
  64.0 49.7 %all-to-all-done = bf16[64,8,4096]{2,1,0:T(8,128)(2,1)} async-done(((bf16[64,8,4096]{2,1,0:T(8,128)(2,1)}), bf16[64,8,4096]{2,1,0:T(8,128)(2,1)}, u32[]{:S(2)}, u32[]{:S(2)}) %all-to-all-start) | async-done | bytes 4194336 | tf_op jit(solution)/shard_map/all_to_all | solution.py:233
  113.7 0.0 copy-done.5
  113.7 11.6 %expert_math.1 = (bf16[512,4096]{1,0:T(8,128)(2,1)}, bf16[512,1152]{1,0:T(8,128)(2,1)}) custom-call(s32[1]{0:T(128)} %bitcast.6.me_ref, bf16[512,4096]{1,0:T(8,128)(2,1)} %bitcast.8.xg_hbm.x_ref.g_ref, bf16[512,1152]{1,0:T(8,128)(2,1)} %get-tuple-element.29.own_hbm, bf16[512,1152]{1,0:T(8,128)(2,1)} %copy-done.5, ...), custom_call_target="tpu_custom_call" | custom-call | flops 4831838208 | bytes 10485760 | tf_op jit(solution)/shard_map/expert_math/pallas_call | solution.py:271
  125.4 5.9 %all-to-all-start.1 = ((bf16[64,8,4096]{2,1,0:T(8,128)(2,1)}), bf16[64,8,4096]{2,1,0:T(8,128)(2,1)}, u32[]{:S(2)}, u32[]{:S(2)}) async-start(bf16[64,8,4096]{2,1,0:T(8,128)(2,1)} %bitcast.19), calls=%async_computation.1 | async-start | bytes 8388608 | tf_op jit(solution)/shard_map/all_to_all | solution.py:233
  131.3 7.1 %weight_grads.1.next_ref.prev_ref.own_ref = bf16[4,512,1152]{2,1,0:T(8,128)(2,1)} custom-call(s32[1]{0:T(128)} %bitcast.6.me_ref, bf16[512,4096]{1,0:T(8,128)(2,1)} %bitcast.8.xg_hbm.x_ref.g_ref, bf16[512,4096]{1,0:T(8,128)(2,1)} %bitcast.8.xg_hbm.x_ref.g_ref, bf16[512,1152]{1,0:T(8,128)(2,1)} %get-tuple-element.31.saved_ref), custom_call_target="tpu_custom_call" | custom-call | flops 2415919104 | bytes 6291456 | tf_op jit(solution)/shard_map/weight_grads/pallas_call | solution.py:284
  138.3 1.3 slice_bitcast_fusion
  139.7 0.6 collective-permute-start.5
  140.3 1.5 collective-permute-start.4
  141.8 12.9 %collective-permute-done.5.high_ref = bf16[256,1152]{1,0:T(8,128)(2,1)S(1)} collective-permute-done((bf16[256,1152]{1,0:T(8,128)(2,1)S(1)}, bf16[256,1152]{1,0:T(8,128)(2,1)S(1)}, u32[]{:S(2)}, u32[]{:S(2)}) %collective-permute-start.5) | collective-permute-done | bytes 589856 | tf_op jit(solution)/shard_map/ppermute | solution.py:260
  154.7 0.0 copy-start.2
  154.7 0.2 collective-permute-done.4.low_ref
  154.9 0.6 copy-done.2
  155.5 0.0 copy-start.3
  155.5 0.8 copy-done.3
  156.3 3.5 %add_far.1 = (bf16[512,1152]{1,0:T(8,128)(2,1)}, bf16[512,1152]{1,0:T(8,128)(2,1)}) custom-call(bf16[4,512,1152]{2,1,0:T(8,128)(2,1)} %weight_grads.1.next_ref.prev_ref.own_ref, bf16[4,512,1152]{2,1,0:T(8,128)(2,1)} %weight_grads.1.next_ref.prev_ref.own_ref, bf16[256,1152]{1,0:T(8,128)(2,1)} %copy-done.3, bf16[256,1152]{1,0:T(8,128)(2,1)} %copy-done.2), custom_call_target="tpu_custom_call" | custom-call | bytes 5898240 | tf_op jit(solution)/shard_map/add_far/pallas_call | solution.py:305
  159.9 2.4 %collective-permute-start.6 = (bf16[512,1152]{1,0:T(8,128)(2,1)}, bf16[512,1152]{1,0:T(8,128)(2,1)S(1)}, u32[]{:S(2)}, u32[]{:S(2)}) collective-permute-start(bf16[512,1152]{1,0:T(8,128)(2,1)} %get-tuple-element.32), channel_id=1, source_target_pairs={{0,64},{64,128},{128,192},{192,0},{1,65},{65,129},{129,193},{193,1... | collective-permute-start | bytes 3538952 | tf_op jit(solution)/shard_map/ppermute | solution.py:257
  162.2 0.0 collective-permute-start.7
  162.3 24.6 %collective-permute-done.6.below_ref = bf16[512,1152]{1,0:T(8,128)(2,1)S(1)} collective-permute-done((bf16[512,1152]{1,0:T(8,128)(2,1)}, bf16[512,1152]{1,0:T(8,128)(2,1)S(1)}, u32[]{:S(2)}, u32[]{:S(2)}) %collective-permute-start.6) | collective-permute-done | bytes 1179680 | tf_op jit(solution)/shard_map/ppermute | solution.py:257
  186.9 0.0 copy-start
  186.9 2.2 collective-permute-done.7.above_ref
  189.1 0.0 copy-done
  189.1 0.0 copy-start.1
  189.1 1.0 copy-done.1
  190.1 3.4 %add_last.1 = (bf16[512,384]{1,0:T(8,128)(2,1)}, bf16[512,384]{1,0:T(8,128)(2,1)}, bf16[384,512]{1,0:T(8,128)(2,1)}) custom-call(bf16[4,512,1152]{2,1,0:T(8,128)(2,1)} %weight_grads.1.next_ref.prev_ref.own_ref, bf16[512,1152]{1,0:T(8,128)(2,1)} %copy-done, bf16[512,1152]{1,0:T(8,128)(2,1)} %copy-done.1), custom_call_target="tpu_custom_call" | custom-call | bytes 4718592 | tf_op jit(solution)/shard_map/add_last/pallas_call | solution.py:313
  193.5 33.8 %all-to-all-done.1 = bf16[64,8,4096]{2,1,0:T(8,128)(2,1)} async-done(((bf16[64,8,4096]{2,1,0:T(8,128)(2,1)}), bf16[64,8,4096]{2,1,0:T(8,128)(2,1)}, u32[]{:S(2)}, u32[]{:S(2)}) %all-to-all-start.1) | async-done | bytes 4194336 | tf_op jit(solution)/shard_map/all_to_all | solution.py:233
  227.3 4.8 %merge.1 = (bf16[128,2048]{1,0:T(8,128)(2,1)}, bf16[128,2048]{1,0:T(8,128)(2,1)}, f32[8,128]{1,0:T(8,128)}) custom-call(s32[8,128]{1,0:T(8,128)} %bitcast.25, bf16[384,512]{1,0:T(8,128)(2,1)} %get-tuple-element.27.tables_ref, bf16[512,128]{1,0:T(8,128)(2,1)} %get-tuple-element.25.pick_ref, bf16[128,2048]{1,0:T(8,128)(2,1)} %cot_ref.3, ...), custom_call_target="tpu_custom_call" | custom-call | flops 1073741824 | bytes 5242880 | tf_op jit(solution)/shard_map/merge/pallas_call | solution.py:323
  (2 shorter events, 0.1 us)
Async XLA Ops:
  5.1 108.6 %all-to-all-start = ((bf16[64,8,4096]{2,1,0:T(8,128)(2,1)}), bf16[64,8,4096]{2,1,0:T(8,128)(2,1)}, u32[]{:S(2)}, u32[]{:S(2)}) async-start(bf16[64,8,4096]{2,1,0:T(8,128)(2,1)} %bitcast.20), calls=%async_computation | async-start | bytes 8388608 | tf_op jit(solution)/shard_map/all_to_all | solution.py:233
  20.2 28.1 %collective-permute-start.1 = (bf16[512,1152]{1,0:T(8,128)(2,1)}, bf16[512,1152]{1,0:T(8,128)(2,1)S(1)}, u32[]{:S(2)}, u32[]{:S(2)}) collective-permute-start(bf16[512,1152]{1,0:T(8,128)(2,1)} %get-tuple-element.29.own_hbm), channel_id=1, source_target_pairs={{0,64},{64,128},{128,192},{192,0},{1,65},{65,129},{129,193},{193,1... | collective-permute-start | bytes 3538952 | tf_op jit(solution)/shard_map/ppermute | solution.py:257
  21.4 28.2 %collective-permute-start = (bf16[512,1152]{1,0:T(8,128)(2,1)}, bf16[512,1152]{1,0:T(8,128)(2,1)S(1)}, u32[]{:S(2)}, u32[]{:S(2)}) collective-permute-start(bf16[512,1152]{1,0:T(8,128)(2,1)} %get-tuple-element.29.own_hbm), channel_id=1, source_target_pairs={{0,192},{64,0},{128,64},{192,128},{1,193},{65,1},{129,65},{193,129... | collective-permute-start | bytes 3538952 | tf_op jit(solution)/shard_map/ppermute | solution.py:260
  48.3 2.3 copy-start.4
  48.3 14.6 %collective-permute-start.2 = (bf16[256,1152]{1,0:T(8,128)(2,1)S(1)}, bf16[256,1152]{1,0:T(8,128)(2,1)}, u32[]{:S(2)}, u32[]{:S(2)}) collective-permute-start(bf16[256,1152]{1,0:T(8,128)(2,1)S(1)} %slice.16), channel_id=1, source_target_pairs={{0,64},{64,128},{128,192},{192,0},{1,65},{65,129},{129,193},{193,1... | collective-permute-start | bytes 1769480 | tf_op jit(solution)/shard_map/ppermute | solution.py:257
  49.6 64.1 %copy-start.5 = (bf16[512,1152]{1,0:T(8,128)(2,1)}, bf16[512,1152]{1,0:T(8,128)(2,1)S(1)}, u32[]{:S(2)}) copy-start(bf16[512,1152]{1,0:T(8,128)(2,1)S(1)} %collective-permute-done.next_hbm) | copy-start | bytes 3538948
  49.6 14.4 %collective-permute-start.3 = (bf16[256,1152]{1,0:T(8,128)(2,1)S(1)}, bf16[256,1152]{1,0:T(8,128)(2,1)}, u32[]{:S(2)}, u32[]{:S(2)}) collective-permute-start(bf16[256,1152]{1,0:T(8,128)(2,1)S(1)} %slice.17), channel_id=1, source_target_pairs={{0,192},{64,0},{128,64},{192,128},{1,193},{65,1},{129,65},{193,129... | collective-permute-start | bytes 1769480 | tf_op jit(solution)/shard_map/ppermute | solution.py:260
  125.4 101.9 %all-to-all-start.1 = ((bf16[64,8,4096]{2,1,0:T(8,128)(2,1)}), bf16[64,8,4096]{2,1,0:T(8,128)(2,1)}, u32[]{:S(2)}, u32[]{:S(2)}) async-start(bf16[64,8,4096]{2,1,0:T(8,128)(2,1)} %bitcast.19), calls=%async_computation.1 | async-start | bytes 8388608 | tf_op jit(solution)/shard_map/all_to_all | solution.py:233
  139.7 15.0 %collective-permute-start.5 = (bf16[256,1152]{1,0:T(8,128)(2,1)S(1)}, bf16[256,1152]{1,0:T(8,128)(2,1)S(1)}, u32[]{:S(2)}, u32[]{:S(2)}) collective-permute-start(bf16[256,1152]{1,0:T(8,128)(2,1)S(1)} %get-tuple-element.44), channel_id=1, source_target_pairs={{0,192},{64,0},{128,64},{192,128},{1,193},{65,1},{129,65},{193,129... | collective-permute-start | bytes 1769480 | tf_op jit(solution)/shard_map/ppermute | solution.py:260
  140.3 14.7 %collective-permute-start.4 = (bf16[256,1152]{1,0:T(8,128)(2,1)S(1)}, bf16[256,1152]{1,0:T(8,128)(2,1)S(1)}, u32[]{:S(2)}, u32[]{:S(2)}) collective-permute-start(bf16[256,1152]{1,0:T(8,128)(2,1)S(1)} %get-tuple-element.45), channel_id=1, source_target_pairs={{0,64},{64,128},{128,192},{192,0},{1,65},{65,129},{129,193},{193,1... | collective-permute-start | bytes 1769480 | tf_op jit(solution)/shard_map/ppermute | solution.py:257
  154.7 0.8 copy-start.2
  155.5 0.8 copy-start.3
  159.9 27.0 %collective-permute-start.6 = (bf16[512,1152]{1,0:T(8,128)(2,1)}, bf16[512,1152]{1,0:T(8,128)(2,1)S(1)}, u32[]{:S(2)}, u32[]{:S(2)}) collective-permute-start(bf16[512,1152]{1,0:T(8,128)(2,1)} %get-tuple-element.32), channel_id=1, source_target_pairs={{0,64},{64,128},{128,192},{192,0},{1,65},{65,129},{129,193},{193,1... | collective-permute-start | bytes 3538952 | tf_op jit(solution)/shard_map/ppermute | solution.py:257
  162.2 26.8 %collective-permute-start.7 = (bf16[512,1152]{1,0:T(8,128)(2,1)}, bf16[512,1152]{1,0:T(8,128)(2,1)S(1)}, u32[]{:S(2)}, u32[]{:S(2)}) collective-permute-start(bf16[512,1152]{1,0:T(8,128)(2,1)} %get-tuple-element.33), channel_id=1, source_target_pairs={{0,192},{64,0},{128,64},{192,128},{1,193},{65,1},{129,65},{193,129... | collective-permute-start | bytes 3538952 | tf_op jit(solution)/shard_map/ppermute | solution.py:260
  186.9 2.2 copy-start
  189.1 1.0 copy-start.1

commit v6 on v5

--- a/solution.py
+++ b/solution.py
@@ -11,7 +11,6 @@
 BF = jnp.bfloat16
 F32 = jnp.float32
 STEP = 512
-MERGE = 1024
 
 
 def contract(left, right, left_dim, right_dim):
@@ -52,34 +51,38 @@
     return held * spread
 
 
-def pick_rows(slots, ids_ref, cap_ref, comb_ref, tokens_ref, cot_ref, out_ref, pick_ref, shares_ref, scale_ref):
-    i = pl.program_id(0)
-    steps = pl.num_programs(0)
-
-    @pl.when(i == 0)
-    def _():
-        held, chosen = hits(ids_ref, cap_ref, slots)
-        pick_ref[...] = held.astype(BF)
-        share = shares(held, chosen, comb_ref, slots)
-        count = share.shape[1]
-        shares_ref[:, :count] = share.astype(BF)
-        shares_ref[:, count:] = (share - share.astype(BF).astype(F32)).astype(BF)
-        scale = jnp.sum(share, axis=1, keepdims=True)
-        scale_ref[...] = jnp.broadcast_to(scale, scale_ref.shape)
-
-    wide = out_ref.shape[1]
-
-    @pl.when(i < steps // 2)
-    def _():
-        for c in range(0, wide, STEP):
-            out_ref[:, c : c + STEP] = contract(pick_ref[...], tokens_ref[:, c : c + STEP], 1, 0).astype(BF)
-
-    @pl.when(i >= steps // 2)
-    def _():
-        scale = scale_ref[:, :1]
-        for c in range(0, wide, STEP):
-            rows = contract(pick_ref[...], cot_ref[:, c : c + STEP], 1, 0)
-            out_ref[:, c : c + STEP] = (scale * rows).astype(BF)
+def pick_rows(
+    slots, ids_ref, cap_ref, comb_ref, tokens_hbm, cot_hbm, out_hbm, pick_ref, shares_ref, in_ref, out_ref, in_sems, out_sems
+):
+    count, width = tokens_hbm.shape
+    pieces = [slice(c, c + STEP) for c in range(0, 2 * width, STEP)]
+
+    def arrive(n):
+        source, at = (tokens_hbm, n * STEP) if n * STEP < width else (cot_hbm, n * STEP - width)
+        return pltpu.make_async_copy(source.at[:, pl.ds(at, STEP)], in_ref.at[:, pl.ds(n * STEP, STEP)], in_sems.at[n])
+
+    def leave(n):
+        at = pl.ds(n * STEP, STEP)
+        return pltpu.make_async_copy(out_ref.at[:, at], out_hbm.at[:, at], out_sems.at[n])
+
+    for n in range(len(pieces)):
+        arrive(n).start()
+    held, chosen = hits(ids_ref, cap_ref, slots)
+    pick = held.astype(BF)
+    share = shares(held, chosen, comb_ref, slots)
+    pick_ref[...] = pick
+    shares_ref[:, :count] = share.astype(BF)
+    shares_ref[:, count:] = (share - share.astype(BF).astype(F32)).astype(BF)
+    scale = jnp.sum(share, axis=1, keepdims=True)
+    for n, piece in enumerate(pieces):
+        arrive(n).wait()
+        rows = contract(pick, in_ref[:, piece], 1, 0)
+        if n * STEP >= width:
+            rows = scale * rows
+        out_ref[:, piece] = rows.astype(BF)
+        leave(n).start()
+    for n in range(len(pieces)):
+        leave(n).wait()
 
 
 def lay_weights(gate_ref, up_ref, down_ref, pick_ref, both_ref, out_ref, turned_ref):
@@ -178,30 +181,60 @@
 
 
 def merge(
-    slots, experts, ids_ref, tables_ref, pick_ref, cot_ref, o_ref, d_ref, mixed_ref, rows_ref, gc_ref, dots_ref
+    slots, experts, ids_ref, tables_hbm, pick_hbm, cot_hbm, back_hbm, mixed_hbm, rows_hbm, gc_ref,
+    tables_ref, pick_ref, cot_ref, back_ref, mixed_ref, rows_ref, table_sems, cot_sems, in_sems, out_sems
 ):
-    i = pl.program_id(0)
-
-    @pl.when(i == 0)
-    def _():
-        dots_ref[...] = jnp.zeros(dots_ref.shape, F32)
-
-    o = o_ref[...]
-    count = ids_ref.shape[1]
-    both = contract(tables_ref[count:, :], o, 1, 0)
-    mixed_ref[...] = (both[:count] + both[count:]).astype(BF)
-    rows_ref[...] = contract(tables_ref[:count, :], d_ref[...], 1, 0).astype(BF)
-    dots_ref[...] += contract(o, cot_ref[...], 1, 1)
-
-    @pl.when(i == pl.num_programs(0) - 1)
-    def _():
-        top, count = ids_ref.shape
-        found = dots_ref[...] * pick_ref[...].astype(F32)
-        per_expert = jnp.sum(found.reshape(experts, slots, count), axis=1)
-        numbers = lax.broadcasted_iota(jnp.int32, (experts, count), 0)
-        for k in range(top):
-            hit = ids_ref[k : k + 1, :] == numbers
-            gc_ref[k : k + 1, :] = jnp.sum(jnp.where(hit, per_expert, 0.0), axis=0, keepdims=True)
+    top, count = ids_ref.shape
+    width = cot_hbm.shape[1]
+    steps = width // STEP
+    tables = [
+        pltpu.make_async_copy(tables_hbm, tables_ref, table_sems.at[0]),
+        pltpu.make_async_copy(pick_hbm, pick_ref, table_sems.at[1]),
+    ]
+
+    def at(n):
+        return pl.ds(n * STEP, STEP)
+
+    def arrive(n):
+        return pltpu.make_async_copy(back_hbm.at[:, at(n)], back_ref.at[:, at(n)], in_sems.at[n])
+
+    def cot(n):
+        return pltpu.make_async_copy(cot_hbm.at[:, at(n)], cot_ref.at[:, at(n)], cot_sems.at[n])
+
+    def leave(n):
+        from_ref, to_hbm, m = (mixed_ref, mixed_hbm, n) if n < steps else (rows_ref, rows_hbm, n - steps)
+        return pltpu.make_async_copy(from_ref.at[:, at(m)], to_hbm.at[:, at(m)], out_sems.at[n])
+
+    tables[0].start()
+    for n in range(steps):
+        arrive(n).start()
+        cot(n).start()
+        arrive(steps + n).start()
+    tables[1].start()
+    tables[0].wait()
+    dots = 0.0
+    for n in range(steps):
+        piece = slice(n * STEP, (n + 1) * STEP)
+        arrive(n).wait()
+        o = back_ref[:, piece]
+        both = contract(tables_ref[count:, :], o, 1, 0)
+        mixed_ref[:, piece] = (both[:count] + both[count:]).astype(BF)
+        leave(n).start()
+        cot(n).wait()
+        dots = dots + contract(o, cot_ref[:, piece], 1, 1)
+        arrive(steps + n).wait()
+        d = back_ref[:, width + n * STEP : width + (n + 1) * STEP]
+        rows_ref[:, piece] = contract(tables_ref[:count, :], d, 1, 0).astype(BF)
+        leave(steps + n).start()
+    tables[1].wait()
+    found = dots * pick_ref[...].astype(F32)
+    per_expert = jnp.sum(found.reshape(experts, slots, count), axis=1)
+    numbers = lax.broadcasted_iota(jnp.int32, (experts, count), 0)
+    for k in range(top):
+        hit = ids_ref[k : k + 1, :] == numbers
+        gc_ref[k : k + 1, :] = jnp.sum(jnp.where(hit, per_expert, 0.0), axis=0, keepdims=True)
+    for n in range(2 * steps):
+        leave(n).wait()
 
 
 def on_device(tokens, cotangent, expert_ids, combine, capacity, w_gate, w_up, w_down):
@@ -232,18 +265,18 @@
         x = x.reshape(peers, slots, 2 * width)
         return lax.all_to_all(x, "expert", 0, 0, tiled=True).reshape(rows, 2 * width)
 
-    block = width
+    whole = pl.BlockSpec(memory_space=pl.ANY)
+    vmem = pl.BlockSpec(memory_space=pltpu.VMEM)
+    copies = pltpu.SemaphoreType.DMA
+    pieces = 2 * width // STEP
     sent, pick, both = pl.pallas_call(
         part(pick_rows, slots),
-        grid=(2,),
-        in_specs=[
-            fixed((top, count)), fixed((1, experts)), fixed((top, count)),
-            pl.BlockSpec((count, block), lambda i: (0, 0)),
-            pl.BlockSpec((count, block), lambda i: (0, 0)),
+        in_specs=[vmem, vmem, vmem, whole, whole],
+        out_specs=[whole, vmem, vmem],
+        out_shape=[of((rows, 2 * width), BF), of((rows, count), BF), of((rows, 2 * count), BF)],
+        scratch_shapes=[
+            pltpu.VMEM((count, 2 * width), BF), pltpu.VMEM((rows, 2 * width), BF), copies((pieces,)), copies((pieces,)),
         ],
-        out_specs=[pl.BlockSpec((rows, block), lambda i: (0, i)), fixed((rows, count)), fixed((rows, 2 * count))],
-        out_shape=[of((rows, 2 * width), BF), of((rows, count), BF), of((rows, 2 * count), BF)],
-        scratch_shapes=[pltpu.VMEM((rows, 128), F32)],
         name="pick_rows", compiler_params=room(60), cost_estimate=cost(2 * pick_flops, 5 * rows * width),
     )(ids, limits, comb, tokens, cotangent)
     xg = exchange(sent)
@@ -266,8 +299,6 @@
     before, after = up(own), down(own)
     far_low, far_high = up(before[:half]), down(after[half:])
 
-    whole = pl.BlockSpec(memory_space=pl.ANY)
-    vmem = pl.BlockSpec(memory_space=pltpu.VMEM)
     od, saved = pl.pallas_call(
         expert_math,
         in_specs=[pl.BlockSpec(memory_space=pltpu.SMEM)] + [whole] * 6,
@@ -322,20 +353,16 @@
 
     mixed, grad_tokens, grad_combine = pl.pallas_call(
         part(merge, slots, experts),
-        grid=(width // MERGE,),
-        in_specs=[
-            fixed((top, count)), fixed((3 * count, rows)), fixed((rows, count)),
-            pl.BlockSpec((count, MERGE), lambda i: (0, i)),
-            pl.BlockSpec((rows, MERGE), lambda i: (0, i)),
-            pl.BlockSpec((rows, MERGE), lambda i: (0, i + width // MERGE)),
+        in_specs=[vmem] + [whole] * 4,
+        out_specs=[whole, whole, vmem],
+        out_shape=[of((count, width), BF), of((count, width), BF), of((top, count), F32)],
+        scratch_shapes=[
+            pltpu.VMEM((3 * count, rows), BF), pltpu.VMEM((rows, count), BF), pltpu.VMEM((count, width), BF),
+            pltpu.VMEM((rows, 2 * width), BF), pltpu.VMEM((count, width), BF), pltpu.VMEM((count, width), BF),
+            copies((2,)), copies((pieces // 2,)), copies((pieces,)), copies((pieces,)),
         ],
-        out_specs=[
-            pl.BlockSpec((count, MERGE), lambda i: (0, i)), pl.BlockSpec((count, MERGE), lambda i: (0, i)), fixed((top, count)),
-        ],
-        out_shape=[of((count, width), BF), of((count, width), BF), of((top, count), F32)],
-        scratch_shapes=[pltpu.VMEM((rows, count), F32)],
         name="merge", compiler_params=room(60), cost_estimate=cost(4 * pick_flops, 5 * rows * width),
-    )(ids, turned, pick, cotangent, back, back)
+    )(ids, turned, pick, cotangent, back)
     return (mixed, grad_tokens, grad_combine.T, grad_gate[None], grad_up[None], grad_down[None])
 
 

time: 233 us -> 237 us (1.017)
  Pallas kernels: 37.7 us -> 42.1 us
    pallas_call x2, Pallas kernels: 9.3 us -> 13.7 us  [the longest x1 8.11 us: on_device(): pl.pallas_call(part(merge, slots, experts), in_specs=[vmem] + [whole] * 4...]
where the time goes in v6:
time: 237 us
  waiting for transfers between devices  163 us (69%)
  Pallas kernels  42.1 us (18%)
  starting transfers between devices  26.9 us (11%)
  local copies, waits for them, and re-layouts  3.83 us (2%)
    all_to_all x2, waiting for transfers between devices, exchange(): lax.all_to_all(x, 'expert', 0, 0, tiled=True).reshape(rows, 2 * width)  83.6 us
    ppermute x4, waiting for transfers between devices, up(): return lax.ppermute(x, 'dp', [(i, (i + 1) % parts) for i in range(parts)])  63.3 us
    all_to_all x2, starting transfers between devices, exchange(): lax.all_to_all(x, 'expert', 0, 0, tiled=True).reshape(rows, 2 * width)  18.3 us
    ppermute x4, waiting for transfers between devices, down(): return lax.ppermute(x, 'dp', [(i, (i - 1) % parts) for i in range(parts)])  16.1 us
    pallas_call x1, Pallas kernels, on_device(): pl.pallas_call(expert_math, in_specs=[pl.BlockSpec(memory_space=pltpu.SME...  11.6 us
    pallas_call x1, Pallas kernels, on_device(): pl.pallas_call(part(merge, slots, experts), in_specs=[vmem] + [whole] * 4...  8.11 us
    pallas_call x1, Pallas kernels, on_device(): pl.pallas_call(weight_grads, grid_spec=pltpu.PrefetchScalarGridSpec(num_s...  7.08 us
    ppermute x4, starting transfers between devices, up(): return lax.ppermute(x, 'dp', [(i, (i + 1) % parts) for i in range(parts)])  6.23 us
  transfers between devices with their start and end apart: 10, of which 9 were waited for; matrix products, arithmetic and copies ran while one was open for 1% of the time, Pallas kernels for 7%

profile of v6, /device:TPU:4, one launch (start us, length us, event | category | flops | bytes accessed | tf_op | source)
XLA Modules:
  0.0 236.7 jit_solution(15236947443039243111)
XLA Ops:
  0.6 5.6 %pick_rows.1 = (bf16[512,4096]{1,0:T(8,128)(2,1)}, bf16[512,128]{1,0:T(8,128)(2,1)}, bf16[512,256]{1,0:T(8,128)(2,1)}) custom-call(s32[8,128]{1,0:T(8,128)} %bitcast.24, s32[1,64]{1,0:T(1,128)} %bitcast.31, f32[8,128]{1,0:T(8,128)} %bitcast.29, bf16[128,2048]{1,0:T(8,128)(2,1)} %tokens_hbm.1, bf16[128,2048]{1,0:T(8,128)(2,1)} %cot_hbm.3), custom_call_target="tpu_custom_call" | custom-call | flops 536870912 | bytes 5242880 | tf_op jit(solution)/shard_map/pick_rows/pallas_call | solution.py:272
  6.2 12.4 %all-to-all-start = ((bf16[64,8,4096]{2,1,0:T(8,128)(2,1)}), bf16[64,8,4096]{2,1,0:T(8,128)(2,1)}, u32[]{:S(2)}, u32[]{:S(2)}) async-start(bf16[64,8,4096]{2,1,0:T(8,128)(2,1)} %bitcast.20), calls=%async_computation | async-start | bytes 8388608 | tf_op jit(solution)/shard_map/all_to_all | solution.py:266
  18.7 2.7 %lay_weights.1 = (bf16[512,1152]{1,0:T(8,128)(2,1)}, bf16[384,512]{1,0:T(8,128)(2,1)}) custom-call(bf16[512,384]{1,0:T(8,128)(2,1)} %bitcast.21, bf16[512,384]{1,0:T(8,128)(2,1)} %bitcast.22, bf16[384,512]{1,0:T(8,128)(2,1)} %bitcast.23, bf16[512,128]{1,0:T(8,128)(2,1)} %get-tuple-element.25.pick_ref.pick_hbm, bf16[512,256]{1,0:T(8,128)(2,1)} %get-tuple-element.26.both_ref), custom_call_target="tpu_custom_call" | custom-call | bytes 2359296 | tf_op jit(solution)/shard_map/lay_weights/pallas_call | solution.py:295
  21.4 1.2 collective-permute-start.1
  22.5 0.9 collective-permute-start
  23.4 26.0 %collective-permute-done.1.prev_hbm = bf16[512,1152]{1,0:T(8,128)(2,1)S(1)} collective-permute-done((bf16[512,1152]{1,0:T(8,128)(2,1)}, bf16[512,1152]{1,0:T(8,128)(2,1)S(1)}, u32[]{:S(2)}, u32[]{:S(2)}) %collective-permute-start.1) | collective-permute-done | bytes 1179680 | tf_op jit(solution)/shard_map/ppermute | solution.py:290
  49.4 0.0 copy-start.4
  49.5 1.2 collective-permute-start.2
  50.7 0.0 collective-permute-done.next_hbm
  50.7 0.0 copy-start.5
  50.8 1.0 collective-permute-start.3
  51.7 0.0 copy-done.4
  51.7 12.4 %collective-permute-done.2.far_low_hbm = bf16[256,1152]{1,0:T(8,128)(2,1)} collective-permute-done((bf16[256,1152]{1,0:T(8,128)(2,1)S(1)}, bf16[256,1152]{1,0:T(8,128)(2,1)}, u32[]{:S(2)}, u32[]{:S(2)}) %collective-permute-start.2) | collective-permute-done | bytes 589856 | tf_op jit(solution)/shard_map/ppermute | solution.py:290
  64.1 1.0 collective-permute-done.3.far_high_hbm
  65.1 49.8 %all-to-all-done = bf16[64,8,4096]{2,1,0:T(8,128)(2,1)} async-done(((bf16[64,8,4096]{2,1,0:T(8,128)(2,1)}), bf16[64,8,4096]{2,1,0:T(8,128)(2,1)}, u32[]{:S(2)}, u32[]{:S(2)}) %all-to-all-start) | async-done | bytes 4194336 | tf_op jit(solution)/shard_map/all_to_all | solution.py:266
  114.9 0.0 copy-done.5
  114.9 11.6 %expert_math.1 = (bf16[512,4096]{1,0:T(8,128)(2,1)}, bf16[512,1152]{1,0:T(8,128)(2,1)}) custom-call(s32[1]{0:T(128)} %bitcast.6.me_ref, bf16[512,4096]{1,0:T(8,128)(2,1)} %bitcast.8.xg_hbm.x_ref.g_ref, bf16[512,1152]{1,0:T(8,128)(2,1)} %get-tuple-element.29.own_hbm, bf16[512,1152]{1,0:T(8,128)(2,1)} %copy-done.5, ...), custom_call_target="tpu_custom_call" | custom-call | flops 4831838208 | bytes 10485760 | tf_op jit(solution)/shard_map/expert_math/pallas_call | solution.py:302
  126.5 5.9 %all-to-all-start.1 = ((bf16[64,8,4096]{2,1,0:T(8,128)(2,1)}), bf16[64,8,4096]{2,1,0:T(8,128)(2,1)}, u32[]{:S(2)}, u32[]{:S(2)}) async-start(bf16[64,8,4096]{2,1,0:T(8,128)(2,1)} %bitcast.19), calls=%async_computation.1 | async-start | bytes 8388608 | tf_op jit(solution)/shard_map/all_to_all | solution.py:266
  132.4 7.1 %weight_grads.1.next_ref.prev_ref.own_ref = bf16[4,512,1152]{2,1,0:T(8,128)(2,1)} custom-call(s32[1]{0:T(128)} %bitcast.6.me_ref, bf16[512,4096]{1,0:T(8,128)(2,1)} %bitcast.8.xg_hbm.x_ref.g_ref, bf16[512,4096]{1,0:T(8,128)(2,1)} %bitcast.8.xg_hbm.x_ref.g_ref, bf16[512,1152]{1,0:T(8,128)(2,1)} %get-tuple-element.31.saved_ref), custom_call_target="tpu_custom_call" | custom-call | flops 2415919104 | bytes 6291456 | tf_op jit(solution)/shard_map/weight_grads/pallas_call | solution.py:315
  139.5 1.3 slice_bitcast_fusion
  140.8 0.6 collective-permute-start.5
  141.4 1.5 collective-permute-start.4
  142.9 12.9 %collective-permute-done.5.high_ref = bf16[256,1152]{1,0:T(8,128)(2,1)S(1)} collective-permute-done((bf16[256,1152]{1,0:T(8,128)(2,1)S(1)}, bf16[256,1152]{1,0:T(8,128)(2,1)S(1)}, u32[]{:S(2)}, u32[]{:S(2)}) %collective-permute-start.5) | collective-permute-done | bytes 589856 | tf_op jit(solution)/shard_map/ppermute | solution.py:293
  155.8 0.0 copy-start.2
  155.8 0.3 collective-permute-done.4.low_ref
  156.1 0.6 copy-done.2
  156.7 0.0 copy-start.3
  156.7 0.8 copy-done.3
  157.5 3.5 %add_far.1 = (bf16[512,1152]{1,0:T(8,128)(2,1)}, bf16[512,1152]{1,0:T(8,128)(2,1)}) custom-call(bf16[4,512,1152]{2,1,0:T(8,128)(2,1)} %weight_grads.1.next_ref.prev_ref.own_ref, bf16[4,512,1152]{2,1,0:T(8,128)(2,1)} %weight_grads.1.next_ref.prev_ref.own_ref, bf16[256,1152]{1,0:T(8,128)(2,1)} %copy-done.3, bf16[256,1152]{1,0:T(8,128)(2,1)} %copy-done.2), custom_call_target="tpu_custom_call" | custom-call | bytes 5898240 | tf_op jit(solution)/shard_map/add_far/pallas_call | solution.py:336
  161.0 2.3 collective-permute-start.6
  163.4 0.0 collective-permute-start.7
  163.4 24.6 %collective-permute-done.6.below_ref = bf16[512,1152]{1,0:T(8,128)(2,1)S(1)} collective-permute-done((bf16[512,1152]{1,0:T(8,128)(2,1)}, bf16[512,1152]{1,0:T(8,128)(2,1)S(1)}, u32[]{:S(2)}, u32[]{:S(2)}) %collective-permute-start.6) | collective-permute-done | bytes 1179680 | tf_op jit(solution)/shard_map/ppermute | solution.py:290
  188.0 0.0 copy-start
  188.0 2.2 collective-permute-done.7.above_ref
  190.2 0.0 copy-done
  190.2 0.0 copy-start.1
  190.2 1.0 copy-done.1
  191.2 3.4 %add_last.1 = (bf16[512,384]{1,0:T(8,128)(2,1)}, bf16[512,384]{1,0:T(8,128)(2,1)}, bf16[384,512]{1,0:T(8,128)(2,1)}) custom-call(bf16[4,512,1152]{2,1,0:T(8,128)(2,1)} %weight_grads.1.next_ref.prev_ref.own_ref, bf16[512,1152]{1,0:T(8,128)(2,1)} %copy-done, bf16[512,1152]{1,0:T(8,128)(2,1)} %copy-done.1), custom_call_target="tpu_custom_call" | custom-call | bytes 4718592 | tf_op jit(solution)/shard_map/add_last/pallas_call | solution.py:344
  194.6 33.8 %all-to-all-done.1 = bf16[64,8,4096]{2,1,0:T(8,128)(2,1)} async-done(((bf16[64,8,4096]{2,1,0:T(8,128)(2,1)}), bf16[64,8,4096]{2,1,0:T(8,128)(2,1)}, u32[]{:S(2)}, u32[]{:S(2)}) %all-to-all-start.1) | async-done | bytes 4194336 | tf_op jit(solution)/shard_map/all_to_all | solution.py:266
  228.5 8.1 %merge.1 = (bf16[128,2048]{1,0:T(8,128)(2,1)}, bf16[128,2048]{1,0:T(8,128)(2,1)}, f32[8,128]{1,0:T(8,128)}) custom-call(s32[8,128]{1,0:T(8,128)} %bitcast.25, bf16[384,512]{1,0:T(8,128)(2,1)} %get-tuple-element.27.tables_hbm, bf16[512,128]{1,0:T(8,128)(2,1)} %get-tuple-element.25.pick_ref.pick_hbm, bf16[128,2048]{1,0:T(8,128)(2,1)} %cot_hbm.3, ...), custom_call_target="tpu_custom_call" | custom-call | flops 1073741824 | bytes 5242880 | tf_op jit(solution)/shard_map/merge/pallas_call | solution.py:354
  (2 shorter events, 0.1 us)
Async XLA Ops:
  6.2 108.6 %all-to-all-start = ((bf16[64,8,4096]{2,1,0:T(8,128)(2,1)}), bf16[64,8,4096]{2,1,0:T(8,128)(2,1)}, u32[]{:S(2)}, u32[]{:S(2)}) async-start(bf16[64,8,4096]{2,1,0:T(8,128)(2,1)} %bitcast.20), calls=%async_computation | async-start | bytes 8388608 | tf_op jit(solution)/shard_map/all_to_all | solution.py:266
  21.4 28.1 %collective-permute-start.1 = (bf16[512,1152]{1,0:T(8,128)(2,1)}, bf16[512,1152]{1,0:T(8,128)(2,1)S(1)}, u32[]{:S(2)}, u32[]{:S(2)}) collective-permute-start(bf16[512,1152]{1,0:T(8,128)(2,1)} %get-tuple-element.29.own_hbm), channel_id=1, source_target_pairs={{0,64},{64,128},{128,192},{192,0},{1,65},{65,129},{129,193},{193,1... | collective-permute-start | bytes 3538952 | tf_op jit(solution)/shard_map/ppermute | solution.py:290
  22.5 28.2 %collective-permute-start = (bf16[512,1152]{1,0:T(8,128)(2,1)}, bf16[512,1152]{1,0:T(8,128)(2,1)S(1)}, u32[]{:S(2)}, u32[]{:S(2)}) collective-permute-start(bf16[512,1152]{1,0:T(8,128)(2,1)} %get-tuple-element.29.own_hbm), channel_id=1, source_target_pairs={{0,192},{64,0},{128,64},{192,128},{1,193},{65,1},{129,65},{193,129... | collective-permute-start | bytes 3538952 | tf_op jit(solution)/shard_map/ppermute | solution.py:293
  49.4 2.3 copy-start.4
  49.5 14.6 %collective-permute-start.2 = (bf16[256,1152]{1,0:T(8,128)(2,1)S(1)}, bf16[256,1152]{1,0:T(8,128)(2,1)}, u32[]{:S(2)}, u32[]{:S(2)}) collective-permute-start(bf16[256,1152]{1,0:T(8,128)(2,1)S(1)} %slice.16), channel_id=1, source_target_pairs={{0,64},{64,128},{128,192},{192,0},{1,65},{65,129},{129,193},{193,1... | collective-permute-start | bytes 1769480 | tf_op jit(solution)/shard_map/ppermute | solution.py:290
  50.7 64.2 %copy-start.5 = (bf16[512,1152]{1,0:T(8,128)(2,1)}, bf16[512,1152]{1,0:T(8,128)(2,1)S(1)}, u32[]{:S(2)}) copy-start(bf16[512,1152]{1,0:T(8,128)(2,1)S(1)} %collective-permute-done.next_hbm) | copy-start | bytes 3538948
  50.8 14.4 %collective-permute-start.3 = (bf16[256,1152]{1,0:T(8,128)(2,1)S(1)}, bf16[256,1152]{1,0:T(8,128)(2,1)}, u32[]{:S(2)}, u32[]{:S(2)}) collective-permute-start(bf16[256,1152]{1,0:T(8,128)(2,1)S(1)} %slice.17), channel_id=1, source_target_pairs={{0,192},{64,0},{128,64},{192,128},{1,193},{65,1},{129,65},{193,129... | collective-permute-start | bytes 1769480 | tf_op jit(solution)/shard_map/ppermute | solution.py:293
  126.5 101.9 %all-to-all-start.1 = ((bf16[64,8,4096]{2,1,0:T(8,128)(2,1)}), bf16[64,8,4096]{2,1,0:T(8,128)(2,1)}, u32[]{:S(2)}, u32[]{:S(2)}) async-start(bf16[64,8,4096]{2,1,0:T(8,128)(2,1)} %bitcast.19), calls=%async_computation.1 | async-start | bytes 8388608 | tf_op jit(solution)/shard_map/all_to_all | solution.py:266
  140.8 15.0 %collective-permute-start.5 = (bf16[256,1152]{1,0:T(8,128)(2,1)S(1)}, bf16[256,1152]{1,0:T(8,128)(2,1)S(1)}, u32[]{:S(2)}, u32[]{:S(2)}) collective-permute-start(bf16[256,1152]{1,0:T(8,128)(2,1)S(1)} %get-tuple-element.44), channel_id=1, source_target_pairs={{0,192},{64,0},{128,64},{192,128},{1,193},{65,1},{129,65},{193,129... | collective-permute-start | bytes 1769480 | tf_op jit(solution)/shard_map/ppermute | solution.py:293
  141.4 14.7 %collective-permute-start.4 = (bf16[256,1152]{1,0:T(8,128)(2,1)S(1)}, bf16[256,1152]{1,0:T(8,128)(2,1)S(1)}, u32[]{:S(2)}, u32[]{:S(2)}) collective-permute-start(bf16[256,1152]{1,0:T(8,128)(2,1)S(1)} %get-tuple-element.45), channel_id=1, source_target_pairs={{0,64},{64,128},{128,192},{192,0},{1,65},{65,129},{129,193},{193,1... | collective-permute-start | bytes 1769480 | tf_op jit(solution)/shard_map/ppermute | solution.py:290
  155.8 0.8 copy-start.2
  156.7 0.8 copy-start.3
  161.0 27.0 %collective-permute-start.6 = (bf16[512,1152]{1,0:T(8,128)(2,1)}, bf16[512,1152]{1,0:T(8,128)(2,1)S(1)}, u32[]{:S(2)}, u32[]{:S(2)}) collective-permute-start(bf16[512,1152]{1,0:T(8,128)(2,1)} %get-tuple-element.32), channel_id=1, source_target_pairs={{0,64},{64,128},{128,192},{192,0},{1,65},{65,129},{129,193},{193,1... | collective-permute-start | bytes 3538952 | tf_op jit(solution)/shard_map/ppermute | solution.py:290
  163.4 26.8 %collective-permute-start.7 = (bf16[512,1152]{1,0:T(8,128)(2,1)}, bf16[512,1152]{1,0:T(8,128)(2,1)S(1)}, u32[]{:S(2)}, u32[]{:S(2)}) collective-permute-start(bf16[512,1152]{1,0:T(8,128)(2,1)} %get-tuple-element.33), channel_id=1, source_target_pairs={{0,192},{64,0},{128,64},{192,128},{1,193},{65,1},{129,65},{193,129... | collective-permute-start | bytes 3538952 | tf_op jit(solution)/shard_map/ppermute | solution.py:293
  188.0 2.2 copy-start
  190.2 1.0 copy-start.1

commit v7 on v5

--- a/solution.py
+++ b/solution.py
@@ -93,12 +93,13 @@
 
 
 def expert_math(
-    me_ref, xg_hbm, own_hbm, next_hbm, far_low_hbm, far_high_hbm, prev_hbm, od_hbm, saved_ref, xg_ref, w_ref, od_ref, in_sems, w_sems, out_sems
+    me_ref, xg_hbm, own_hbm, next_hbm, far_low_ref, far_high_ref, prev_hbm, od_hbm, saved_ref, xg_ref, w_ref, od_ref, in_sems, w_sems, out_sems
 ):
-    parts, deep, hidden = w_ref.shape
+    deep, hidden = own_hbm.shape
     hidden //= 3
+    parts = od_ref.shape[1] // (2 * deep)
     half = deep // 2
-    order = (0, 1, 3, 2)
+    order = (2, 0, 1, 3)
 
     def lanes(n):
         block = lax.rem(me_ref[0] + n % parts, parts) + n // parts * parts
@@ -110,38 +111,43 @@
     def leave(n):
         return pltpu.make_async_copy(od_ref.at[:, pl.ds(n * deep, deep)], od_hbm.at[:, lanes(n)], out_sems.at[n])
 
-    def weights(n):
-        if n != 2:
-            source = {0: own_hbm, 1: next_hbm, 3: prev_hbm}[n]
-            return [pltpu.make_async_copy(source, w_ref.at[n], w_sems.at[n])]
-        return [
-            pltpu.make_async_copy(far_low_hbm, w_ref.at[n, pl.ds(0, half)], w_sems.at[n]),
-            pltpu.make_async_copy(far_high_hbm, w_ref.at[n, pl.ds(half, half)], w_sems.at[parts]),
-        ]
-
-    for n in order:
-        for copy in weights(n):
-            copy.start()
+    places = {0: 0, 1: 1, 3: 2}
+    sources = {0: own_hbm, 1: next_hbm, 3: prev_hbm}
+    moved = {n: pltpu.make_async_copy(sources[n], w_ref.at[p], w_sems.at[p]) for n, p in places.items()}
+
+    def pieces(n):
+        if n == 2:
+            return [(0, far_low_ref), (half, far_high_ref)]
+        return [(0, w_ref.at[places[n]])]
+
+    for n in order:
         arrive(n).start()
+        if n in moved:
+            moved[n].start()
     for n in order:
         arrive(parts + n).start()
     hu = da = 0.0
     for n in order:
-        for copy in weights(n):
-            copy.wait()
         arrive(n).wait()
-        hu = hu + contract(xg_ref[:, n * deep : (n + 1) * deep], w_ref[n, :, : 2 * hidden], 1, 0)
+        if n in moved:
+            moved[n].wait()
+        for start, w in pieces(n):
+            at = n * deep + start
+            hu = hu + contract(xg_ref[:, at : at + w.shape[0]], w[:, : 2 * hidden], 1, 0)
     h, u = hu[:, :hidden], hu[:, hidden:]
     s = jax.nn.sigmoid(h)
     a = (h * s * u).astype(BF)
     saved_ref[:, 2 * hidden :] = a
     for n in order:
-        od_ref[:, n * deep : (n + 1) * deep] = contract(a, w_ref[n, :, 2 * hidden :], 1, 1).astype(BF)
+        for start, w in pieces(n):
+            at = n * deep + start
+            od_ref[:, at : at + w.shape[0]] = contract(a, w[:, 2 * hidden :], 1, 1).astype(BF)
         leave(n).start()
     for n in order:
         arrive(parts + n).wait()
-        g = xg_ref[:, (parts + n) * deep : (parts + n + 1) * deep]
-        da = da + contract(g, w_ref[n, :, 2 * hidden :], 1, 0)
+        for start, w in pieces(n):
+            at = (parts + n) * deep + start
+            da = da + contract(xg_ref[:, at : at + w.shape[0]], w[:, 2 * hidden :], 1, 0)
     dh = (da * u * s * (1.0 + h * (1.0 - s))).astype(BF)
     du = (da * h * s).astype(BF)
     saved_ref[:, :hidden] = dh
@@ -149,7 +155,9 @@
     both = jnp.concatenate([dh, du], axis=1)
     for n in order:
         m = parts + n
-        od_ref[:, m * deep : (m + 1) * deep] = contract(both, w_ref[n, :, : 2 * hidden], 1, 1).astype(BF)
+        for start, w in pieces(n):
+            at = m * deep + start
+            od_ref[:, at : at + w.shape[0]] = contract(both, w[:, : 2 * hidden], 1, 1).astype(BF)
         leave(m).start()
     for n in range(2 * parts):
         leave(n).wait()
@@ -270,14 +278,14 @@
     vmem = pl.BlockSpec(memory_space=pltpu.VMEM)
     od, saved = pl.pallas_call(
         expert_math,
-        in_specs=[pl.BlockSpec(memory_space=pltpu.SMEM)] + [whole] * 6,
+        in_specs=[pl.BlockSpec(memory_space=pltpu.SMEM), whole, whole, whole, vmem, vmem, whole],
         out_specs=[whole, vmem],
         out_shape=[of((rows, 2 * width), BF), of((rows, 3 * hidden), BF)],
         scratch_shapes=[
-            pltpu.VMEM((rows, 2 * width), BF), pltpu.VMEM((parts, deep, 3 * hidden), BF), pltpu.VMEM((rows, 2 * width), BF),
-            pltpu.SemaphoreType.DMA((2 * parts,)), pltpu.SemaphoreType.DMA((parts + 1,)), pltpu.SemaphoreType.DMA((2 * parts,)),
+            pltpu.VMEM((rows, 2 * width), BF), pltpu.VMEM((3, deep, 3 * hidden), BF), pltpu.VMEM((rows, 2 * width), BF),
+            pltpu.SemaphoreType.DMA((2 * parts,)), pltpu.SemaphoreType.DMA((3,)), pltpu.SemaphoreType.DMA((2 * parts,)),
         ],
-        name="expert_math", compiler_params=room(60), cost_estimate=cost(6 * unit, 10 * rows * width),
+        name="expert_math", compiler_params=room(51), cost_estimate=cost(6 * unit, 10 * rows * width),
     )(me, xg, own, after, far_low, far_high, before)
     back = exchange(od)
 
@@ -294,7 +302,7 @@
             out_specs=pl.BlockSpec((1, deep, 3 * hidden), lambda i, me: (i, 0, 0)),
         ),
         out_shape=of((parts, deep, 3 * hidden), BF),
-        name="weight_grads", compiler_params=room(60), cost_estimate=cost(3 * unit, 6 * rows * width),
+        name="weight_grads", compiler_params=room(51), cost_estimate=cost(3 * unit, 6 * rows * width),
     )(me, xg, xg, saved)
     low, high = up(grads[2, :half]), down(grads[2, half:])
 

time: 233 us -> 231 us (level)
  no operation moved by 1% of the time
where the time goes in v7:
time: 231 us
  waiting for transfers between devices  163 us (71%)
  Pallas kernels  35.5 us (15%)
  starting transfers between devices  26.9 us (12%)
  local copies, waits for them, and re-layouts  4.02 us (2%)
    all_to_all x2, waiting for transfers between devices, exchange(): lax.all_to_all(x, 'expert', 0, 0, tiled=True).reshape(rows, 2 * width)  84.1 us
    ppermute x4, waiting for transfers between devices, up(): return lax.ppermute(x, 'dp', [(i, (i + 1) % parts) for i in range(parts)])  63.1 us
    all_to_all x2, starting transfers between devices, exchange(): lax.all_to_all(x, 'expert', 0, 0, tiled=True).reshape(rows, 2 * width)  18.2 us
    ppermute x4, waiting for transfers between devices, down(): return lax.ppermute(x, 'dp', [(i, (i - 1) % parts) for i in range(parts)])  16.1 us
    pallas_call x1, Pallas kernels, on_device(): pl.pallas_call(expert_math, in_specs=[pl.BlockSpec(memory_space=pltpu.SME...  9.93 us
    pallas_call x1, Pallas kernels, on_device(): pl.pallas_call(weight_grads, grid_spec=pltpu.PrefetchScalarGridSpec(num_s...  6.66 us
    ppermute x4, starting transfers between devices, up(): return lax.ppermute(x, 'dp', [(i, (i + 1) % parts) for i in range(parts)])  6.38 us
    pallas_call x1, Pallas kernels, on_device(): pl.pallas_call(part(merge, slots, experts), grid=(width // MERGE,), in_sp...  4.8 us
  transfers between devices with their start and end apart: 10, of which 9 were waited for; matrix products, arithmetic and copies ran while one was open for 1% of the time, Pallas kernels for 7%

profile of v7, /device:TPU:4, one launch (start us, length us, event | category | flops | bytes accessed | tf_op | source)
XLA Modules:
  0.0 230.6 jit_solution(9044901174292112975)
XLA Ops:
  0.6 4.5 %pick_rows.1 = (bf16[512,4096]{1,0:T(8,128)(2,1)}, bf16[512,128]{1,0:T(8,128)(2,1)}, bf16[512,256]{1,0:T(8,128)(2,1)}) custom-call(s32[8,128]{1,0:T(8,128)} %bitcast.24, s32[1,64]{1,0:T(1,128)} %bitcast.31, f32[8,128]{1,0:T(8,128)} %bitcast.29, bf16[128,2048]{1,0:T(8,128)(2,1)} %tokens_ref.1, bf16[128,2048]{1,0:T(8,128)(2,1)} %cot_ref.3), custom_call_target="tpu_custom_call" | custom-call | flops 536870912 | bytes 5242880 | tf_op jit(solution)/shard_map/pick_rows/pallas_call | solution.py:244
  5.2 12.4 %all-to-all-start = ((bf16[64,8,4096]{2,1,0:T(8,128)(2,1)}), bf16[64,8,4096]{2,1,0:T(8,128)(2,1)}, u32[]{:S(2)}, u32[]{:S(2)}) async-start(bf16[64,8,4096]{2,1,0:T(8,128)(2,1)} %bitcast.20), calls=%async_computation | async-start | bytes 8388608 | tf_op jit(solution)/shard_map/all_to_all | solution.py:241
  17.5 2.7 %lay_weights.1 = (bf16[512,1152]{1,0:T(8,128)(2,1)}, bf16[384,512]{1,0:T(8,128)(2,1)}) custom-call(bf16[512,384]{1,0:T(8,128)(2,1)} %bitcast.21, bf16[512,384]{1,0:T(8,128)(2,1)} %bitcast.22, bf16[384,512]{1,0:T(8,128)(2,1)} %bitcast.23, bf16[512,128]{1,0:T(8,128)(2,1)} %get-tuple-element.25.pick_ref, bf16[512,256]{1,0:T(8,128)(2,1)} %get-tuple-element.26.both_ref), custom_call_target="tpu_custom_call" | custom-call | bytes 2359296 | tf_op jit(solution)/shard_map/lay_weights/pallas_call | solution.py:270
  20.2 1.2 collective-permute-start.1
  21.4 0.8 collective-permute-start
  22.2 26.0 %collective-permute-done.1.prev_hbm = bf16[512,1152]{1,0:T(8,128)(2,1)S(1)} collective-permute-done((bf16[512,1152]{1,0:T(8,128)(2,1)}, bf16[512,1152]{1,0:T(8,128)(2,1)S(1)}, u32[]{:S(2)}, u32[]{:S(2)}) %collective-permute-start.1) | collective-permute-done | bytes 1179680 | tf_op jit(solution)/shard_map/ppermute | solution.py:265
  48.3 0.0 copy-start.4
  48.3 1.3 collective-permute-start.2
  49.6 0.0 collective-permute-done.next_hbm
  49.6 0.0 copy-start.5
  49.6 0.9 collective-permute-start.3
  50.6 0.1 copy-done.5
  50.6 0.0 copy-done.4
  50.6 12.2 %collective-permute-done.2.far_low_ref = bf16[256,1152]{1,0:T(8,128)(2,1)S(1)} collective-permute-done((bf16[256,1152]{1,0:T(8,128)(2,1)S(1)}, bf16[256,1152]{1,0:T(8,128)(2,1)S(1)}, u32[]{:S(2)}, u32[]{:S(2)}) %collective-permute-start.2) | collective-permute-done | bytes 589856 | tf_op jit(solution)/shard_map/ppermute | solution.py:265
  62.9 1.0 collective-permute-done.3.far_high_ref
  63.9 49.9 %all-to-all-done = bf16[64,8,4096]{2,1,0:T(8,128)(2,1)} async-done(((bf16[64,8,4096]{2,1,0:T(8,128)(2,1)}), bf16[64,8,4096]{2,1,0:T(8,128)(2,1)}, u32[]{:S(2)}, u32[]{:S(2)}) %all-to-all-start) | async-done | bytes 4194336 | tf_op jit(solution)/shard_map/all_to_all | solution.py:241
  113.8 9.9 %expert_math.1 = (bf16[512,4096]{1,0:T(8,128)(2,1)}, bf16[512,1152]{1,0:T(8,128)(2,1)S(1)}) custom-call(s32[1]{0:T(128)} %bitcast.6.me_ref, bf16[512,4096]{1,0:T(8,128)(2,1)} %bitcast.8.xg_hbm.x_ref.g_ref, bf16[512,1152]{1,0:T(8,128)(2,1)} %get-tuple-element.29.own_hbm, bf16[512,1152]{1,0:T(8,128)(2,1)} %copy-done.5, ...), custom_call_target="tpu_custom_call" | custom-call | flops 4831838208 | bytes 10485760 | tf_op jit(solution)/shard_map/expert_math/pallas_call | solution.py:279
  123.7 5.9 %all-to-all-start.1 = ((bf16[64,8,4096]{2,1,0:T(8,128)(2,1)}), bf16[64,8,4096]{2,1,0:T(8,128)(2,1)}, u32[]{:S(2)}, u32[]{:S(2)}) async-start(bf16[64,8,4096]{2,1,0:T(8,128)(2,1)} %bitcast.19), calls=%async_computation.1 | async-start | bytes 8388608 | tf_op jit(solution)/shard_map/all_to_all | solution.py:241
  129.6 6.7 %weight_grads.1.next_ref.prev_ref.own_ref = bf16[4,512,1152]{2,1,0:T(8,128)(2,1)} custom-call(s32[1]{0:T(128)} %bitcast.6.me_ref, bf16[512,4096]{1,0:T(8,128)(2,1)} %bitcast.8.xg_hbm.x_ref.g_ref, bf16[512,4096]{1,0:T(8,128)(2,1)} %bitcast.8.xg_hbm.x_ref.g_ref, bf16[512,1152]{1,0:T(8,128)(2,1)S(1)} %get-tuple-element.31.saved_ref), custom_call_target="tpu_custom_call" | custom-call | flops 2415919104 | bytes 6291456 | tf_op jit(solution)/shard_map/weight_grads/pallas_call | solution.py:292
  136.2 1.3 slice_bitcast_fusion
  137.6 0.6 collective-permute-start.5
  138.1 1.5 collective-permute-start.4
  139.7 12.9 %collective-permute-done.5.high_ref = bf16[256,1152]{1,0:T(8,128)(2,1)S(1)} collective-permute-done((bf16[256,1152]{1,0:T(8,128)(2,1)S(1)}, bf16[256,1152]{1,0:T(8,128)(2,1)S(1)}, u32[]{:S(2)}, u32[]{:S(2)}) %collective-permute-start.5) | collective-permute-done | bytes 589856 | tf_op jit(solution)/shard_map/ppermute | solution.py:268
  152.6 0.0 copy-start.2
  152.6 0.2 collective-permute-done.4.low_ref
  152.8 0.7 copy-done.2
  153.4 0.0 copy-start.3
  153.4 0.9 copy-done.3
  154.3 3.5 %add_far.1 = (bf16[512,1152]{1,0:T(8,128)(2,1)}, bf16[512,1152]{1,0:T(8,128)(2,1)}) custom-call(bf16[4,512,1152]{2,1,0:T(8,128)(2,1)} %weight_grads.1.next_ref.prev_ref.own_ref, bf16[4,512,1152]{2,1,0:T(8,128)(2,1)} %weight_grads.1.next_ref.prev_ref.own_ref, bf16[256,1152]{1,0:T(8,128)(2,1)} %copy-done.3, bf16[256,1152]{1,0:T(8,128)(2,1)} %copy-done.2), custom_call_target="tpu_custom_call" | custom-call | bytes 5898240 | tf_op jit(solution)/shard_map/add_far/pallas_call | solution.py:313
  157.8 2.4 %collective-permute-start.6 = (bf16[512,1152]{1,0:T(8,128)(2,1)}, bf16[512,1152]{1,0:T(8,128)(2,1)S(1)}, u32[]{:S(2)}, u32[]{:S(2)}) collective-permute-start(bf16[512,1152]{1,0:T(8,128)(2,1)} %get-tuple-element.32), channel_id=1, source_target_pairs={{0,64},{64,128},{128,192},{192,0},{1,65},{65,129},{129,193},{193,1... | collective-permute-start | bytes 3538952 | tf_op jit(solution)/shard_map/ppermute | solution.py:265
  160.2 0.0 collective-permute-start.7
  160.2 24.6 %collective-permute-done.6.below_ref = bf16[512,1152]{1,0:T(8,128)(2,1)S(1)} collective-permute-done((bf16[512,1152]{1,0:T(8,128)(2,1)}, bf16[512,1152]{1,0:T(8,128)(2,1)S(1)}, u32[]{:S(2)}, u32[]{:S(2)}) %collective-permute-start.6) | collective-permute-done | bytes 1179680 | tf_op jit(solution)/shard_map/ppermute | solution.py:265
  184.8 0.0 copy-start
  184.8 2.1 collective-permute-done.7.above_ref
  187.0 0.0 copy-done
  187.0 0.0 copy-start.1
  187.0 1.0 copy-done.1
  188.0 3.4 %add_last.1 = (bf16[512,384]{1,0:T(8,128)(2,1)}, bf16[512,384]{1,0:T(8,128)(2,1)}, bf16[384,512]{1,0:T(8,128)(2,1)}) custom-call(bf16[4,512,1152]{2,1,0:T(8,128)(2,1)} %weight_grads.1.next_ref.prev_ref.own_ref, bf16[512,1152]{1,0:T(8,128)(2,1)} %copy-done, bf16[512,1152]{1,0:T(8,128)(2,1)} %copy-done.1), custom_call_target="tpu_custom_call" | custom-call | bytes 4718592 | tf_op jit(solution)/shard_map/add_last/pallas_call | solution.py:321
  191.4 34.2 %all-to-all-done.1 = bf16[64,8,4096]{2,1,0:T(8,128)(2,1)} async-done(((bf16[64,8,4096]{2,1,0:T(8,128)(2,1)}), bf16[64,8,4096]{2,1,0:T(8,128)(2,1)}, u32[]{:S(2)}, u32[]{:S(2)}) %all-to-all-start.1) | async-done | bytes 4194336 | tf_op jit(solution)/shard_map/all_to_all | solution.py:241
  225.6 4.8 %merge.1 = (bf16[128,2048]{1,0:T(8,128)(2,1)}, bf16[128,2048]{1,0:T(8,128)(2,1)}, f32[8,128]{1,0:T(8,128)}) custom-call(s32[8,128]{1,0:T(8,128)} %bitcast.25, bf16[384,512]{1,0:T(8,128)(2,1)} %get-tuple-element.27.tables_ref, bf16[512,128]{1,0:T(8,128)(2,1)} %get-tuple-element.25.pick_ref, bf16[128,2048]{1,0:T(8,128)(2,1)} %cot_ref.3, ...), custom_call_target="tpu_custom_call" | custom-call | flops 1073741824 | bytes 5242880 | tf_op jit(solution)/shard_map/merge/pallas_call | solution.py:331
  (2 shorter events, 0.1 us)
Async XLA Ops:
  5.2 108.6 %all-to-all-start = ((bf16[64,8,4096]{2,1,0:T(8,128)(2,1)}), bf16[64,8,4096]{2,1,0:T(8,128)(2,1)}, u32[]{:S(2)}, u32[]{:S(2)}) async-start(bf16[64,8,4096]{2,1,0:T(8,128)(2,1)} %bitcast.20), calls=%async_computation | async-start | bytes 8388608 | tf_op jit(solution)/shard_map/all_to_all | solution.py:241
  20.2 28.1 %collective-permute-start.1 = (bf16[512,1152]{1,0:T(8,128)(2,1)}, bf16[512,1152]{1,0:T(8,128)(2,1)S(1)}, u32[]{:S(2)}, u32[]{:S(2)}) collective-permute-start(bf16[512,1152]{1,0:T(8,128)(2,1)} %get-tuple-element.29.own_hbm), channel_id=1, source_target_pairs={{0,64},{64,128},{128,192},{192,0},{1,65},{65,129},{129,193},{193,1... | collective-permute-start | bytes 3538952 | tf_op jit(solution)/shard_map/ppermute | solution.py:265
  21.4 28.2 %collective-permute-start = (bf16[512,1152]{1,0:T(8,128)(2,1)}, bf16[512,1152]{1,0:T(8,128)(2,1)S(1)}, u32[]{:S(2)}, u32[]{:S(2)}) collective-permute-start(bf16[512,1152]{1,0:T(8,128)(2,1)} %get-tuple-element.29.own_hbm), channel_id=1, source_target_pairs={{0,192},{64,0},{128,64},{192,128},{1,193},{65,1},{129,65},{193,129... | collective-permute-start | bytes 3538952 | tf_op jit(solution)/shard_map/ppermute | solution.py:268
  48.3 2.3 %copy-start.4 = (bf16[512,1152]{1,0:T(8,128)(2,1)}, bf16[512,1152]{1,0:T(8,128)(2,1)S(1)}, u32[]{:S(2)}) copy-start(bf16[512,1152]{1,0:T(8,128)(2,1)S(1)} %collective-permute-done.1.prev_hbm) | copy-start | bytes 3538948
  48.3 14.5 %collective-permute-start.2 = (bf16[256,1152]{1,0:T(8,128)(2,1)S(1)}, bf16[256,1152]{1,0:T(8,128)(2,1)S(1)}, u32[]{:S(2)}, u32[]{:S(2)}) collective-permute-start(bf16[256,1152]{1,0:T(8,128)(2,1)S(1)} %slice.16), channel_id=1, source_target_pairs={{0,64},{64,128},{128,192},{192,0},{1,65},{65,129},{129,193},{193,1... | collective-permute-start | bytes 1769480 | tf_op jit(solution)/shard_map/ppermute | solution.py:265
  49.6 1.0 copy-start.5
  49.6 14.3 %collective-permute-start.3 = (bf16[256,1152]{1,0:T(8,128)(2,1)S(1)}, bf16[256,1152]{1,0:T(8,128)(2,1)S(1)}, u32[]{:S(2)}, u32[]{:S(2)}) collective-permute-start(bf16[256,1152]{1,0:T(8,128)(2,1)S(1)} %slice.17), channel_id=1, source_target_pairs={{0,192},{64,0},{128,64},{192,128},{1,193},{65,1},{129,65},{193,129... | collective-permute-start | bytes 1769480 | tf_op jit(solution)/shard_map/ppermute | solution.py:268
  123.7 101.9 %all-to-all-start.1 = ((bf16[64,8,4096]{2,1,0:T(8,128)(2,1)}), bf16[64,8,4096]{2,1,0:T(8,128)(2,1)}, u32[]{:S(2)}, u32[]{:S(2)}) async-start(bf16[64,8,4096]{2,1,0:T(8,128)(2,1)} %bitcast.19), calls=%async_computation.1 | async-start | bytes 8388608 | tf_op jit(solution)/shard_map/all_to_all | solution.py:241
  137.6 15.0 %collective-permute-start.5 = (bf16[256,1152]{1,0:T(8,128)(2,1)S(1)}, bf16[256,1152]{1,0:T(8,128)(2,1)S(1)}, u32[]{:S(2)}, u32[]{:S(2)}) collective-permute-start(bf16[256,1152]{1,0:T(8,128)(2,1)S(1)} %get-tuple-element.44), channel_id=1, source_target_pairs={{0,192},{64,0},{128,64},{192,128},{1,193},{65,1},{129,65},{193,129... | collective-permute-start | bytes 1769480 | tf_op jit(solution)/shard_map/ppermute | solution.py:268
  138.1 14.7 %collective-permute-start.4 = (bf16[256,1152]{1,0:T(8,128)(2,1)S(1)}, bf16[256,1152]{1,0:T(8,128)(2,1)S(1)}, u32[]{:S(2)}, u32[]{:S(2)}) collective-permute-start(bf16[256,1152]{1,0:T(8,128)(2,1)S(1)} %get-tuple-element.45), channel_id=1, source_target_pairs={{0,64},{64,128},{128,192},{192,0},{1,65},{65,129},{129,193},{193,1... | collective-permute-start | bytes 1769480 | tf_op jit(solution)/shard_map/ppermute | solution.py:265
  152.6 0.8 copy-start.2
  153.4 0.9 copy-start.3
  157.8 27.0 %collective-permute-start.6 = (bf16[512,1152]{1,0:T(8,128)(2,1)}, bf16[512,1152]{1,0:T(8,128)(2,1)S(1)}, u32[]{:S(2)}, u32[]{:S(2)}) collective-permute-start(bf16[512,1152]{1,0:T(8,128)(2,1)} %get-tuple-element.32), channel_id=1, source_target_pairs={{0,64},{64,128},{128,192},{192,0},{1,65},{65,129},{129,193},{193,1... | collective-permute-start | bytes 3538952 | tf_op jit(solution)/shard_map/ppermute | solution.py:265
  160.2 26.8 %collective-permute-start.7 = (bf16[512,1152]{1,0:T(8,128)(2,1)}, bf16[512,1152]{1,0:T(8,128)(2,1)S(1)}, u32[]{:S(2)}, u32[]{:S(2)}) collective-permute-start(bf16[512,1152]{1,0:T(8,128)(2,1)} %get-tuple-element.33), channel_id=1, source_target_pairs={{0,192},{64,0},{128,64},{192,128},{1,193},{65,1},{129,65},{193,129... | collective-permute-start | bytes 3538952 | tf_op jit(solution)/shard_map/ppermute | solution.py:268
  184.8 2.2 copy-start
  187.0 1.0 copy-start.1

commit v8 on v7

--- a/solution.py
+++ b/solution.py
@@ -11,7 +11,7 @@
 BF = jnp.bfloat16
 F32 = jnp.float32
 STEP = 512
-MERGE = 1024
+MERGE = 2048
 
 
 def contract(left, right, left_dim, right_dim):

time: 231 us -> 231 us (level)
  no operation moved by 1% of the time
where the time goes in v8:
time: 231 us; the launch traced here: 230 us
  waiting for transfers between devices  163 us (71%)
  Pallas kernels  35.4 us (15%)
  starting transfers between devices  26.9 us (12%)
  local copies, waits for them, and re-layouts  4.02 us (2%)
    all_to_all x2, waiting for transfers between devices, exchange(): lax.all_to_all(x, 'expert', 0, 0, tiled=True).reshape(rows, 2 * width)  84.1 us
    ppermute x4, waiting for transfers between devices, up(): return lax.ppermute(x, 'dp', [(i, (i + 1) % parts) for i in range(parts)])  63.1 us
    all_to_all x2, starting transfers between devices, exchange(): lax.all_to_all(x, 'expert', 0, 0, tiled=True).reshape(rows, 2 * width)  18.2 us
    ppermute x4, waiting for transfers between devices, down(): return lax.ppermute(x, 'dp', [(i, (i - 1) % parts) for i in range(parts)])  16.1 us
    pallas_call x1, Pallas kernels, on_device(): pl.pallas_call(expert_math, in_specs=[pl.BlockSpec(memory_space=pltpu.SME...  9.93 us
    pallas_call x1, Pallas kernels, on_device(): pl.pallas_call(weight_grads, grid_spec=pltpu.PrefetchScalarGridSpec(num_s...  6.66 us
    ppermute x4, starting transfers between devices, up(): return lax.ppermute(x, 'dp', [(i, (i + 1) % parts) for i in range(parts)])  6.38 us
    pallas_call x1, Pallas kernels, on_device(): pl.pallas_call(part(merge, slots, experts), grid=(width // MERGE,), in_sp...  4.72 us
  transfers between devices with their start and end apart: 10, of which 9 were waited for; matrix products, arithmetic and copies ran while one was open for 1% of the time, Pallas kernels for 7%

profile of v8, /device:TPU:4, one launch (start us, length us, event | category | flops | bytes accessed | tf_op | source)
XLA Modules:
  0.0 230.3 jit_solution(12247804331747103922)
XLA Ops:
  0.6 4.5 %pick_rows.1 = (bf16[512,4096]{1,0:T(8,128)(2,1)}, bf16[512,128]{1,0:T(8,128)(2,1)}, bf16[512,256]{1,0:T(8,128)(2,1)}) custom-call(s32[8,128]{1,0:T(8,128)} %bitcast.24, s32[1,64]{1,0:T(1,128)} %bitcast.31, f32[8,128]{1,0:T(8,128)} %bitcast.29, bf16[128,2048]{1,0:T(8,128)(2,1)} %tokens_ref.1, bf16[128,2048]{1,0:T(8,128)(2,1)} %cot_ref.3), custom_call_target="tpu_custom_call" | custom-call | flops 536870912 | bytes 5242880 | tf_op jit(solution)/shard_map/pick_rows/pallas_call | solution.py:244
  5.2 12.4 %all-to-all-start = ((bf16[64,8,4096]{2,1,0:T(8,128)(2,1)}), bf16[64,8,4096]{2,1,0:T(8,128)(2,1)}, u32[]{:S(2)}, u32[]{:S(2)}) async-start(bf16[64,8,4096]{2,1,0:T(8,128)(2,1)} %bitcast.20), calls=%async_computation | async-start | bytes 8388608 | tf_op jit(solution)/shard_map/all_to_all | solution.py:241
  17.5 2.7 %lay_weights.1 = (bf16[512,1152]{1,0:T(8,128)(2,1)}, bf16[384,512]{1,0:T(8,128)(2,1)}) custom-call(bf16[512,384]{1,0:T(8,128)(2,1)} %bitcast.21, bf16[512,384]{1,0:T(8,128)(2,1)} %bitcast.22, bf16[384,512]{1,0:T(8,128)(2,1)} %bitcast.23, bf16[512,128]{1,0:T(8,128)(2,1)} %get-tuple-element.25.pick_ref, bf16[512,256]{1,0:T(8,128)(2,1)} %get-tuple-element.26.both_ref), custom_call_target="tpu_custom_call" | custom-call | bytes 2359296 | tf_op jit(solution)/shard_map/lay_weights/pallas_call | solution.py:270
  20.2 1.2 collective-permute-start.1
  21.4 0.8 collective-permute-start
  22.2 26.0 %collective-permute-done.1.prev_hbm = bf16[512,1152]{1,0:T(8,128)(2,1)S(1)} collective-permute-done((bf16[512,1152]{1,0:T(8,128)(2,1)}, bf16[512,1152]{1,0:T(8,128)(2,1)S(1)}, u32[]{:S(2)}, u32[]{:S(2)}) %collective-permute-start.1) | collective-permute-done | bytes 1179680 | tf_op jit(solution)/shard_map/ppermute | solution.py:265
  48.3 0.0 copy-start.4
  48.3 1.3 collective-permute-start.2
  49.6 0.0 collective-permute-done.next_hbm
  49.6 0.0 copy-start.5
  49.6 0.9 collective-permute-start.3
  50.6 0.1 copy-done.5
  50.6 0.0 copy-done.4
  50.6 12.2 %collective-permute-done.2.far_low_ref = bf16[256,1152]{1,0:T(8,128)(2,1)S(1)} collective-permute-done((bf16[256,1152]{1,0:T(8,128)(2,1)S(1)}, bf16[256,1152]{1,0:T(8,128)(2,1)S(1)}, u32[]{:S(2)}, u32[]{:S(2)}) %collective-permute-start.2) | collective-permute-done | bytes 589856 | tf_op jit(solution)/shard_map/ppermute | solution.py:265
  62.9 1.0 collective-permute-done.3.far_high_ref
  63.9 49.9 %all-to-all-done = bf16[64,8,4096]{2,1,0:T(8,128)(2,1)} async-done(((bf16[64,8,4096]{2,1,0:T(8,128)(2,1)}), bf16[64,8,4096]{2,1,0:T(8,128)(2,1)}, u32[]{:S(2)}, u32[]{:S(2)}) %all-to-all-start) | async-done | bytes 4194336 | tf_op jit(solution)/shard_map/all_to_all | solution.py:241
  113.8 9.9 %expert_math.1 = (bf16[512,4096]{1,0:T(8,128)(2,1)}, bf16[512,1152]{1,0:T(8,128)(2,1)S(1)}) custom-call(s32[1]{0:T(128)} %bitcast.6.me_ref, bf16[512,4096]{1,0:T(8,128)(2,1)} %bitcast.8.xg_hbm.x_ref.g_ref, bf16[512,1152]{1,0:T(8,128)(2,1)} %get-tuple-element.29.own_hbm, bf16[512,1152]{1,0:T(8,128)(2,1)} %copy-done.5, ...), custom_call_target="tpu_custom_call" | custom-call | flops 4831838208 | bytes 10485760 | tf_op jit(solution)/shard_map/expert_math/pallas_call | solution.py:279
  123.7 5.9 %all-to-all-start.1 = ((bf16[64,8,4096]{2,1,0:T(8,128)(2,1)}), bf16[64,8,4096]{2,1,0:T(8,128)(2,1)}, u32[]{:S(2)}, u32[]{:S(2)}) async-start(bf16[64,8,4096]{2,1,0:T(8,128)(2,1)} %bitcast.19), calls=%async_computation.1 | async-start | bytes 8388608 | tf_op jit(solution)/shard_map/all_to_all | solution.py:241
  129.6 6.7 %weight_grads.1.next_ref.prev_ref.own_ref = bf16[4,512,1152]{2,1,0:T(8,128)(2,1)} custom-call(s32[1]{0:T(128)} %bitcast.6.me_ref, bf16[512,4096]{1,0:T(8,128)(2,1)} %bitcast.8.xg_hbm.x_ref.g_ref, bf16[512,4096]{1,0:T(8,128)(2,1)} %bitcast.8.xg_hbm.x_ref.g_ref, bf16[512,1152]{1,0:T(8,128)(2,1)S(1)} %get-tuple-element.31.saved_ref), custom_call_target="tpu_custom_call" | custom-call | flops 2415919104 | bytes 6291456 | tf_op jit(solution)/shard_map/weight_grads/pallas_call | solution.py:292
  136.2 1.3 slice_bitcast_fusion
  137.6 0.6 collective-permute-start.5
  138.1 1.5 collective-permute-start.4
  139.7 12.9 %collective-permute-done.5.high_ref = bf16[256,1152]{1,0:T(8,128)(2,1)S(1)} collective-permute-done((bf16[256,1152]{1,0:T(8,128)(2,1)S(1)}, bf16[256,1152]{1,0:T(8,128)(2,1)S(1)}, u32[]{:S(2)}, u32[]{:S(2)}) %collective-permute-start.5) | collective-permute-done | bytes 589856 | tf_op jit(solution)/shard_map/ppermute | solution.py:268
  152.6 0.0 copy-start.2
  152.6 0.2 collective-permute-done.4.low_ref
  152.8 0.7 copy-done.2
  153.4 0.0 copy-start.3
  153.4 0.9 copy-done.3
  154.3 3.5 %add_far.1 = (bf16[512,1152]{1,0:T(8,128)(2,1)}, bf16[512,1152]{1,0:T(8,128)(2,1)}) custom-call(bf16[4,512,1152]{2,1,0:T(8,128)(2,1)} %weight_grads.1.next_ref.prev_ref.own_ref, bf16[4,512,1152]{2,1,0:T(8,128)(2,1)} %weight_grads.1.next_ref.prev_ref.own_ref, bf16[256,1152]{1,0:T(8,128)(2,1)} %copy-done.3, bf16[256,1152]{1,0:T(8,128)(2,1)} %copy-done.2), custom_call_target="tpu_custom_call" | custom-call | bytes 5898240 | tf_op jit(solution)/shard_map/add_far/pallas_call | solution.py:313
  157.8 2.4 %collective-permute-start.6 = (bf16[512,1152]{1,0:T(8,128)(2,1)}, bf16[512,1152]{1,0:T(8,128)(2,1)S(1)}, u32[]{:S(2)}, u32[]{:S(2)}) collective-permute-start(bf16[512,1152]{1,0:T(8,128)(2,1)} %get-tuple-element.32), channel_id=1, source_target_pairs={{0,64},{64,128},{128,192},{192,0},{1,65},{65,129},{129,193},{193,1... | collective-permute-start | bytes 3538952 | tf_op jit(solution)/shard_map/ppermute | solution.py:265
  160.2 0.0 collective-permute-start.7
  160.2 24.6 %collective-permute-done.6.below_ref = bf16[512,1152]{1,0:T(8,128)(2,1)S(1)} collective-permute-done((bf16[512,1152]{1,0:T(8,128)(2,1)}, bf16[512,1152]{1,0:T(8,128)(2,1)S(1)}, u32[]{:S(2)}, u32[]{:S(2)}) %collective-permute-start.6) | collective-permute-done | bytes 1179680 | tf_op jit(solution)/shard_map/ppermute | solution.py:265
  184.8 0.0 copy-start
  184.8 2.1 collective-permute-done.7.above_ref
  187.0 0.0 copy-done
  187.0 0.0 copy-start.1
  187.0 1.0 copy-done.1
  188.0 3.4 %add_last.1 = (bf16[512,384]{1,0:T(8,128)(2,1)}, bf16[512,384]{1,0:T(8,128)(2,1)}, bf16[384,512]{1,0:T(8,128)(2,1)}) custom-call(bf16[4,512,1152]{2,1,0:T(8,128)(2,1)} %weight_grads.1.next_ref.prev_ref.own_ref, bf16[512,1152]{1,0:T(8,128)(2,1)} %copy-done, bf16[512,1152]{1,0:T(8,128)(2,1)} %copy-done.1), custom_call_target="tpu_custom_call" | custom-call | bytes 4718592 | tf_op jit(solution)/shard_map/add_last/pallas_call | solution.py:321
  191.4 34.2 %all-to-all-done.1 = bf16[64,8,4096]{2,1,0:T(8,128)(2,1)} async-done(((bf16[64,8,4096]{2,1,0:T(8,128)(2,1)}), bf16[64,8,4096]{2,1,0:T(8,128)(2,1)}, u32[]{:S(2)}, u32[]{:S(2)}) %all-to-all-start.1) | async-done | bytes 4194336 | tf_op jit(solution)/shard_map/all_to_all | solution.py:241
  225.6 4.7 %merge.1 = (bf16[128,2048]{1,0:T(8,128)(2,1)}, bf16[128,2048]{1,0:T(8,128)(2,1)}, f32[8,128]{1,0:T(8,128)}) custom-call(s32[8,128]{1,0:T(8,128)} %bitcast.25, bf16[384,512]{1,0:T(8,128)(2,1)} %get-tuple-element.27.tables_ref, bf16[512,128]{1,0:T(8,128)(2,1)} %get-tuple-element.25.pick_ref, bf16[128,2048]{1,0:T(8,128)(2,1)} %cot_ref.3, ...), custom_call_target="tpu_custom_call" | custom-call | flops 1073741824 | bytes 5242880 | tf_op jit(solution)/shard_map/merge/pallas_call | solution.py:331
  (2 shorter events, 0.1 us)
Async XLA Ops:
  5.2 108.6 %all-to-all-start = ((bf16[64,8,4096]{2,1,0:T(8,128)(2,1)}), bf16[64,8,4096]{2,1,0:T(8,128)(2,1)}, u32[]{:S(2)}, u32[]{:S(2)}) async-start(bf16[64,8,4096]{2,1,0:T(8,128)(2,1)} %bitcast.20), calls=%async_computation | async-start | bytes 8388608 | tf_op jit(solution)/shard_map/all_to_all | solution.py:241
  20.2 28.1 %collective-permute-start.1 = (bf16[512,1152]{1,0:T(8,128)(2,1)}, bf16[512,1152]{1,0:T(8,128)(2,1)S(1)}, u32[]{:S(2)}, u32[]{:S(2)}) collective-permute-start(bf16[512,1152]{1,0:T(8,128)(2,1)} %get-tuple-element.29.own_hbm), channel_id=1, source_target_pairs={{0,64},{64,128},{128,192},{192,0},{1,65},{65,129},{129,193},{193,1... | collective-permute-start | bytes 3538952 | tf_op jit(solution)/shard_map/ppermute | solution.py:265
  21.4 28.2 %collective-permute-start = (bf16[512,1152]{1,0:T(8,128)(2,1)}, bf16[512,1152]{1,0:T(8,128)(2,1)S(1)}, u32[]{:S(2)}, u32[]{:S(2)}) collective-permute-start(bf16[512,1152]{1,0:T(8,128)(2,1)} %get-tuple-element.29.own_hbm), channel_id=1, source_target_pairs={{0,192},{64,0},{128,64},{192,128},{1,193},{65,1},{129,65},{193,129... | collective-permute-start | bytes 3538952 | tf_op jit(solution)/shard_map/ppermute | solution.py:268
  48.3 2.3 %copy-start.4 = (bf16[512,1152]{1,0:T(8,128)(2,1)}, bf16[512,1152]{1,0:T(8,128)(2,1)S(1)}, u32[]{:S(2)}) copy-start(bf16[512,1152]{1,0:T(8,128)(2,1)S(1)} %collective-permute-done.1.prev_hbm) | copy-start | bytes 3538948
  48.3 14.5 %collective-permute-start.2 = (bf16[256,1152]{1,0:T(8,128)(2,1)S(1)}, bf16[256,1152]{1,0:T(8,128)(2,1)S(1)}, u32[]{:S(2)}, u32[]{:S(2)}) collective-permute-start(bf16[256,1152]{1,0:T(8,128)(2,1)S(1)} %slice.16), channel_id=1, source_target_pairs={{0,64},{64,128},{128,192},{192,0},{1,65},{65,129},{129,193},{193,1... | collective-permute-start | bytes 1769480 | tf_op jit(solution)/shard_map/ppermute | solution.py:265
  49.6 1.0 copy-start.5
  49.6 14.3 %collective-permute-start.3 = (bf16[256,1152]{1,0:T(8,128)(2,1)S(1)}, bf16[256,1152]{1,0:T(8,128)(2,1)S(1)}, u32[]{:S(2)}, u32[]{:S(2)}) collective-permute-start(bf16[256,1152]{1,0:T(8,128)(2,1)S(1)} %slice.17), channel_id=1, source_target_pairs={{0,192},{64,0},{128,64},{192,128},{1,193},{65,1},{129,65},{193,129... | collective-permute-start | bytes 1769480 | tf_op jit(solution)/shard_map/ppermute | solution.py:268
  123.7 101.9 %all-to-all-start.1 = ((bf16[64,8,4096]{2,1,0:T(8,128)(2,1)}), bf16[64,8,4096]{2,1,0:T(8,128)(2,1)}, u32[]{:S(2)}, u32[]{:S(2)}) async-start(bf16[64,8,4096]{2,1,0:T(8,128)(2,1)} %bitcast.19), calls=%async_computation.1 | async-start | bytes 8388608 | tf_op jit(solution)/shard_map/all_to_all | solution.py:241
  137.6 15.0 %collective-permute-start.5 = (bf16[256,1152]{1,0:T(8,128)(2,1)S(1)}, bf16[256,1152]{1,0:T(8,128)(2,1)S(1)}, u32[]{:S(2)}, u32[]{:S(2)}) collective-permute-start(bf16[256,1152]{1,0:T(8,128)(2,1)S(1)} %get-tuple-element.44), channel_id=1, source_target_pairs={{0,192},{64,0},{128,64},{192,128},{1,193},{65,1},{129,65},{193,129... | collective-permute-start | bytes 1769480 | tf_op jit(solution)/shard_map/ppermute | solution.py:268
  138.1 14.7 %collective-permute-start.4 = (bf16[256,1152]{1,0:T(8,128)(2,1)S(1)}, bf16[256,1152]{1,0:T(8,128)(2,1)S(1)}, u32[]{:S(2)}, u32[]{:S(2)}) collective-permute-start(bf16[256,1152]{1,0:T(8,128)(2,1)S(1)} %get-tuple-element.45), channel_id=1, source_target_pairs={{0,64},{64,128},{128,192},{192,0},{1,65},{65,129},{129,193},{193,1... | collective-permute-start | bytes 1769480 | tf_op jit(solution)/shard_map/ppermute | solution.py:265
  152.6 0.8 copy-start.2
  153.4 0.9 copy-start.3
  157.8 27.0 %collective-permute-start.6 = (bf16[512,1152]{1,0:T(8,128)(2,1)}, bf16[512,1152]{1,0:T(8,128)(2,1)S(1)}, u32[]{:S(2)}, u32[]{:S(2)}) collective-permute-start(bf16[512,1152]{1,0:T(8,128)(2,1)} %get-tuple-element.32), channel_id=1, source_target_pairs={{0,64},{64,128},{128,192},{192,0},{1,65},{65,129},{129,193},{193,1... | collective-permute-start | bytes 3538952 | tf_op jit(solution)/shard_map/ppermute | solution.py:265
  160.2 26.8 %collective-permute-start.7 = (bf16[512,1152]{1,0:T(8,128)(2,1)}, bf16[512,1152]{1,0:T(8,128)(2,1)S(1)}, u32[]{:S(2)}, u32[]{:S(2)}) collective-permute-start(bf16[512,1152]{1,0:T(8,128)(2,1)} %get-tuple-element.33), channel_id=1, source_target_pairs={{0,192},{64,0},{128,64},{192,128},{1,193},{65,1},{129,65},{193,129... | collective-permute-start | bytes 3538952 | tf_op jit(solution)/shard_map/ppermute | solution.py:268
  184.8 2.2 copy-start
  187.0 1.0 copy-start.1
